TPU v7x, 256 devices: a whole 4x4x8 slice. The times are simulated.
256 devices in a mesh: tile: 16 (over x, z_lo, core), kern: 16 (over y, z_hi).
Axes of the slice: x: 4, y: 4, z: 8 (z_hi: 4, z_lo: 2; z = z_hi * 2 + z_lo), core: 2. Of those that a mesh axis runs over, the one named last changes fastest.
Arguments:
- mask_field: float32 [4096, 1024], P('tile', 'kern'), may hold values from -6 to 6
- target: int32 [4096, 1024], P('tile'), may hold values 0 or 1
- kernel_spectra: float32 [32, 2, 128, 128], P('kern'), may hold values from -5 to 5
- kernel_weight: float32 [32], P('kern'), may hold values from 0.01 to 0.1
Outputs:
- resist: float32 [4096, 1024], P('tile', 'kern')
- mask_grad: float32 [4096, 1024], P('tile', 'kern')
All inputs are finite; a program needn't handle non-finite values. No bound on the sum of `target` on one device may be relied on, other than what follows from the above.
Results may differ from a plain program's by a relative error of at most 0.00065.
Values may be sent and summed in bfloat16 or wider, within the bound.
No kernel may reach another device: no remote copies, remote signals or barrier semaphores. Data moves between devices by JAX's collectives and lax.ppermute only.
A program may use at most 64 MiB of HBM per device.

v0:
```python
import math

import jax
import jax.numpy as jnp
from jax import lax
from jax.sharding import PartitionSpec as P

HALO_ROWS = 128
ROW_FREQS = 128
COL_FREQS = 128


STEEPNESS = 4.0
THRESHOLD = 1.0


def with_halo(value, sides, width):
    for axis, dim in sides:
        peers, length = (lax.axis_size(axis), value.shape[dim])
        up = [(i, (i + 1) % peers) for i in range(peers - 1)]
        down = [(j, i) for i, j in up]
        last = lax.slice_in_dim(value, length - width, length, axis=dim)
        first = lax.slice_in_dim(value, 0, width, axis=dim)
        before = lax.ppermute(last, axis, up)
        after = lax.ppermute(first, axis, down)
        value = jnp.concatenate([before, value, after], axis=dim)
    return value


def from_behind(block, axis, distance):
    devices = range(lax.axis_size(axis))
    route = [(i - distance, i) for i in devices if i - distance in devices]
    return lax.ppermute(block, axis, route)


def matmul(former, latter):
    return jnp.dot(
        former, latter, precision=lax.Precision.HIGHEST, preferred_element_type=jnp.float32
    )


def inner_product(former, latter):
    return lax.dot_general(
        former,
        latter,
        (((0,), (0,)), ((), ())),
        precision=lax.Precision.HIGHEST,
        preferred_element_type=jnp.float32,
    )


def phases(frequencies, places, length):
    turn_count = places[:, None] * frequencies[None, :] % length
    angles = turn_count.astype(jnp.float32) * (2.0 * math.pi / length)
    return (jnp.cos(angles), jnp.sin(angles))


def complex_block(real_part, imag_part):
    upper = jnp.concatenate([real_part, imag_part], 1)
    lower = jnp.concatenate([-imag_part, real_part], 1)
    return jnp.concatenate([upper, lower], 0)


def halves(values):
    half_width = values.shape[-1] // 2
    return (values[..., :half_width], values[..., half_width:])


def quadrants(values):
    rows_half = values.shape[0] // 2
    top_left, top_right = halves(values[:rows_half])
    low_left, low_right = halves(values[rows_half:])
    return (top_left, top_right, low_left, low_right)


def resist_pass(image, target_part):
    resist = jax.nn.sigmoid(STEEPNESS * (image - THRESHOLD))
    slope_map = 2.0 * STEEPNESS * (resist - target_part) * resist * (1.0 - resist)
    return (resist, slope_map.astype(jnp.bfloat16))


def per_device(mask_field, target, kernel_spectra, kernel_weight):
    tile_rows, shard_cols = mask_field.shape
    mask_cols = shard_cols * lax.axis_size("kern")
    window_rows = tile_rows + 2 * HALO_ROWS
    full_scale = 1.0 / math.sqrt(window_rows * mask_cols)
    band_scale = 1.0 / math.sqrt(ROW_FREQS * COL_FREQS)
    row_freq = jnp.arange(ROW_FREQS, dtype=jnp.int32) - ROW_FREQS // 2
    col_freq = jnp.arange(COL_FREQS, dtype=jnp.int32) - COL_FREQS // 2
    col_start = lax.axis_index("kern") * shard_cols
    own_places = col_start + jnp.arange(shard_cols, dtype=jnp.int32)
    own_cos, own_sin = phases(col_freq, own_places, mask_cols)
    win_cos, win_sin = phases(row_freq, jnp.arange(window_rows, dtype=jnp.int32), window_rows)
    out_cos, out_sin = phases(
        row_freq, HALO_ROWS + jnp.arange(tile_rows, dtype=jnp.int32), window_rows
    )
    win_table = jnp.concatenate([win_cos, win_sin], 1)
    out_table = jnp.concatenate([out_cos, out_sin], 1)
    target_rows = target.astype(jnp.float32)
    window = with_halo(mask_field, (("tile", 0),), HALO_ROWS)
    col_done = matmul(window, jnp.concatenate([own_cos, own_sin], 1))
    spec_parts = quadrants(inner_product(win_table, col_done))
    spectrum_re = (spec_parts[0] - spec_parts[3]) * full_scale
    spectrum_im = -(spec_parts[1] + spec_parts[2]) * full_scale
    spectrum_re, spectrum_im = lax.psum((spectrum_re, spectrum_im), "kern")
    full_cos, full_sin = phases(col_freq, jnp.arange(mask_cols, dtype=jnp.int32), mask_cols)
    to_pixels = complex_block(full_cos.T, full_sin.T)
    aerials = []
    partial_image = jnp.zeros((tile_rows, mask_cols), jnp.float32)
    for kernel_slot in range(kernel_spectra.shape[0]):
        kern_re = kernel_spectra[kernel_slot, 0]
        kern_im = kernel_spectra[kernel_slot, 1]
        band_re = kern_re * spectrum_re - kern_im * spectrum_im
        band_im = kern_re * spectrum_im + kern_im * spectrum_re
        rows_done = matmul(out_table, complex_block(band_re, band_im))
        aerial = matmul(rows_done, to_pixels) * band_scale
        aerial_re, aerial_im = halves(aerial)
        partial_image = partial_image + kernel_weight[kernel_slot] * (
            aerial_re * aerial_re + aerial_im * aerial_im
        )
        aerials.append(aerial)
    aerials, partial_image, to_bands = (aerials, partial_image, complex_block(full_cos, full_sin))
    image_all = lax.psum(partial_image, "kern")
    resist_all, slope_all = resist_pass(image_all, target_rows)
    resist_own = lax.dynamic_slice_in_dim(resist_all, col_start, shard_cols, 1)
    slope_wide = slope_all.astype(jnp.float32)
    combined_re = jnp.zeros((ROW_FREQS, COL_FREQS), jnp.float32)
    combined_im = jnp.zeros((ROW_FREQS, COL_FREQS), jnp.float32)
    for kernel_slot in range(kernel_spectra.shape[0]):
        aerial_re, aerial_im = halves(aerials[kernel_slot])
        weighted = jnp.concatenate([slope_wide * aerial_re, -(slope_wide * aerial_im)], 1)
        quarter = quadrants(inner_product(out_table, matmul(weighted, to_bands)))
        adjoint_re = (quarter[0] - quarter[3]) * band_scale
        adjoint_im = (quarter[1] + quarter[2]) * band_scale
        kern_re = kernel_spectra[kernel_slot, 0]
        kern_im = kernel_spectra[kernel_slot, 1]
        combined_re = combined_re + kernel_weight[kernel_slot] * (
            kern_re * adjoint_re - kern_im * adjoint_im
        )
        combined_im = combined_im + kernel_weight[kernel_slot] * (
            kern_re * adjoint_im + kern_im * adjoint_re
        )
    combined_re, combined_im = (combined_re, combined_im)
    combined_re, combined_im = lax.psum((combined_re, combined_im), "kern")
    upper_block = jnp.concatenate([combined_re, combined_im], 1)
    lower_block = jnp.concatenate([combined_im, -combined_re], 1)
    grad_rows = matmul(win_table, jnp.concatenate([upper_block, lower_block], 0))
    window_grad = matmul(grad_rows, jnp.concatenate([own_cos.T, own_sin.T], 0)) * (2.0 * full_scale)
    from_above = from_behind(window_grad[window_rows - HALO_ROWS :], "tile", 1)
    from_below = from_behind(window_grad[:HALO_ROWS], "tile", -1)
    mask_grad = window_grad[HALO_ROWS : HALO_ROWS + tile_rows]
    mask_grad = mask_grad.at[:HALO_ROWS].add(from_above)
    mask_grad = mask_grad.at[tile_rows - HALO_ROWS :].add(from_below)
    return (resist_own, mask_grad)


def solution(mesh):
    in_specs = (P("tile", "kern"), P("tile", None), P("kern", None, None, None), P("kern"))
    out_specs = (P("tile", "kern"), P("tile", "kern"))
    return jax.shard_map(
        per_device, mesh=mesh, in_specs=in_specs, out_specs=out_specs, check_vma=False
    )
```

profile of v0, /device:TPU:64, one launch (start us, length us, event | category | flops | bytes accessed | tf_op | source)
XLA Modules:
  0.0 557.1 jit_solution(14915419313602347539)
XLA Ops:
  7.2 0.0 all-reduce.10.cloned.1.call-start
  7.2 0.8 fusion.130
  8.0 1.3 collective-permute-start.1
  9.3 3.0 collective-permute-start
  12.3 1.0 fusion.72
  13.4 2.1 fusion.52
  15.6 0.2 fusion.112
  15.8 0.6 fusion.62
  16.5 1.0 fusion.23
  17.5 0.7 fusion.84
  18.2 0.0 all-reduce.10.cloned.1.call-update
  18.2 0.0 all-reduce.6.cloned.1.call-start
  18.2 0.6 fusion.103
  18.8 0.6 fusion.131
  19.4 165.7 %all-reduce.10.cloned.1.call-done = (f32[128,128]{1,0:T(8,128)}, f32[128,128]{1,0:T(8,128)}) async-done(((f32[128,128]{1,0:T(8,128)}, f32[128,128]{1,0:T(8,128)}), (f32[128,128]{1,0:T(8,128)}, f32[128,128]{1,0:T(8,128)})) %all-reduce.10.cloned.1.call-update) | async-done | bytes 131088 | tf_op jit(solution)/shard_map/psum | solution.py:105
  185.2 0.9 fusion.125
  186.1 0.4 fusion.35
  186.5 0.4 fusion.27
  186.9 1.9 convolution_multiply_fusion
  188.8 4.2 convolution_multiply_fusion.1
  193.0 2.7 multiply_add_fusion
  195.7 0.0 all-reduce.6.cloned.1.call-update
  195.7 0.2 all-reduce.8.cloned.1.call-start
  196.0 3.0 fusion.50
  199.0 164.8 %all-reduce.6.cloned.1.call-done = f32[256,1024]{1,0:T(8,128)} async-done(((f32[256,1024]{1,0:T(8,128)}), f32[256,1024]{1,0:T(8,128)}) %all-reduce.6.cloned.1.call-update) | async-done | bytes 1048592 | tf_op jit(solution)/shard_map/psum | solution.py:123
  363.8 3.5 convert_multiply_fusion.1
  367.3 0.5 convert_multiply_fusion.3
  367.9 0.5 copy-done.6
  368.4 0.2 copy-done.7
  368.5 0.2 copy-done.8
  368.7 1.9 fusion
  370.6 0.6 fusion.74
  371.2 1.9 fusion.4
  373.1 0.6 fusion.73
  373.7 2.0 fusion.92
  375.6 2.0 fusion.95
  377.6 0.0 all-reduce.8.cloned.1.call-update
  377.6 0.3 fusion.110
  377.9 162.0 %all-reduce.8.cloned.1.call-done = (f32[128,128]{1,0:T(8,128)}, f32[128,128]{1,0:T(8,128)}) async-done(((f32[128,128]{1,0:T(8,128)}, f32[128,128]{1,0:T(8,128)}), (f32[128,128]{1,0:T(8,128)}, f32[128,128]{1,0:T(8,128)})) %all-reduce.8.cloned.1.call-update) | async-done | bytes 131088 | tf_op jit(solution)/shard_map/psum | solution.py:144
  540.0 0.8 neg.35
  540.8 1.5 fusion.22
  542.3 0.7 convolution_multiply_fusion.2
  543.0 1.3 collective-permute-start.2
  544.3 1.0 constant_dynamic-slice_fusion
  545.3 0.7 copy.6
  546.0 1.3 collective-permute-start.3
  547.3 2.7 collective-permute-done.3
  550.0 0.6 copy-done.10
  (30 shorter events, 0.1 us)
Async XLA Ops:
  7.2 8.7 %copy-start.9 = (f32[256,64]{0,1:T(8,128)S(1)}, f32[256,64]{0,1:T(8,128)}, u32[]{:S(2)}) copy-start(f32[256,64]{0,1:T(8,128)} %param.8) | copy-start | bytes 196612
  7.2 178.0 %all-reduce.10.cloned.1.call-start = ((), (), s32[]{:S(2)}) async-start(), calls=%async_computation.2 | async-start | bytes 262144 | tf_op jit(solution)/shard_map/psum | solution.py:105
  8.0 7.8 %collective-permute-start.1 = (f32[128,64]{0,1:T(8,128)S(1)}, f32[128,64]{0,1:T(8,128)S(1)}, u32[]{:S(2)}, u32[]{:S(2)}) collective-permute-start(f32[128,64]{0,1:T(8,128)S(1)} %get-tuple-element.51), channel_id=1, source_target_pairs={{16,0},{32,16},{48,32},{64,48},{80,64},{96,80},{112,96},{128,112},... | collective-permute-start | bytes 98312 | tf_op jit(solution)/shard_map/ppermute | solution.py:25
  9.3 6.5 %collective-permute-start = (f32[128,64]{0,1:T(8,128)S(1)}, f32[128,64]{0,1:T(8,128)S(1)}, u32[]{:S(2)}, u32[]{:S(2)}) collective-permute-start(f32[128,64]{0,1:T(8,128)S(1)} %get-tuple-element.50), channel_id=1, source_target_pairs={{0,16},{16,32},{32,48},{48,64},{64,80},{80,96},{96,112},{112,128},... | collective-permute-start | bytes 98312 | tf_op jit(solution)/shard_map/ppermute | solution.py:24
  13.4 5.4 copy-start.11
  13.4 171.8 %copy-start.2 = (f32[2,2,128,128]{3,2,1,0:T(8,128)S(1)}, f32[2,2,128,128]{3,2,1,0:T(8,128)}, u32[]{:S(2)}) copy-start(f32[2,2,128,128]{3,2,1,0:T(8,128)} %param.10) | copy-start | bytes 786436
  15.5 171.3 %copy-start.3 = (f32[128,1024]{1,0:T(8,128)}, f32[128,1024]{1,0:T(8,128)S(1)}, u32[]{:S(2)}) copy-start(f32[128,1024]{1,0:T(8,128)S(1)} %get-tuple-element.63) | copy-start | bytes 1572868
  15.6 171.3 %copy-start.4 = (f32[128,1024]{1,0:T(8,128)}, f32[128,1024]{1,0:T(8,128)S(1)}, u32[]{:S(2)}) copy-start(f32[128,1024]{1,0:T(8,128)S(1)} %get-tuple-element.64) | copy-start | bytes 1572868
  15.6 171.3 %copy-start.5 = (f32[128,1024]{1,0:T(8,128)}, f32[128,1024]{1,0:T(8,128)S(1)}, u32[]{:S(2)}) copy-start(f32[128,1024]{1,0:T(8,128)S(1)} %get-tuple-element.65) | copy-start | bytes 1572868
  18.2 345.6 %all-reduce.6.cloned.1.call-start = ((), (), s32[]{:S(2)}) async-start(), calls=%async_computation | async-start | bytes 2097152 | tf_op jit(solution)/shard_map/psum | solution.py:123
  188.8 4.2 copy-start
  195.7 344.2 %all-reduce.8.cloned.1.call-start = ((), (), s32[]{:S(2)}) async-start(), calls=%async_computation.1 | async-start | bytes 262144 | tf_op jit(solution)/shard_map/psum | solution.py:144
  363.8 3.5 copy-start.1
  367.3 1.0 copy-start.6
  367.3 1.2 copy-start.7
  367.3 1.4 copy-start.8
  543.0 4.3 collective-permute-start.2
  546.0 4.0 collective-permute-start.3
  550.0 0.6 copy-start.10
Sparse Core Ops, SparseCore 0:
  18.3 166.8 all-reduce.9
  195.9 167.9 all-reduce.5
  377.7 162.1 all-reduce.7
where the time goes:
time: 564 us; the launch traced here: 557 us
  waiting for transfers between devices  495 us (88%)
  other arithmetic  20.4 us (4%)
  matrix products  15.6 us (3%)
  between operations  14.1 us (2%)
  starting transfers between devices  7.19 us (1%)
    psum x1, waiting for transfers between devices, per_device(): spectrum_re, spectrum_im = lax.psum((spectrum_re, spectrum_im), 'kern')  166 us
    psum x1, waiting for transfers between devices, per_device(): image_all = lax.psum(partial_image, 'kern')  165 us
    psum x1, waiting for transfers between devices, per_device(): combined_re, combined_im = lax.psum((combined_re, combined_im), 'kern')  162 us
    dot_general x9, matrix products, matmul(): jnp.dot(former, latter, precision=lax.Precision.HIGHEST, preferred_elemen...  13.4 us
  transfers between devices with their start and end apart: 7, of which 4 were waited for; matrix products, arithmetic and copies ran while one was open for 2% of the time, Pallas kernels for 0%

commit v1 on v0

v1 whole, which is shorter than its diff:
```python
import math

import jax
import jax.numpy as jnp
import numpy as np
from jax import lax
from jax.sharding import PartitionSpec as P

COLS = 1024
HALO = 128
FREQS = 128
TILE = 256
WINDOW = 512
SIDE = 4
SHARD = 64
SAMPLES = 256
QUARTER = 64
STEEPNESS = 4.0
THRESHOLD = 1.0

HIGH = lax.Precision.HIGHEST


def angles(places, frequencies, length):
    return (np.outer(places, frequencies) % length) * (2.0 * math.pi / length)


def tables():
    freq = np.arange(FREQS) - FREQS // 2
    scale = 1.0 / math.sqrt(WINDOW * COLS)
    win = angles(freq, np.arange(WINDOW), WINDOW)
    row_cos = np.cos(win) * scale
    row_sin = -np.sin(win) * scale
    col = angles(np.arange(COLS), freq, COLS)
    cos, sin = np.cos(col), np.sin(col)
    cos = cos.reshape(COLS // SHARD, SHARD, FREQS)
    sin = sin.reshape(COLS // SHARD, SHARD, FREQS)
    band = np.concatenate(
        [np.concatenate([cos, -sin], 2), np.concatenate([sin, cos], 2)], 1
    )
    out = angles(HALO + np.arange(TILE), freq, WINDOW)
    out_cos, out_sin = np.cos(out), np.sin(out)
    pix = angles(freq, np.arange(SAMPLES), SAMPLES)
    pix_cos, pix_sin = np.cos(pix), np.sin(pix)
    pixels = np.concatenate(
        [np.concatenate([pix_cos, pix_sin], 1), np.concatenate([-pix_sin, pix_cos], 1)], 0
    )
    gap = np.arange(COLS)[None, :] - (COLS // SAMPLES) * np.arange(SAMPLES)[:, None]
    waves = np.arange(1, SAMPLES // 2)
    base = 2.0 * math.pi / COLS
    line = (1.0 + 2.0 * np.cos(base * np.outer(np.arange(COLS), waves)).sum(1)) / SAMPLES
    spread = line[gap % COLS]
    as32 = lambda value: value.astype(np.float32)
    return tuple(
        map(as32, (row_cos, row_sin, band, np.concatenate([out_cos, out_sin], 1), pixels, spread))
    )


def dot(former, latter, dims=((1,), (0,))):
    return lax.dot_general(
        former, latter, (dims, ((), ())), precision=HIGH, preferred_element_type=jnp.float32
    )


def shift_y(value, step):
    route = [(4 * y + z, 4 * ((y + step) % 4) + z) for y in range(4) for z in range(4)]
    return lax.ppermute(value, "kern", route)


def shift_z(value, step):
    route = [(4 * y + z, 4 * y + (z + step) % 4) for y in range(4) for z in range(4)]
    return lax.ppermute(value, "kern", route)


def shift_tile(value, step):
    peers = lax.axis_size("tile")
    return lax.ppermute(value, "tile", [(i, (i + step) % peers) for i in range(peers)])


def swap_core(value):
    return lax.ppermute(value, "tile", [(i, i ^ 1) for i in range(lax.axis_size("tile"))])


def sum_over(value, shift):
    return value + shift(value, 1) + shift(value, 2) + shift(value, 3)


def per_device(mask_field, target, kernel_spectra, kernel_weight):
    row_cos, row_sin, band, out_table, pixels, spread = tables()
    tile = lax.axis_index("tile")
    kern = lax.axis_index("kern")
    at_y, at_z = kern // 4, kern % 4
    core = tile % 2
    above = shift_tile(mask_field[TILE - HALO :], 1)
    below = shift_tile(mask_field[:HALO], -1)

    scaled = kernel_spectra * (jnp.sqrt(kernel_weight) / FREQS)[:, None, None, None]
    own_half = lax.dynamic_index_in_dim(scaled, core, 0, False)
    half = jnp.stack([own_half] + [shift_y(own_half, step) for step in (1, 2, 3)])
    kernels = jnp.concatenate([half, swap_core(half)], 0)

    above = jnp.where(tile > 0, above, 0.0)
    below = jnp.where(tile < lax.axis_size("tile") - 1, below, 0.0)
    window = jnp.concatenate([above, mask_field, below], 0)
    rows_done = jnp.concatenate([dot(row_cos, window), dot(row_sin, window)], 1)

    band_of = lambda step: lax.dynamic_index_in_dim(
        band, 4 * at_y + (at_z + step) % 4, 0, False
    )
    bands = [band_of(step) for step in range(4)]
    part = dot(rows_done, bands[0])
    for step in (1, 2, 3):
        part = part + dot(shift_z(rows_done, -step), bands[step])
    spectrum = sum_over(part, shift_y)
    spec_re, spec_im = spectrum[:, :FREQS], spectrum[:, FREQS:]

    out_rows = lax.dynamic_slice_in_dim(out_table, at_y * QUARTER, QUARTER, 0)
    out_re, out_im = out_rows[:, :FREQS], out_rows[:, FREQS:]
    count = kernels.shape[0]
    fields = []
    image = jnp.zeros((QUARTER, SAMPLES), jnp.float32)
    for slot in range(count):
        kern_re, kern_im = kernels[slot, 0], kernels[slot, 1]
        band_re = kern_re * spec_re - kern_im * spec_im
        band_im = kern_re * spec_im + kern_im * spec_re
        block = jnp.concatenate(
            [jnp.concatenate([band_re, band_im], 1), jnp.concatenate([-band_im, band_re], 1)], 0
        )
        field = dot(dot(out_rows, block), pixels)
        fields.append(field)
        image = image + field[:, :SAMPLES] ** 2 + field[:, SAMPLES:] ** 2
    image = dot(sum_over(image, shift_z), spread)
    resist = jax.nn.sigmoid(STEEPNESS * (image - THRESHOLD))
    goal = lax.dynamic_slice_in_dim(target, at_y * QUARTER, QUARTER, 0).astype(jnp.float32)
    slope = 2.0 * STEEPNESS * (resist - goal) * resist * (1.0 - resist)
    slope = slope.astype(jnp.bfloat16).astype(jnp.float32)
    slope = dot(slope, spread, ((1,), (1,)))

    grad_re = jnp.zeros((FREQS, FREQS), jnp.float32)
    grad_im = jnp.zeros((FREQS, FREQS), jnp.float32)
    back_rows = jnp.concatenate([out_re, out_im], 0)
    for slot in range(count):
        kern_re, kern_im = kernels[slot, 0], kernels[slot, 1]
        weighted = jnp.concatenate([slope, slope], 1) * fields[slot]
        freqs = dot(weighted, pixels, ((1,), (1,)))
        turned = jnp.concatenate([freqs[:, FREQS:], -freqs[:, :FREQS]], 1)
        adjoint = dot(back_rows, jnp.concatenate([freqs, turned], 0), ((0,), (0,)))
        adj_re, adj_im = adjoint[:, :FREQS], adjoint[:, FREQS:]
        grad_re = grad_re + kern_re * adj_re + kern_im * adj_im
        grad_im = grad_im + kern_re * adj_im - kern_im * adj_re
    grad = sum_over(jnp.concatenate([grad_re, grad_im], 1), shift_y)

    column_parts = [dot(grad, bands[step], ((1,), (1,))) for step in range(4)]
    rows_grad = column_parts[0]
    for step in (1, 2, 3):
        rows_grad = rows_grad + shift_z(column_parts[step], step)
    grad_re, grad_im = rows_grad[:, :SHARD], rows_grad[:, SHARD:]
    window_grad = 2.0 * (
        dot(row_cos, grad_re, ((0,), (0,))) + dot(row_sin, grad_im, ((0,), (0,)))
    )
    from_above = shift_tile(window_grad[WINDOW - HALO :], 1)
    from_below = shift_tile(window_grad[:HALO], -1)
    from_above = jnp.where(tile > 0, from_above, 0.0)
    from_below = jnp.where(tile < lax.axis_size("tile") - 1, from_below, 0.0)
    mask_grad = window_grad[HALO : HALO + TILE] + jnp.concatenate([from_above, from_below], 0)

    place = lambda step: lax.dynamic_slice_in_dim(
        resist, (4 * ((at_y + step) % 4) + at_z) * SHARD, SHARD, 1
    )
    pieces = [place(0)] + [shift_y(place(step), step) for step in (1, 2, 3)]
    resist_own = jnp.zeros((TILE, SHARD), jnp.float32)
    for step in range(4):
        resist_own = lax.dynamic_update_slice_in_dim(
            resist_own, pieces[step], ((at_y - step) % 4) * QUARTER, 0
        )
    return (resist_own, mask_grad)


def solution(mesh):
    in_specs = (P("tile", "kern"), P("tile", None), P("kern", None, None, None), P("kern"))
    out_specs = (P("tile", "kern"), P("tile", "kern"))
    return jax.shard_map(
        per_device, mesh=mesh, in_specs=in_specs, out_specs=out_specs, check_vma=False
    )
```

time: 564 us -> 118 us (0.21)
  the two profiles are of different devices: /device:TPU:64 before, /device:TPU:33 now
where the time goes in v1:
time: 118 us; the launch traced here: 117 us
  starting transfers between devices  51.5 us (44%)
  matrix products  32.2 us (27%)
  waiting for transfers between devices  24.5 us (21%)
  other arithmetic  4.24 us (4%)
  local copies, waits for them, and re-layouts  3.55 us (3%)
  between operations  1.36 us (1%)
    dot_general x50, matrix products, dot(): lax.dot_general(former, latter, (dims, ((), ())), precision=HIGH, preferr...  32.2 us
    ppermute x9, starting transfers between devices, shift_z(): return lax.ppermute(value, 'kern', route)  23.9 us
    ppermute x12, starting transfers between devices, shift_y(): return lax.ppermute(value, 'kern', route)  18.6 us
    ppermute x9, waiting for transfers between devices, shift_z(): return lax.ppermute(value, 'kern', route)  10.3 us
    ppermute x12, waiting for transfers between devices, shift_y(): return lax.ppermute(value, 'kern', route)  9.98 us
    ppermute x4, starting transfers between devices, shift_tile(): lax.ppermute(value, 'tile', [(i, (i + step) % peers) for i in range(peers)])  7.46 us
    ppermute x4, waiting for transfers between devices, shift_tile(): lax.ppermute(value, 'tile', [(i, (i + step) % peers) for i in range(peers)])  4.21 us
  transfers between devices with their start and end apart: 26, of which 13 were waited for; matrix products, arithmetic and copies ran while one was open for 15% of the time, Pallas kernels for 0%

profile of v1, /device:TPU:33, one launch (start us, length us, event | category | flops | bytes accessed | tf_op | source)
XLA Modules:
  0.0 117.4 jit_solution(17490738867743219471)
XLA Ops:
  0.7 0.7 sqrt_multiply_fusion
  1.9 1.6 %fusion.329 = f32[2,128,128]{2,1,0:T(8,128)S(1)} fusion(f32[1]{0:T(128)} %dynamic-slice, f32[2,2,128,128]{3,2,1,0:T(8,128)} %param.12, s32[]{:T(128)S(6)} %select_n.131), kind=kLoop, calls=%fused_computation.364 | loop fusion | flops 32768 | bytes 262152 | tf_op jit(solution)/shard_map/jit(dynamic_index_in_dim)/squeeze | solution.py:98
  3.5 1.4 %collective-permute-start.8 = (f32[2,128,128]{2,1,0:T(8,128)S(1)}, f32[2,128,128]{2,1,0:T(8,128)S(1)}, u32[]{:S(2)}, u32[]{:S(2)}) collective-permute-start(f32[2,128,128]{2,1,0:T(8,128)S(1)} %fusion.329), channel_id=1, source_target_pairs={{0,4},{1,5},{2,6},{3,7},{4,8},{5,9},{6,10},{7,11},{8,12},{9,13},{1... | collective-permute-start | bytes 393224 | tf_op jit(solution)/shard_map/ppermute | solution.py:67
  4.9 2.6 %collective-permute-start.9 = (f32[2,128,128]{2,1,0:T(8,128)S(1)}, f32[2,128,128]{2,1,0:T(8,128)S(1)}, u32[]{:S(2)}, u32[]{:S(2)}) collective-permute-start(f32[2,128,128]{2,1,0:T(8,128)S(1)} %fusion.329), channel_id=1, source_target_pairs={{0,8},{1,9},{2,10},{3,11},{4,12},{5,13},{6,14},{7,15},{8,0},{9,1},... | collective-permute-start | bytes 393224 | tf_op jit(solution)/shard_map/ppermute | solution.py:67
  7.5 1.1 collective-permute-start.10
  8.6 0.8 fusion.277
  9.4 1.5 %collective-permute-start.1 = (f32[128,64]{0,1:T(8,128)S(1)}, f32[128,64]{0,1:T(8,128)S(1)}, u32[]{:S(2)}, u32[]{:S(2)}) collective-permute-start(f32[128,64]{0,1:T(8,128)S(1)} %get-tuple-element.61), channel_id=1, source_target_pairs={{0,240},{16,0},{32,16},{48,32},{64,48},{80,64},{96,80},{112,96},{1... | collective-permute-start | bytes 98312 | tf_op jit(solution)/shard_map/ppermute | solution.py:77
  10.9 1.1 collective-permute-start
  12.0 1.2 convolution_bitcast_fusion
  13.2 1.2 convolution_bitcast_fusion.1
  14.5 1.1 fusion.201
  15.5 1.1 fusion.199
  16.6 1.1 fusion.11
  17.7 1.1 fusion.13
  18.8 5.7 %collective-permute-start.2 = (f32[128,128]{0,1:T(8,128)S(1)}, f32[128,128]{0,1:T(8,128)S(1)}, u32[]{:S(2)}, u32[]{:S(2)}) collective-permute-start(f32[128,128]{0,1:T(8,128)S(1)} %pad_maximum_fusion.3), channel_id=1, source_target_pairs={{0,3},{1,0},{2,1},{3,2},{4,7},{5,4},{6,5},{7,6},{8,11},{9,8},{10,9... | collective-permute-start | bytes 196616 | tf_op jit(solution)/shard_map/ppermute | solution.py:72
  24.5 1.2 %fusion.159 = f32[128,256]{1,0:T(8,128)S(1)} fusion(f32[16,128,256]{2,1,0:T(8,128)} %constant.148.clone, s32[]{:T(128)S(6)} %select_n.138, f32[128,64]{0,1:T(8,128)S(1)} %fusion.11, f32[128,64]{0,1:T(8,128)S(1)} %fusion.13), kind=kOutput, calls=%fused_computation.173 | convolution fusion | flops 50348032 | bytes 327684 | tf_op jit(solution)/shard_map/dot_general | solution.py:60
  25.9 3.6 %collective-permute-start.3 = (f32[128,128]{0,1:T(8,128)S(1)}, f32[128,128]{0,1:T(8,128)S(1)}, u32[]{:S(2)}, u32[]{:S(2)}) collective-permute-start(f32[128,128]{0,1:T(8,128)S(1)} %pad_maximum_fusion.3), channel_id=1, source_target_pairs={{0,2},{1,3},{2,0},{3,1},{4,6},{5,7},{6,4},{7,5},{8,10},{9,11},{10,... | collective-permute-start | bytes 196616 | tf_op jit(solution)/shard_map/ppermute | solution.py:72
  29.5 1.2 %convolution_add_fusion.2 = f32[128,256]{1,0:T(8,128)S(1)} fusion(f32[128,256]{1,0:T(8,128)S(1)} %fusion.159, f32[128,128]{0,1:T(8,128)S(1)} %collective-permute-done.2, f32[16,128,256]{2,1,0:T(8,128)} %constant.148.clone, s32[]{:T(128)S(6)} %select_n.140), kind=kOutput, calls=%fused_computation.7 | convolution fusion | flops 50364416 | bytes 458756 | tf_op jit(solution)/shard_map/dot_general | solution.py:60
  30.7 1.2 %fusion.144 = f32[128,256]{1,0:T(8,128)S(1)} fusion(f32[128,128]{0,1:T(8,128)S(1)} %collective-permute-done.4, f32[16,128,256]{2,1,0:T(8,128)} %constant.148.clone, s32[]{:T(128)S(6)} %select_n.144), kind=kOutput, calls=%fused_computation.158 | convolution fusion | flops 50331648 | bytes 327684 | tf_op jit(solution)/shard_map/dot_general | solution.py:60
  32.0 1.7 %collective-permute-done.3 = f32[128,128]{0,1:T(8,128)S(1)} collective-permute-done((f32[128,128]{0,1:T(8,128)S(1)}, f32[128,128]{0,1:T(8,128)S(1)}, u32[]{:S(2)}, u32[]{:S(2)}) %collective-permute-start.3) | collective-permute-done | bytes 65568 | tf_op jit(solution)/shard_map/ppermute | solution.py:72
  33.7 1.2 %fusion.5 = f32[128,256]{1,0:T(8,128)S(1)} fusion(f32[128,256]{1,0:T(8,128)S(1)} %fusion.144, f32[128,256]{1,0:T(8,128)S(1)} %convolution_add_fusion.2, f32[128,128]{0,1:T(8,128)S(1)} %collective-permute-done.3, f32[16,128,256]{2,1,0:T(8,128)} %constant.148.clone, s32[]{:T(128)S(6)} %select_n.142), kind=kOutput, calls=%fused_computation.8 | convolution fusion | flops 50397184 | bytes 589828 | tf_op jit(solution)/shard_map/dot_general | solution.py:60
  35.9 2.0 %collective-permute-start.7 = (f32[128,256]{1,0:T(8,128)S(1)}, f32[128,256]{1,0:T(8,128)S(1)}, u32[]{:S(2)}, u32[]{:S(2)}) collective-permute-start(f32[128,256]{1,0:T(8,128)S(1)} %fusion.5), channel_id=1, source_target_pairs={{0,12},{1,13},{2,14},{3,15},{4,0},{5,1},{6,2},{7,3},{8,4},{9,5},{1... | collective-permute-start | bytes 393224 | tf_op jit(solution)/shard_map/ppermute | solution.py:67
  37.9 0.7 dynamic-slice_multiply_fusion
  38.6 1.5 %collective-permute-start.11 = (f32[4,2,128,128]{3,2,1,0:T(8,128)S(1)}, f32[4,2,128,128]{3,2,1,0:T(8,128)S(1)}, u32[]{:S(2)}, u32[]{:S(2)}) collective-permute-start(f32[4,2,128,128]{3,2,1,0:T(8,128)S(1)} %pad_maximum_fusion), channel_id=1, source_target_pairs={{0,16},{16,0},{32,48},{48,32},{64,80},{80,64},{96,112},{112,96},{1... | collective-permute-start | bytes 1572872 | tf_op jit(solution)/shard_map/ppermute | solution.py:81
  40.1 3.4 %collective-permute-done.5 = f32[128,256]{1,0:T(8,128)S(1)} collective-permute-done((f32[128,256]{1,0:T(8,128)S(1)}, f32[128,256]{1,0:T(8,128)S(1)}, u32[]{:S(2)}, u32[]{:S(2)}) %collective-permute-start.5) | collective-permute-done | bytes 131104 | tf_op jit(solution)/shard_map/ppermute | solution.py:67
  49.8 4.5 %collective-permute-start.12 = (f32[64,256]{1,0:T(8,128)S(1)}, f32[64,256]{1,0:T(8,128)S(1)}, u32[]{:S(2)}, u32[]{:S(2)}) collective-permute-start(f32[64,256]{1,0:T(8,128)S(1)} %fusion.180), channel_id=1, source_target_pairs={{0,1},{1,2},{2,3},{3,0},{4,5},{5,6},{6,7},{7,4},{8,9},{9,10},{10,1... | collective-permute-start | bytes 196616 | tf_op jit(solution)/shard_map/ppermute | solution.py:72
  54.3 2.8 %collective-permute-start.13 = (f32[64,256]{1,0:T(8,128)S(1)}, f32[64,256]{1,0:T(8,128)S(1)}, u32[]{:S(2)}, u32[]{:S(2)}) collective-permute-start(f32[64,256]{1,0:T(8,128)S(1)} %fusion.180), channel_id=1, source_target_pairs={{0,2},{1,3},{2,0},{3,1},{4,6},{5,7},{6,4},{7,5},{8,10},{9,11},{10,... | collective-permute-start | bytes 196616 | tf_op jit(solution)/shard_map/ppermute | solution.py:72
  57.7 4.1 %collective-permute-done.13 = f32[64,256]{1,0:T(8,128)S(1)} collective-permute-done((f32[64,256]{1,0:T(8,128)S(1)}, f32[64,256]{1,0:T(8,128)S(1)}, u32[]{:S(2)}, u32[]{:S(2)}) %collective-permute-start.13) | collective-permute-done | bytes 65568 | tf_op jit(solution)/shard_map/ppermute | solution.py:72
  62.2 0.8 fusion.4
  63.0 1.6 %fusion.179 = f32[64,256]{1,0:T(8,128)S(1)} fusion(f32[256,1024]{1,0:T(8,128)S(1)} %copy-done.1, f32[64,1024]{1,0:T(8,128)S(1)} %fusion.4, s32[256,1024]{1,0:T(8,128)} %param.11, s32[]{:T(128)S(6)} %select_n.129), kind=kOutput, calls=%fused_computation.187 | convolution fusion | flops 201785344 | bytes 1638404 | tf_op jit(solution)/shard_map/dot_general | solution.py:60
  72.5 1.8 %collective-permute-start.18 = (f32[128,256]{1,0:T(8,128)S(1)}, f32[128,256]{1,0:T(8,128)S(1)}, u32[]{:S(2)}, u32[]{:S(2)}) collective-permute-start(f32[128,256]{1,0:T(8,128)S(1)} %pad_maximum_fusion.2), channel_id=1, source_target_pairs={{0,4},{1,5},{2,6},{3,7},{4,8},{5,9},{6,10},{7,11},{8,12},{9,13},{1... | collective-permute-start | bytes 393224 | tf_op jit(solution)/shard_map/ppermute | solution.py:67
  74.2 4.0 %collective-permute-start.19 = (f32[128,256]{1,0:T(8,128)S(1)}, f32[128,256]{1,0:T(8,128)S(1)}, u32[]{:S(2)}, u32[]{:S(2)}) collective-permute-start(f32[128,256]{1,0:T(8,128)S(1)} %pad_maximum_fusion.2), channel_id=1, source_target_pairs={{0,8},{1,9},{2,10},{3,11},{4,12},{5,13},{6,14},{7,15},{8,0},{9,1},... | collective-permute-start | bytes 393224 | tf_op jit(solution)/shard_map/ppermute | solution.py:67
  78.2 1.2 collective-permute-done.18
  79.4 3.2 %collective-permute-done.19 = f32[128,256]{1,0:T(8,128)S(1)} collective-permute-done((f32[128,256]{1,0:T(8,128)S(1)}, f32[128,256]{1,0:T(8,128)S(1)}, u32[]{:S(2)}, u32[]{:S(2)}) %collective-permute-start.19) | collective-permute-done | bytes 131104 | tf_op jit(solution)/shard_map/ppermute | solution.py:67
  82.6 0.7 collective-permute-done.20
  83.3 1.2 %fusion.153 = f32[128,128]{0,1:T(8,128)S(1)} fusion(f32[128,256]{1,0:T(8,128)S(1)} %add_add_fusion, f32[16,128,256]{2,1,0:T(8,128)} %constant.148.clone, s32[]{:T(128)S(6)} %select_n.140), kind=kOutput, calls=%fused_computation.167 | convolution fusion | flops 50331648 | bytes 327684 | tf_op jit(solution)/shard_map/dot_general | solution.py:60
  84.5 1.2 %fusion.148 = f32[128,128]{0,1:T(8,128)S(1)} fusion(f32[128,256]{1,0:T(8,128)S(1)} %add_add_fusion, f32[16,128,256]{2,1,0:T(8,128)} %constant.148.clone, s32[]{:T(128)S(6)} %select_n.142), kind=kOutput, calls=%fused_computation.162 | convolution fusion | flops 50331648 | bytes 327684 | tf_op jit(solution)/shard_map/dot_general | solution.py:60
  85.7 1.2 %fusion.142 = f32[128,128]{0,1:T(8,128)S(1)} fusion(f32[128,256]{1,0:T(8,128)S(1)} %add_add_fusion, f32[16,128,256]{2,1,0:T(8,128)} %constant.148.clone, s32[]{:T(128)S(6)} %select_n.144), kind=kOutput, calls=%fused_computation.156 | convolution fusion | flops 50331648 | bytes 327684 | tf_op jit(solution)/shard_map/dot_general | solution.py:60
  86.9 2.8 %collective-permute-start.21 = (f32[128,128]{0,1:T(8,128)S(1)}, f32[128,128]{0,1:T(8,128)S(1)}, u32[]{:S(2)}, u32[]{:S(2)}) collective-permute-start(f32[128,128]{0,1:T(8,128)S(1)} %fusion.153), channel_id=1, source_target_pairs={{0,1},{1,2},{2,3},{3,0},{4,5},{5,6},{6,7},{7,4},{8,9},{9,10},{10,1... | collective-permute-start | bytes 196616 | tf_op jit(solution)/shard_map/ppermute | solution.py:72
  89.7 2.6 %collective-permute-start.22 = (f32[128,128]{0,1:T(8,128)S(1)}, f32[128,128]{0,1:T(8,128)S(1)}, u32[]{:S(2)}, u32[]{:S(2)}) collective-permute-start(f32[128,128]{0,1:T(8,128)S(1)} %fusion.148), channel_id=1, source_target_pairs={{0,2},{1,3},{2,0},{3,1},{4,6},{5,7},{6,4},{7,5},{8,10},{9,11},{10,... | collective-permute-start | bytes 196616 | tf_op jit(solution)/shard_map/ppermute | solution.py:72
  92.3 1.3 %collective-permute-start.23 = (f32[128,128]{0,1:T(8,128)S(1)}, f32[128,128]{0,1:T(8,128)S(1)}, u32[]{:S(2)}, u32[]{:S(2)}) collective-permute-start(f32[128,128]{0,1:T(8,128)S(1)} %fusion.142), channel_id=1, source_target_pairs={{0,3},{1,0},{2,1},{3,2},{4,7},{5,4},{6,5},{7,6},{8,11},{9,8},{10,9... | collective-permute-start | bytes 196616 | tf_op jit(solution)/shard_map/ppermute | solution.py:72
  93.5 4.0 %collective-permute-done.22 = f32[128,128]{0,1:T(8,128)S(1)} collective-permute-done((f32[128,128]{0,1:T(8,128)S(1)}, f32[128,128]{0,1:T(8,128)S(1)}, u32[]{:S(2)}, u32[]{:S(2)}) %collective-permute-start.22) | collective-permute-done | bytes 65568 | tf_op jit(solution)/shard_map/ppermute | solution.py:72
  97.5 1.2 %fusion.9 = f32[128,128]{0,1:T(8,128)S(1)} fusion(f32[128,128]{0,1:T(8,128)S(1)} %collective-permute-done.23, f32[128,128]{0,1:T(8,128)S(1)} %collective-permute-done.22, f32[128,128]{0,1:T(8,128)S(1)} %collective-permute-done.21, f32[128,256]{1,0:T(8,128)S(1)} %add_add_fusion, f32[16,128,256]{2,1,0:T(8,128)} %constant.148.clone, s32[]{:T(128)S(6)} %select_n.138), kind=kOutput, calls=%fused_computation.14 | convolution fusion | flops 50380800 | bytes 524292 | tf_op jit(solution)/shard_map/dot_general | solution.py:60
  99.3 4.7 %collective-permute-start.24 = (f32[128,64]{0,1:T(8,128)S(1)}, f32[128,64]{0,1:T(8,128)S(1)}, u32[]{:S(2)}, u32[]{:S(2)}) collective-permute-start(f32[128,64]{0,1:T(8,128)S(1)} %get-tuple-element.36), channel_id=1, source_target_pairs={{0,16},{16,32},{32,48},{48,64},{64,80},{80,96},{96,112},{112,128},... | collective-permute-start | bytes 98312 | tf_op jit(solution)/shard_map/ppermute | solution.py:77
  104.1 1.0 collective-permute-start.15
  105.2 3.8 %collective-permute-start.16 = (f32[64,64]{1,0:T(8,128)S(1)}, f32[64,64]{1,0:T(8,128)S(1)}, u32[]{:S(2)}, u32[]{:S(2)}) collective-permute-start(f32[64,64]{1,0:T(8,128)S(1)} %get-tuple-element.29), channel_id=1, source_target_pairs={{0,8},{1,9},{2,10},{3,11},{4,12},{5,13},{6,14},{7,15},{8,0},{9,1},... | collective-permute-start | bytes 49160 | tf_op jit(solution)/shard_map/ppermute | solution.py:67
  111.0 0.8 collective-permute-done.17
  112.5 4.2 %collective-permute-done.25 = f32[128,64]{0,1:T(8,128)S(1)} collective-permute-done((f32[128,64]{0,1:T(8,128)S(1)}, f32[128,64]{0,1:T(8,128)S(1)}, u32[]{:S(2)}, u32[]{:S(2)}) %collective-permute-start.25) | collective-permute-done | bytes 32800 | tf_op jit(solution)/shard_map/ppermute | solution.py:77
  (108 shorter events, 20.7 us)
Async XLA Ops:
  0.6 37.3 %copy-start.2 = (f32[2,2,128,128]{3,2,1,0:T(8,128)S(1)}, f32[2,2,128,128]{3,2,1,0:T(8,128)}, u32[]{:S(2)}) copy-start(f32[2,2,128,128]{3,2,1,0:T(8,128)} %param.12) | copy-start | bytes 786436
  3.5 32.4 %collective-permute-start.8 = (f32[2,128,128]{2,1,0:T(8,128)S(1)}, f32[2,128,128]{2,1,0:T(8,128)S(1)}, u32[]{:S(2)}, u32[]{:S(2)}) collective-permute-start(f32[2,128,128]{2,1,0:T(8,128)S(1)} %fusion.329), channel_id=1, source_target_pairs={{0,4},{1,5},{2,6},{3,7},{4,8},{5,9},{6,10},{7,11},{8,12},{9,13},{1... | collective-permute-start | bytes 393224 | tf_op jit(solution)/shard_map/ppermute | solution.py:67
  4.9 33.7 %collective-permute-start.9 = (f32[2,128,128]{2,1,0:T(8,128)S(1)}, f32[2,128,128]{2,1,0:T(8,128)S(1)}, u32[]{:S(2)}, u32[]{:S(2)}) collective-permute-start(f32[2,128,128]{2,1,0:T(8,128)S(1)} %fusion.329), channel_id=1, source_target_pairs={{0,8},{1,9},{2,10},{3,11},{4,12},{5,13},{6,14},{7,15},{8,0},{9,1},... | collective-permute-start | bytes 393224 | tf_op jit(solution)/shard_map/ppermute | solution.py:67
  7.5 31.1 %collective-permute-start.10 = (f32[2,128,128]{2,1,0:T(8,128)S(1)}, f32[2,128,128]{2,1,0:T(8,128)S(1)}, u32[]{:S(2)}, u32[]{:S(2)}) collective-permute-start(f32[2,128,128]{2,1,0:T(8,128)S(1)} %fusion.329), channel_id=1, source_target_pairs={{0,12},{1,13},{2,14},{3,15},{4,0},{5,1},{6,2},{7,3},{8,4},{9,5},{1... | collective-permute-start | bytes 393224 | tf_op jit(solution)/shard_map/ppermute | solution.py:67
  9.4 5.1 %collective-permute-start.1 = (f32[128,64]{0,1:T(8,128)S(1)}, f32[128,64]{0,1:T(8,128)S(1)}, u32[]{:S(2)}, u32[]{:S(2)}) collective-permute-start(f32[128,64]{0,1:T(8,128)S(1)} %get-tuple-element.61), channel_id=1, source_target_pairs={{0,240},{16,0},{32,16},{48,32},{64,48},{80,64},{96,80},{112,96},{1... | collective-permute-start | bytes 98312 | tf_op jit(solution)/shard_map/ppermute | solution.py:77
  10.9 5.8 %collective-permute-start = (f32[128,64]{0,1:T(8,128)S(1)}, f32[128,64]{0,1:T(8,128)S(1)}, u32[]{:S(2)}, u32[]{:S(2)}) collective-permute-start(f32[128,64]{0,1:T(8,128)S(1)} %get-tuple-element.60), channel_id=1, source_target_pairs={{0,16},{16,32},{32,48},{48,64},{64,80},{80,96},{96,112},{112,128},... | collective-permute-start | bytes 98312 | tf_op jit(solution)/shard_map/ppermute | solution.py:77
  18.8 7.0 %collective-permute-start.2 = (f32[128,128]{0,1:T(8,128)S(1)}, f32[128,128]{0,1:T(8,128)S(1)}, u32[]{:S(2)}, u32[]{:S(2)}) collective-permute-start(f32[128,128]{0,1:T(8,128)S(1)} %pad_maximum_fusion.3), channel_id=1, source_target_pairs={{0,3},{1,0},{2,1},{3,2},{4,7},{5,4},{6,5},{7,6},{8,11},{9,8},{10,9... | collective-permute-start | bytes 196616 | tf_op jit(solution)/shard_map/ppermute | solution.py:72
  24.5 6.2 %collective-permute-start.4 = (f32[128,128]{0,1:T(8,128)S(1)}, f32[128,128]{0,1:T(8,128)S(1)}, u32[]{:S(2)}, u32[]{:S(2)}) collective-permute-start(f32[128,128]{0,1:T(8,128)S(1)} %pad_maximum_fusion.3), channel_id=1, source_target_pairs={{0,1},{1,2},{2,3},{3,0},{4,5},{5,6},{6,7},{7,4},{8,9},{9,10},{10,1... | collective-permute-start | bytes 196616 | tf_op jit(solution)/shard_map/ppermute | solution.py:72
  25.9 7.8 %collective-permute-start.3 = (f32[128,128]{0,1:T(8,128)S(1)}, f32[128,128]{0,1:T(8,128)S(1)}, u32[]{:S(2)}, u32[]{:S(2)}) collective-permute-start(f32[128,128]{0,1:T(8,128)S(1)} %pad_maximum_fusion.3), channel_id=1, source_target_pairs={{0,2},{1,3},{2,0},{3,1},{4,6},{5,7},{6,4},{7,5},{8,10},{9,11},{10,... | collective-permute-start | bytes 196616 | tf_op jit(solution)/shard_map/ppermute | solution.py:72
  32.0 11.9 %copy-start.6 = (f32[256,256]{1,0:T(8,128)S(1)}, f32[256,256]{1,0:T(8,128)}, u32[]{:S(2)}) copy-start(f32[256,256]{1,0:T(8,128)} %constant.149.clone) | copy-start | bytes 786436
  34.9 9.2 %copy-start = (f32[256,512]{1,0:T(8,128)S(1)}, f32[256,512]{1,0:T(8,128)}, u32[]{:S(2)}) copy-start(f32[256,512]{1,0:T(8,128)} %constant.150.clone) | copy-start | bytes 1572868
  34.9 8.7 %collective-permute-start.5 = (f32[128,256]{1,0:T(8,128)S(1)}, f32[128,256]{1,0:T(8,128)S(1)}, u32[]{:S(2)}, u32[]{:S(2)}) collective-permute-start(f32[128,256]{1,0:T(8,128)S(1)} %fusion.5), channel_id=1, source_target_pairs={{0,4},{1,5},{2,6},{3,7},{4,8},{5,9},{6,10},{7,11},{8,12},{9,13},{1... | collective-permute-start | bytes 393224 | tf_op jit(solution)/shard_map/ppermute | solution.py:67
  35.4 8.2 %collective-permute-start.6 = (f32[128,256]{1,0:T(8,128)S(1)}, f32[128,256]{1,0:T(8,128)S(1)}, u32[]{:S(2)}, u32[]{:S(2)}) collective-permute-start(f32[128,256]{1,0:T(8,128)S(1)} %fusion.5), channel_id=1, source_target_pairs={{0,8},{1,9},{2,10},{3,11},{4,12},{5,13},{6,14},{7,15},{8,0},{9,1},... | collective-permute-start | bytes 393224 | tf_op jit(solution)/shard_map/ppermute | solution.py:67
  35.9 7.8 %collective-permute-start.7 = (f32[128,256]{1,0:T(8,128)S(1)}, f32[128,256]{1,0:T(8,128)S(1)}, u32[]{:S(2)}, u32[]{:S(2)}) collective-permute-start(f32[128,256]{1,0:T(8,128)S(1)} %fusion.5), channel_id=1, source_target_pairs={{0,12},{1,13},{2,14},{3,15},{4,0},{5,1},{6,2},{7,3},{8,4},{9,5},{1... | collective-permute-start | bytes 393224 | tf_op jit(solution)/shard_map/ppermute | solution.py:67
  38.6 8.1 %collective-permute-start.11 = (f32[4,2,128,128]{3,2,1,0:T(8,128)S(1)}, f32[4,2,128,128]{3,2,1,0:T(8,128)S(1)}, u32[]{:S(2)}, u32[]{:S(2)}) collective-permute-start(f32[4,2,128,128]{3,2,1,0:T(8,128)S(1)} %pad_maximum_fusion), channel_id=1, source_target_pairs={{0,16},{16,0},{32,48},{48,32},{64,80},{80,64},{96,112},{112,96},{1... | collective-permute-start | bytes 1572872 | tf_op jit(solution)/shard_map/ppermute | solution.py:81
  48.2 14.0 %copy-start.1 = (f32[256,1024]{1,0:T(8,128)S(1)}, f32[256,1024]{1,0:T(8,128)}, u32[]{:S(2)}) copy-start(f32[256,1024]{1,0:T(8,128)} %constant.151.clone) | copy-start | bytes 3145732
  49.8 7.9 %collective-permute-start.12 = (f32[64,256]{1,0:T(8,128)S(1)}, f32[64,256]{1,0:T(8,128)S(1)}, u32[]{:S(2)}, u32[]{:S(2)}) collective-permute-start(f32[64,256]{1,0:T(8,128)S(1)} %fusion.180), channel_id=1, source_target_pairs={{0,1},{1,2},{2,3},{3,0},{4,5},{5,6},{6,7},{7,4},{8,9},{9,10},{10,1... | collective-permute-start | bytes 196616 | tf_op jit(solution)/shard_map/ppermute | solution.py:72
  54.3 7.5 %collective-permute-start.13 = (f32[64,256]{1,0:T(8,128)S(1)}, f32[64,256]{1,0:T(8,128)S(1)}, u32[]{:S(2)}, u32[]{:S(2)}) collective-permute-start(f32[64,256]{1,0:T(8,128)S(1)} %fusion.180), channel_id=1, source_target_pairs={{0,2},{1,3},{2,0},{3,1},{4,6},{5,7},{6,4},{7,5},{8,10},{9,11},{10,... | collective-permute-start | bytes 196616 | tf_op jit(solution)/shard_map/ppermute | solution.py:72
  57.1 5.2 %collective-permute-start.14 = (f32[64,256]{1,0:T(8,128)S(1)}, f32[64,256]{1,0:T(8,128)S(1)}, u32[]{:S(2)}, u32[]{:S(2)}) collective-permute-start(f32[64,256]{1,0:T(8,128)S(1)} %fusion.180), channel_id=1, source_target_pairs={{0,3},{1,0},{2,1},{3,2},{4,7},{5,4},{6,5},{7,6},{8,11},{9,8},{10,9... | collective-permute-start | bytes 196616 | tf_op jit(solution)/shard_map/ppermute | solution.py:72
  72.3 26.4 %copy-start.4 = (f32[128,512]{1,0:T(8,128)S(1)}, f32[128,512]{1,0:T(8,128)}, u32[]{:S(2)}) copy-start(f32[128,512]{1,0:T(8,128)} %constant.147.clone) | copy-start | bytes 786436
  72.3 26.7 %copy-start.3 = (f32[128,512]{1,0:T(8,128)S(1)}, f32[128,512]{1,0:T(8,128)}, u32[]{:S(2)}) copy-start(f32[128,512]{1,0:T(8,128)} %constant.146.clone) | copy-start | bytes 786436
  72.5 6.9 %collective-permute-start.18 = (f32[128,256]{1,0:T(8,128)S(1)}, f32[128,256]{1,0:T(8,128)S(1)}, u32[]{:S(2)}, u32[]{:S(2)}) collective-permute-start(f32[128,256]{1,0:T(8,128)S(1)} %pad_maximum_fusion.2), channel_id=1, source_target_pairs={{0,4},{1,5},{2,6},{3,7},{4,8},{5,9},{6,10},{7,11},{8,12},{9,13},{1... | collective-permute-start | bytes 393224 | tf_op jit(solution)/shard_map/ppermute | solution.py:67
  74.2 8.3 %collective-permute-start.19 = (f32[128,256]{1,0:T(8,128)S(1)}, f32[128,256]{1,0:T(8,128)S(1)}, u32[]{:S(2)}, u32[]{:S(2)}) collective-permute-start(f32[128,256]{1,0:T(8,128)S(1)} %pad_maximum_fusion.2), channel_id=1, source_target_pairs={{0,8},{1,9},{2,10},{3,11},{4,12},{5,13},{6,14},{7,15},{8,0},{9,1},... | collective-permute-start | bytes 393224 | tf_op jit(solution)/shard_map/ppermute | solution.py:67
  78.2 5.1 %collective-permute-start.20 = (f32[128,256]{1,0:T(8,128)S(1)}, f32[128,256]{1,0:T(8,128)S(1)}, u32[]{:S(2)}, u32[]{:S(2)}) collective-permute-start(f32[128,256]{1,0:T(8,128)S(1)} %pad_maximum_fusion.2), channel_id=1, source_target_pairs={{0,12},{1,13},{2,14},{3,15},{4,0},{5,1},{6,2},{7,3},{8,4},{9,5},{1... | collective-permute-start | bytes 393224 | tf_op jit(solution)/shard_map/ppermute | solution.py:67
  86.9 6.7 %collective-permute-start.21 = (f32[128,128]{0,1:T(8,128)S(1)}, f32[128,128]{0,1:T(8,128)S(1)}, u32[]{:S(2)}, u32[]{:S(2)}) collective-permute-start(f32[128,128]{0,1:T(8,128)S(1)} %fusion.153), channel_id=1, source_target_pairs={{0,1},{1,2},{2,3},{3,0},{4,5},{5,6},{6,7},{7,4},{8,9},{9,10},{10,1... | collective-permute-start | bytes 196616 | tf_op jit(solution)/shard_map/ppermute | solution.py:72
  89.7 7.8 %collective-permute-start.22 = (f32[128,128]{0,1:T(8,128)S(1)}, f32[128,128]{0,1:T(8,128)S(1)}, u32[]{:S(2)}, u32[]{:S(2)}) collective-permute-start(f32[128,128]{0,1:T(8,128)S(1)} %fusion.148), channel_id=1, source_target_pairs={{0,2},{1,3},{2,0},{3,1},{4,6},{5,7},{6,4},{7,5},{8,10},{9,11},{10,... | collective-permute-start | bytes 196616 | tf_op jit(solution)/shard_map/ppermute | solution.py:72
  92.3 5.3 %collective-permute-start.23 = (f32[128,128]{0,1:T(8,128)S(1)}, f32[128,128]{0,1:T(8,128)S(1)}, u32[]{:S(2)}, u32[]{:S(2)}) collective-permute-start(f32[128,128]{0,1:T(8,128)S(1)} %fusion.142), channel_id=1, source_target_pairs={{0,3},{1,0},{2,1},{3,2},{4,7},{5,4},{6,5},{7,6},{8,11},{9,8},{10,9... | collective-permute-start | bytes 196616 | tf_op jit(solution)/shard_map/ppermute | solution.py:72
  99.3 13.2 %collective-permute-start.24 = (f32[128,64]{0,1:T(8,128)S(1)}, f32[128,64]{0,1:T(8,128)S(1)}, u32[]{:S(2)}, u32[]{:S(2)}) collective-permute-start(f32[128,64]{0,1:T(8,128)S(1)} %get-tuple-element.36), channel_id=1, source_target_pairs={{0,16},{16,32},{32,48},{48,64},{64,80},{80,96},{96,112},{112,128},... | collective-permute-start | bytes 98312 | tf_op jit(solution)/shard_map/ppermute | solution.py:77
  104.1 5.4 %collective-permute-start.15 = (f32[64,64]{1,0:T(8,128)S(1)}, f32[64,64]{1,0:T(8,128)S(1)}, u32[]{:S(2)}, u32[]{:S(2)}) collective-permute-start(f32[64,64]{1,0:T(8,128)S(1)} %get-tuple-element.30), channel_id=1, source_target_pairs={{0,4},{1,5},{2,6},{3,7},{4,8},{5,9},{6,10},{7,11},{8,12},{9,13},{1... | collective-permute-start | bytes 49160 | tf_op jit(solution)/shard_map/ppermute | solution.py:67
  105.2 5.5 %collective-permute-start.16 = (f32[64,64]{1,0:T(8,128)S(1)}, f32[64,64]{1,0:T(8,128)S(1)}, u32[]{:S(2)}, u32[]{:S(2)}) collective-permute-start(f32[64,64]{1,0:T(8,128)S(1)} %get-tuple-element.29), channel_id=1, source_target_pairs={{0,8},{1,9},{2,10},{3,11},{4,12},{5,13},{6,14},{7,15},{8,0},{9,1},... | collective-permute-start | bytes 49160 | tf_op jit(solution)/shard_map/ppermute | solution.py:67
  109.0 2.8 %collective-permute-start.17 = (f32[64,64]{1,0:T(8,128)S(1)}, f32[64,64]{1,0:T(8,128)S(1)}, u32[]{:S(2)}, u32[]{:S(2)}) collective-permute-start(f32[64,64]{1,0:T(8,128)S(1)} %get-tuple-element.28), channel_id=1, source_target_pairs={{0,12},{1,13},{2,14},{3,15},{4,0},{5,1},{6,2},{7,3},{8,4},{9,5},{1... | collective-permute-start | bytes 49160 | tf_op jit(solution)/shard_map/ppermute | solution.py:67
  112.4 5.0 %copy-start.5 = (f32[256,64]{0,1:T(8,128)}, f32[256,64]{0,1:T(8,128)S(1)}, u32[]{:S(2)}) copy-start(f32[256,64]{0,1:T(8,128)S(1)} %dynamic_update_slice.15) | copy-start | bytes 196612
  112.4 4.3 %collective-permute-start.25 = (f32[128,64]{0,1:T(8,128)S(1)}, f32[128,64]{0,1:T(8,128)S(1)}, u32[]{:S(2)}, u32[]{:S(2)}) collective-permute-start(f32[128,64]{0,1:T(8,128)S(1)} %get-tuple-element.37), channel_id=1, source_target_pairs={{0,240},{16,0},{32,16},{48,32},{64,48},{80,64},{96,80},{112,96},{1... | collective-permute-start | bytes 98312 | tf_op jit(solution)/shard_map/ppermute | solution.py:77

commit v2 on v1

v2 whole, which is shorter than its diff:
```python
import math

import jax
import jax.numpy as jnp
import ml_dtypes
import numpy as np
from jax import lax
from jax.experimental import pallas as pl
from jax.experimental.pallas import tpu as pltpu
from jax.sharding import PartitionSpec as P

COLS = 1024
HALO = 128
FREQS = 128
TILE = 256
WINDOW = 512
SHARD = 64
SAMPLES = 256
QUARTER = 64
COUNT = 8
HALF = 72
EDGE_ROW = 65
WEIGHT_ROW = 67
EXTRA = 32
WIDE = 4 * SHARD
STEEPNESS = 4.0
THRESHOLD = 1.0
F32 = jnp.float32
BF16 = jnp.bfloat16


def angles(places, frequencies, length):
    return (np.outer(places, frequencies) % length) * (2.0 * math.pi / length)


def split_table(value):
    value = value.astype(np.float32)
    high = value.astype(ml_dtypes.bfloat16)
    low = (value - high.astype(np.float32)).astype(ml_dtypes.bfloat16)
    return np.stack([high, low])


def tables():
    freq = np.arange(FREQS) - FREQS // 2
    scale = 1.0 / math.sqrt(WINDOW * COLS)
    win = angles(np.arange(FREQS // 2 + 1), np.arange(WINDOW), WINDOW)
    rows = np.zeros((2, HALF, WINDOW))
    rows[0, : FREQS // 2 + 1] = np.cos(win) * scale
    rows[1, : FREQS // 2 + 1] = np.sin(win) * scale
    rows = rows.reshape(2 * HALF, WINDOW)
    col = angles(np.arange(COLS), freq, COLS)
    keep = FREQS // 2
    band = np.concatenate([np.cos(col[:, keep:]), np.sin(col[:, keep:])], 1)
    band[:, keep] = np.cos(col[:, 0])
    edge = np.zeros((16, COLS))
    edge[0] = np.sin(col[:, 0])
    unfold = np.zeros((FREQS, 2 * FREQS))
    for place, value in enumerate(freq):
        size = abs(value)
        unfold[size, place] = 1.0
        if 0 < size < keep:
            unfold[keep + size, FREQS + place] = np.sign(value)
    flip = np.zeros((FREQS // 2, HALF))
    flip[np.arange(FREQS // 2), FREQS // 2 - np.arange(FREQS // 2)] = 1.0
    out = angles(HALO + np.arange(TILE), freq, WINDOW).reshape(4, QUARTER, FREQS)
    out_rows = np.concatenate([np.cos(out), np.sin(out)], 1) / FREQS
    pix = angles(freq, np.arange(SAMPLES), SAMPLES)
    pix_cos, pix_sin = np.cos(pix), np.sin(pix)
    pixels = np.concatenate(
        [np.concatenate([pix_cos, pix_sin], 1), np.concatenate([-pix_sin, pix_cos], 1)], 0
    )
    gap = np.arange(COLS)[None, :] - (COLS // SAMPLES) * np.arange(SAMPLES)[:, None]
    waves = np.arange(1, SAMPLES // 2)
    base = 2.0 * math.pi / COLS
    line = (1.0 + 2.0 * np.cos(base * np.outer(np.arange(COLS), waves)).sum(1)) / SAMPLES
    spread = line[gap % COLS]
    return {
        "rows": split_table(rows),
        "rows_back": split_table(2.0 * rows),
        "band": split_table(band),
        "band_back": split_table(band.T),
        "edge": split_table(edge),
        "edge_back": edge[:8].astype(np.float32),
        "unfold": unfold.astype(ml_dtypes.bfloat16),
        "fold": unfold.T.astype(ml_dtypes.bfloat16),
        "flip": flip.astype(ml_dtypes.bfloat16),
        "flip_back": flip.T.astype(ml_dtypes.bfloat16),
        "out": split_table(out_rows),
        "out_back": split_table(out_rows.transpose(0, 2, 1)),
        "pixels": split_table(pixels),
        "pixels_back": split_table(pixels.T),
        "spread": split_table(spread),
        "spread_back": split_table(spread.T),
    }


def split(value):
    high = value.astype(BF16)
    low = (value - high.astype(F32)).astype(BF16)
    return high, low


def dot(former, latter):
    return lax.dot_general(
        former, latter, (((1,), (0,)), ((), ())), preferred_element_type=F32
    )


def dot_last(former, latter):
    return lax.dot_general(
        former, latter, (((1,), (1,)), ((), ())), preferred_element_type=F32
    )


def dot3(former, latter, dot=dot):
    return (
        dot(former[0], latter[0]) + dot(former[0], latter[1]) + dot(former[1], latter[0])
    )


def pair(ref):
    return ref[0], ref[1]


def moved(flip, value):
    high, rest = value.astype(BF16), value
    total = dot(flip, high)
    for _ in range(2):
        rest = rest - high.astype(F32)
        high = rest.astype(BF16)
        total = total + dot(flip, high)
    return total


def moved_right(value, flip):
    high, rest = value.astype(BF16), value
    total = dot(high, flip)
    for _ in range(2):
        rest = rest - high.astype(F32)
        high = rest.astype(BF16)
        total = total + dot(high, flip)
    return total


def window_kernel(above_ref, mask_ref, below_ref, rows_ref, out_ref):
    tile = lax.axis_index("tile")
    last = lax.axis_size("tile") - 1
    above = jnp.where(tile > 0, above_ref[:, TILE - HALO :], 0.0)
    below = jnp.where(tile < last, below_ref[:, :HALO], 0.0)
    window = jnp.concatenate([above, mask_ref[...], below], 1)
    done = dot3(pair(rows_ref), split(window), dot_last)
    out_ref[...] = jnp.concatenate([done[:HALF], done[HALF:]], 1)


def padded(row):
    return jnp.concatenate([row, jnp.zeros((1, FREQS - HALF), F32)], 1)


def with_edges(value, edges, weights=()):
    row = lax.broadcasted_iota(jnp.int32, value.shape, 0)
    for slot, edge in enumerate(edges):
        value = jnp.where(row == EDGE_ROW + slot, padded(edge), value)
    for slot, weight in enumerate(weights):
        value = jnp.where(row == WEIGHT_ROW + slot, weight, value)
    return value


def edge_columns(value):
    columns = value[HALF - 8 : HALF].T[:HALF]
    first = EDGE_ROW - (HALF - 8)
    return jnp.concatenate([columns[:, first : first + 1], columns[:, first + 1 : first + 2]], 0)


def band_kernel(
    weight_ref, r0, r1, r2, r3, band_ref, edge_ref, out_ref, order_ref
):
    kern = lax.axis_index("kern")
    at_y, at_z = kern // 4, kern % 4
    for step, ref in enumerate((r0, r1, r2, r3)):
        order_ref[pl.ds((at_z + step) % 4, 1)] = ref[...][None]
    blocks = [order_ref[slot] for slot in range(4)]
    cos = jnp.concatenate([block[:, :SHARD] for block in blocks], 1)
    sin = jnp.concatenate([block[:, SHARD:] for block in blocks], 1)
    rows = split(jnp.concatenate([cos, sin], 0))
    start = pl.multiple_of(at_y * WIDE, WIDE)
    band = tuple(band_ref[i, pl.ds(start, WIDE), :] for i in range(2))
    edge = tuple(edge_ref[i, :, pl.ds(start, WIDE)] for i in range(2))
    done = dot3(rows, band)
    edges = dot3(edge, rows, dot_last)[:1]
    out_ref[...] = with_edges(
        done, (edges[:, :HALF], edges[:, HALF:]), (weight_ref[0], weight_ref[1])
    )


def aerial_kernel(
    p0, p1, p2, p3, h0, h1, h2, h3, unfold_ref, flip_ref, out_rows_ref, pixels_ref,
    field_ref, image_ref,
):
    at_y = lax.axis_index("kern") // 4
    total = (p0[...] + p1[...]) + (p2[...] + p3[...])
    done = moved_right(total, unfold_ref[...])
    lane = lax.broadcasted_iota(jnp.int32, done.shape, 1)
    done = jnp.where(lane == FREQS, edge_columns(total), done)
    cos_cos, cos_sin = done[:HALF, :FREQS], done[:HALF, FREQS:]
    sin_cos, sin_sin = done[HALF:, :FREQS], done[HALF:, FREQS:]
    plus = jnp.concatenate([cos_cos - sin_sin, -(cos_sin + sin_cos)], 1)
    minus = jnp.concatenate([cos_cos + sin_sin, sin_cos - cos_sin], 1)
    spectrum = jnp.concatenate([moved(flip_ref[...], minus), plus[: FREQS // 2]], 0)
    spec_re, spec_im = spectrum[:, :FREQS], spectrum[:, FREQS:]
    out_rows = (
        out_rows_ref[0, pl.ds(at_y, 1)][0],
        out_rows_ref[1, pl.ds(at_y, 1)][0],
    )
    mids = []
    weights = []
    for part_ref, kernel_ref in zip((p0, p1, p2, p3), (h0, h1, h2, h3)):
        for slot in range(2):
            kern_re, kern_im = kernel_ref[slot, 0], kernel_ref[slot, 1]
            row = WEIGHT_ROW + slot
            weights.append(part_ref[row : row + 1, :1])
            band = jnp.concatenate(
                [
                    kern_re * spec_re - kern_im * spec_im,
                    kern_re * spec_im + kern_im * spec_re,
                ],
                1,
            )
            quads = dot3(out_rows, split(band))
            upper, lower = quads[:QUARTER], quads[QUARTER:]
            mids.append(
                jnp.concatenate(
                    [
                        upper[:, :FREQS] - lower[:, FREQS:],
                        upper[:, FREQS:] + lower[:, :FREQS],
                    ],
                    1,
                )
            )
    field = dot3(split(jnp.concatenate(mids, 0)), pair(pixels_ref))
    image = None
    for slot in range(COUNT):
        part = field[slot * QUARTER : (slot + 1) * QUARTER]
        heavy = part * weights[slot]
        field_ref[slot * QUARTER : (slot + 1) * QUARTER, :] = heavy
        part = part * heavy
        part = part[:, :SAMPLES] + part[:, SAMPLES:]
        image = part if image is None else image + part
    image_ref[...] = image


def slope_kernel(
    i0, i1, i2, i3, goal_ref, field_ref, h0, h1, h2, h3,
    spread_ref, spread_back_ref, pixels_back_ref, out_back_ref, flip_back_ref,
    fold_ref, m0, m1, m2, m3, resist_ref,
):
    kern = lax.axis_index("kern")
    at_y, at_z = kern // 4, kern % 4
    image = (i0[...] + i1[...]) + (i2[...] + i3[...])
    image = dot3(split(image), pair(spread_ref))
    resist = 1.0 / (1.0 + jnp.exp(-STEEPNESS * (image - THRESHOLD)))
    goal = goal_ref[...].astype(F32)
    slope = 2.0 * STEEPNESS * (resist - goal) * resist * (1.0 - resist)
    slope = slope.astype(BF16)
    slope = dot(slope, spread_back_ref[0]) + dot(slope, spread_back_ref[1])
    slope = jnp.concatenate([slope, slope], 1)
    weighted = jnp.concatenate(
        [slope * field_ref[slot * QUARTER : (slot + 1) * QUARTER, :] for slot in range(COUNT)], 0
    )
    freqs = dot3(split(weighted), pair(pixels_back_ref))
    out_back = (
        out_back_ref[0, pl.ds(at_y, 1)][0],
        out_back_ref[1, pl.ds(at_y, 1)][0],
    )
    grad_re = grad_im = None
    for slot in range(COUNT):
        kernel_ref = (h0, h1, h2, h3)[slot // 2]
        kern_re, kern_im = kernel_ref[slot % 2, 0], kernel_ref[slot % 2, 1]
        part = freqs[slot * QUARTER : (slot + 1) * QUARTER]
        block = jnp.concatenate(
            [part, jnp.concatenate([part[:, FREQS:], -part[:, :FREQS]], 1)], 0
        )
        adjoint = dot3(out_back, split(block))
        adj_re, adj_im = adjoint[:, :FREQS], adjoint[:, FREQS:]
        term_re = kern_re * adj_re + kern_im * adj_im
        term_im = kern_re * adj_im - kern_im * adj_re
        grad_re = term_re if grad_re is None else grad_re + term_re
        grad_im = term_im if grad_im is None else grad_im + term_im
    grad = jnp.concatenate([grad_re, grad_im], 1)
    plus = jnp.concatenate(
        [grad[FREQS // 2 :], jnp.zeros((HALF - FREQS // 2, 2 * FREQS), F32)], 0
    )
    minus = moved(flip_back_ref[...], grad[: FREQS // 2])
    both, less = plus + minus, minus - plus
    done = jnp.concatenate(
        [
            jnp.concatenate([both[:, :FREQS], -both[:, FREQS:]], 1),
            jnp.concatenate([less[:, FREQS:], less[:, :FREQS]], 1),
        ],
        0,
    )
    first = done[:, FREQS : FREQS + 8].T[:1]
    done = moved_right(done, fold_ref[...])
    done = with_edges(done, (first[:, :HALF], first[:, HALF:]))
    resist_ref[...] = resist
    for step, message in enumerate((m0, m1, m2, m3)):
        message[: 2 * HALF, :] = done
        block = 4 * ((at_y + step) % 4) + at_z
        start = pl.multiple_of((block // 2) * 2 * SHARD, 2 * SHARD)
        wide = resist_ref[:, pl.ds(start, 2 * SHARD)].T
        piece = jnp.where(block % 2 == 0, wide[:SHARD], wide[SHARD:])
        message[2 * HALF :, :] = jnp.concatenate([piece[:EXTRA], piece[EXTRA:]], 1)


def columns_kernel(
    m0, m1, m2, m3, band_back_ref, edge_ref, g0, g1, g2, g3, resist_ref, order_ref
):
    kern = lax.axis_index("kern")
    at_y, at_z = kern // 4, kern % 4
    rows = slice(0, 2 * HALF)
    total = (m0[rows] + m1[rows]) + (m2[rows] + m3[rows])
    start = pl.multiple_of(at_y * WIDE, WIDE)
    band = tuple(band_back_ref[i, :, pl.ds(start, WIDE)] for i in range(2))
    done = dot3(split(total), band)
    done = done + edge_columns(total) * edge_ref[:1, pl.ds(start, WIDE)]
    for slot in range(4):
        cols = slice(slot * SHARD, (slot + 1) * SHARD)
        order_ref[slot] = jnp.concatenate([done[:HALF, cols], done[HALF:, cols]], 1)
    for step, out in enumerate((g0, g1, g2, g3)):
        out[...] = order_ref[pl.ds((at_z + step) % 4, 1)][0]
    pieces = []
    for message in (m0, m1, m2, m3):
        piece = message[2 * HALF :, :]
        pieces.append(jnp.concatenate([piece[:, :SHARD], piece[:, SHARD:]], 0))
    spots = []
    for slot in range(4):
        spot = pieces[0]
        for step in (1, 2, 3):
            spot = jnp.where((at_y - step + 4) % 4 == slot, pieces[step], spot)
        spots.append(spot)
    resist_ref[...] = jnp.concatenate(spots, 1)


def stack(value):
    value = value.T
    return split(value[:SHARD]), split(value[SHARD:])


def final_kernel(above_ref, own_ref, below_ref, rows_ref, out_ref):
    tile = lax.axis_index("tile")
    last = lax.axis_size("tile") - 1
    above = stack(jnp.where(tile > 0, above_ref[...], 0.0))
    below = stack(jnp.where(tile < last, below_ref[...], 0.0))
    own = stack(own_ref[...])

    def rows(value, first, count):
        total = None
        for half in range(2):
            part = dot3(
                value[half],
                tuple(
                    rows_ref[i, half * HALF : (half + 1) * HALF, first : first + count]
                    for i in range(2)
                ),
            )
            total = part if total is None else total + part
        return total

    out_ref[:, :HALO] = rows(own, HALO, HALO) + rows(above, WINDOW - HALO, HALO)
    out_ref[:, HALO:] = rows(own, 2 * HALO, HALO) + rows(below, 0, HALO)


def call(kernel, shapes, *operands, flops=10**7, smem=(), scratch=()):
    many = isinstance(shapes, list)
    spec = lambda i: pl.BlockSpec(
        memory_space=pltpu.SMEM if i in smem else pltpu.VMEM
    )
    out = [jax.ShapeDtypeStruct(shape, F32) for shape in (shapes if many else [shapes])]
    return pl.pallas_call(
        kernel,
        scratch_shapes=list(scratch),
        out_shape=out if many else out[0],
        in_specs=[spec(i) for i in range(len(operands))],
        out_specs=[pl.BlockSpec(memory_space=pltpu.VMEM)] * len(out)
        if many
        else pl.BlockSpec(memory_space=pltpu.VMEM),
        compiler_params=pltpu.CompilerParams(vmem_limit_bytes=32 * 2**20),
        cost_estimate=pl.CostEstimate(flops=flops, bytes_accessed=10**6, transcendentals=0),
        name=kernel.__name__,
    )(*operands)


def shift_y(value, step):
    route = [(4 * y + z, 4 * ((y + step) % 4) + z) for y in range(4) for z in range(4)]
    return lax.ppermute(value, "kern", route)


def shift_z(value, step):
    route = [(4 * y + z, 4 * y + (z + step) % 4) for y in range(4) for z in range(4)]
    return lax.ppermute(value, "kern", route)


def shift_tile(value, step):
    peers = lax.axis_size("tile")
    return lax.ppermute(value, "tile", [(i, (i + step) % peers) for i in range(peers)])


def per_device(mask_field, target, kernel_spectra, kernel_weight):
    table = {name: jnp.asarray(value) for name, value in tables().items()}
    at_y = lax.axis_index("kern") // 4
    order = [pltpu.VMEM((4, HALF, 2 * SHARD), F32)]
    mask_field = mask_field.T
    above = shift_tile(mask_field, 1)
    below = shift_tile(mask_field, -1)
    kernels = [kernel_spectra] + [shift_y(kernel_spectra, step) for step in (1, 2, 3)]

    rows = call(
        window_kernel, (HALF, 2 * SHARD), above, mask_field, below, table["rows"]
    )
    rows = [rows] + [shift_z(rows, -step) for step in (1, 2, 3)]
    *rows, h1, h2, h3 = lax.optimization_barrier((*rows, *kernels[1:]))
    kernels = [kernel_spectra, h1, h2, h3]
    part = call(
        band_kernel, (2 * HALF, FREQS), kernel_weight, *rows, table["band"],
        table["edge"], smem=(0,), scratch=order,
    )
    parts = [part] + [shift_y(part, step) for step in (1, 2, 3)]
    field, image = call(
        aerial_kernel,
        [(COUNT * QUARTER, 2 * SAMPLES), (QUARTER, SAMPLES)],
        *parts, *kernels, table["unfold"], table["flip"], table["out"],
        table["pixels"], flops=6 * 10**8,
    )
    images = [image] + [shift_z(image, step) for step in (1, 2, 3)]
    goal = lax.dynamic_slice_in_dim(target, at_y * QUARTER, QUARTER, 0)
    *messages, _ = call(
        slope_kernel,
        [(2 * HALF + EXTRA, FREQS)] * 4 + [(QUARTER, COLS)],
        *images, goal, field, *kernels, table["spread"], table["spread_back"],
        table["pixels_back"], table["out_back"], table["flip_back"], table["fold"],
        flops=6 * 10**8,
    )
    messages = [messages[0]] + [shift_y(messages[step], step) for step in (1, 2, 3)]
    *grads, resist = call(
        columns_kernel,
        [(HALF, 2 * SHARD)] * 4 + [(SHARD, TILE)],
        *messages, table["band_back"], table["edge_back"], scratch=order,
    )
    grad = grads[0]
    for step in (1, 2, 3):
        grad = grad + shift_z(grads[step], step)
    mask_grad = call(
        final_kernel, (SHARD, TILE), shift_tile(grad, 1), grad, shift_tile(grad, -1),
        table["rows_back"],
    )
    return (resist.T, mask_grad.T)


def solution(mesh):
    in_specs = (P("tile", "kern"), P("tile", None), P("kern", None, None, None), P("kern"))
    out_specs = (P("tile", "kern"), P("tile", "kern"))
    return jax.shard_map(
        per_device, mesh=mesh, in_specs=in_specs, out_specs=out_specs, check_vma=False
    )
```

time: 118 us -> 83.9 us (0.71)
  the two profiles are of different devices: /device:TPU:33 before, /device:TPU:64 now
where the time goes in v2:
time: 83.9 us; the launch traced here: 83.7 us
  starting transfers between devices  37.2 us (44%)
  waiting for transfers between devices  34.1 us (41%)
  Pallas kernels  7.77 us (9%)
  local copies, waits for them, and re-layouts  3.77 us (4%)
    ppermute x9, starting transfers between devices, shift_z(): return lax.ppermute(value, 'kern', route)  21.5 us
    ppermute x9, waiting for transfers between devices, shift_z(): return lax.ppermute(value, 'kern', route)  13.6 us
    ppermute x9, starting transfers between devices, shift_y(): return lax.ppermute(value, 'kern', route)  12.4 us
    ppermute x4, waiting for transfers between devices, shift_tile(): lax.ppermute(value, 'tile', [(i, (i + step) % peers) for i in range(peers)])  11.1 us
    ppermute x9, waiting for transfers between devices, shift_y(): return lax.ppermute(value, 'kern', route)  9.41 us
    pallas_call x6, Pallas kernels, call(): pl.pallas_call(kernel, scratch_shapes=list(scratch), out_shape=out if man...  7.77 us
    unnamed x40, local copies, waits for them, and re-layouts  3.75 us
    ppermute x4, starting transfers between devices, shift_tile(): lax.ppermute(value, 'tile', [(i, (i + step) % peers) for i in range(peers)])  3.29 us
  transfers between devices with their start and end apart: 22, of which 16 were waited for; matrix products, arithmetic and copies ran while one was open for 0% of the time, Pallas kernels for 0%

profile of v2, /device:TPU:64, one launch (start us, length us, event | category | flops | bytes accessed | tf_op | source)
XLA Modules:
  0.0 83.7 jit_solution(14880877410457496020)
XLA Ops:
  0.6 0.0 copy-start
  0.6 0.0 copy-start.5
  0.7 3.1 %collective-permute-start.7 = (f32[2,2,128,128]{3,2,1,0:T(8,128)}, f32[2,2,128,128]{3,2,1,0:T(8,128)S(1)}, u32[]{:S(2)}, u32[]{:S(2)}) collective-permute-start(f32[2,2,128,128]{3,2,1,0:T(8,128)} %h0.3), channel_id=1, source_target_pairs={{0,12},{1,13},{2,14},{3,15},{4,0},{5,1},{6,2},{7,3},{8,4},{9,5},{1... | collective-permute-start | bytes 786440 | tf_op jit(solution)/shard_map/ppermute | solution.py:394
  3.7 0.6 collective-permute-start.6
  4.4 1.0 %collective-permute-start.5 = (f32[2,2,128,128]{3,2,1,0:T(8,128)}, f32[2,2,128,128]{3,2,1,0:T(8,128)S(1)}, u32[]{:S(2)}, u32[]{:S(2)}) collective-permute-start(f32[2,2,128,128]{3,2,1,0:T(8,128)} %h0.3), channel_id=1, source_target_pairs={{0,4},{1,5},{2,6},{3,7},{4,8},{5,9},{6,10},{7,11},{8,12},{9,13},{1... | collective-permute-start | bytes 786440 | tf_op jit(solution)/shard_map/ppermute | solution.py:394
  5.4 2.7 %collective-permute-start.1 = (f32[64,256]{1,0:T(8,128)}, f32[64,256]{1,0:T(8,128)S(1)}, u32[]{:S(2)}, u32[]{:S(2)}) collective-permute-start(f32[64,256]{1,0:T(8,128)} %bitcast.3), channel_id=1, source_target_pairs={{0,240},{16,0},{32,16},{48,32},{64,48},{80,64},{96,80},{112,96},{1... | collective-permute-start | bytes 196616 | tf_op jit(solution)/shard_map/ppermute | solution.py:404
  8.1 2.2 %collective-permute-done.1.below_ref = f32[64,256]{1,0:T(8,128)S(1)} collective-permute-done((f32[64,256]{1,0:T(8,128)}, f32[64,256]{1,0:T(8,128)S(1)}, u32[]{:S(2)}, u32[]{:S(2)}) %collective-permute-start.1) | collective-permute-done | bytes 65568 | tf_op jit(solution)/shard_map/ppermute | solution.py:404
  10.3 3.8 %collective-permute-done.above_ref = f32[64,256]{1,0:T(8,128)S(1)} collective-permute-done((f32[64,256]{1,0:T(8,128)}, f32[64,256]{1,0:T(8,128)S(1)}, u32[]{:S(2)}, u32[]{:S(2)}) %collective-permute-start) | collective-permute-done | bytes 65568 | tf_op jit(solution)/shard_map/ppermute | solution.py:404
  14.1 1.0 %copy-done.7 = bf16[2,144,512]{2,1,0:T(8,128)(2,1)S(1)} copy-done((bf16[2,144,512]{2,1,0:T(8,128)(2,1)S(1)}, bf16[2,144,512]{2,1,0:T(8,128)(2,1)}, u32[]{:S(2)}) %copy-start.7) | copy-done | bytes 294936
  15.0 0.8 %copy-done.11 = f32[256,64]{0,1:T(8,128)S(1)} copy-done((f32[256,64]{0,1:T(8,128)S(1)}, f32[256,64]{0,1:T(8,128)}, u32[]{:S(2)}) %copy-start.11) | copy-done | bytes 65560
  15.9 0.3 window_kernel.1.r0
  16.2 3.7 %collective-permute-start.4 = (f32[72,128]{1,0:T(8,128)S(1)}, f32[72,128]{1,0:T(8,128)S(1)}, u32[]{:S(2)}, u32[]{:S(2)}) collective-permute-start(f32[72,128]{1,0:T(8,128)S(1)} %window_kernel.1.r0), channel_id=1, source_target_pairs={{0,1},{1,2},{2,3},{3,0},{4,5},{5,6},{6,7},{7,4},{8,9},{9,10},{10,1... | collective-permute-start | bytes 110600 | tf_op jit(solution)/shard_map/ppermute | solution.py:399
  19.9 1.0 %collective-permute-start.3 = (f32[72,128]{1,0:T(8,128)S(1)}, f32[72,128]{1,0:T(8,128)S(1)}, u32[]{:S(2)}, u32[]{:S(2)}) collective-permute-start(f32[72,128]{1,0:T(8,128)S(1)} %window_kernel.1.r0), channel_id=1, source_target_pairs={{0,2},{1,3},{2,0},{3,1},{4,6},{5,7},{6,4},{7,5},{8,10},{9,11},{10,... | collective-permute-start | bytes 110600 | tf_op jit(solution)/shard_map/ppermute | solution.py:399
  20.9 0.6 collective-permute-done.4.r3
  21.5 2.2 %collective-permute-start.2 = (f32[72,128]{1,0:T(8,128)S(1)}, f32[72,128]{1,0:T(8,128)S(1)}, u32[]{:S(2)}, u32[]{:S(2)}) collective-permute-start(f32[72,128]{1,0:T(8,128)S(1)} %window_kernel.1.r0), channel_id=1, source_target_pairs={{0,3},{1,0},{2,1},{3,2},{4,7},{5,4},{6,5},{7,6},{8,11},{9,8},{10,9... | collective-permute-start | bytes 110600 | tf_op jit(solution)/shard_map/ppermute | solution.py:399
  23.7 4.0 %collective-permute-done.3.r2 = f32[72,128]{1,0:T(8,128)S(1)} collective-permute-done((f32[72,128]{1,0:T(8,128)S(1)}, f32[72,128]{1,0:T(8,128)S(1)}, u32[]{:S(2)}, u32[]{:S(2)}) %collective-permute-start.3) | collective-permute-done | bytes 36896 | tf_op jit(solution)/shard_map/ppermute | solution.py:399
  27.8 0.1 collective-permute-done.2.r1
  27.9 0.0 copy-start.12
  27.9 0.8 copy-done.12
  28.8 0.9 %band_kernel.1.p0 = f32[144,128]{1,0:T(8,128)S(1)} custom-call(f32[2]{0:T(128)S(1)} %copy-done.15, f32[72,128]{1,0:T(8,128)S(1)} %window_kernel.1.r0, f32[72,128]{1,0:T(8,128)S(1)} %collective-permute-done.2.r1, f32[72,128]{1,0:T(8,128)S(1)} %collective-permute-done.3.r2, f32[72,128]{1,0:T(8,128)S(1)} %collective-permute-done.4.r3, ...), custom_call_target="tpu_custom_call" | custom-call | flops 10000000 | bytes 1000000 | tf_op jit(solution)/shard_map/band_kernel/pallas_call | solution.py:378
  29.7 2.3 %collective-permute-start.10 = (f32[144,128]{1,0:T(8,128)S(1)}, f32[144,128]{1,0:T(8,128)S(1)}, u32[]{:S(2)}, u32[]{:S(2)}) collective-permute-start(f32[144,128]{1,0:T(8,128)S(1)} %band_kernel.1.p0), channel_id=1, source_target_pairs={{0,12},{1,13},{2,14},{3,15},{4,0},{5,1},{6,2},{7,3},{8,4},{9,5},{1... | collective-permute-start | bytes 221192 | tf_op jit(solution)/shard_map/ppermute | solution.py:394
  32.0 1.7 %collective-permute-start.9 = (f32[144,128]{1,0:T(8,128)S(1)}, f32[144,128]{1,0:T(8,128)S(1)}, u32[]{:S(2)}, u32[]{:S(2)}) collective-permute-start(f32[144,128]{1,0:T(8,128)S(1)} %band_kernel.1.p0), channel_id=1, source_target_pairs={{0,8},{1,9},{2,10},{3,11},{4,12},{5,13},{6,14},{7,15},{8,0},{9,1},... | collective-permute-start | bytes 221192 | tf_op jit(solution)/shard_map/ppermute | solution.py:394
  33.7 0.4 collective-permute-done.10.p3
  34.1 3.8 %collective-permute-done.9.p2 = f32[144,128]{1,0:T(8,128)S(1)} collective-permute-done((f32[144,128]{1,0:T(8,128)S(1)}, f32[144,128]{1,0:T(8,128)S(1)}, u32[]{:S(2)}, u32[]{:S(2)}) %collective-permute-start.9) | collective-permute-done | bytes 73760 | tf_op jit(solution)/shard_map/ppermute | solution.py:394
  37.8 1.4 %collective-permute-done.8.p1 = f32[144,128]{1,0:T(8,128)S(1)} collective-permute-done((f32[144,128]{1,0:T(8,128)S(1)}, f32[144,128]{1,0:T(8,128)S(1)}, u32[]{:S(2)}, u32[]{:S(2)}) %collective-permute-start.8) | collective-permute-done | bytes 73760 | tf_op jit(solution)/shard_map/ppermute | solution.py:394
  39.3 1.0 %copy-done.16 = bf16[2,256,512]{2,1,0:T(8,128)(2,1)S(1)} copy-done((bf16[2,256,512]{2,1,0:T(8,128)(2,1)S(1)}, bf16[2,256,512]{2,1,0:T(8,128)(2,1)}, u32[]{:S(2)}) %copy-start.16) | copy-done | bytes 524312
  40.3 1.5 %aerial_kernel.1 = (f32[512,512]{1,0:T(8,128)S(1)}, f32[64,256]{1,0:T(8,128)S(1)}) custom-call(f32[144,128]{1,0:T(8,128)S(1)} %band_kernel.1.p0, f32[144,128]{1,0:T(8,128)S(1)} %collective-permute-done.8.p1, f32[144,128]{1,0:T(8,128)S(1)} %collective-permute-done.9.p2, f32[144,128]{1,0:T(8,128)S(1)} %collective-permute-done.10.p3, ...), custom_call_target="tpu_custom_call" | custom-call | flops 600000000 | bytes 1000000 | tf_op jit(solution)/shard_map/aerial_kernel/pallas_call | solution.py:378
  41.8 0.8 collective-permute-start.13
  42.6 4.6 %collective-permute-start.12 = (f32[64,256]{1,0:T(8,128)S(1)}, f32[64,256]{1,0:T(8,128)S(1)}, u32[]{:S(2)}, u32[]{:S(2)}) collective-permute-start(f32[64,256]{1,0:T(8,128)S(1)} %get-tuple-element.27.i0), channel_id=1, source_target_pairs={{0,2},{1,3},{2,0},{3,1},{4,6},{5,7},{6,4},{7,5},{8,10},{9,11},{10,... | collective-permute-start | bytes 196616 | tf_op jit(solution)/shard_map/ppermute | solution.py:399
  47.2 2.9 %collective-permute-start.11 = (f32[64,256]{1,0:T(8,128)S(1)}, f32[64,256]{1,0:T(8,128)S(1)}, u32[]{:S(2)}, u32[]{:S(2)}) collective-permute-start(f32[64,256]{1,0:T(8,128)S(1)} %get-tuple-element.27.i0), channel_id=1, source_target_pairs={{0,1},{1,2},{2,3},{3,0},{4,5},{5,6},{6,7},{7,4},{8,9},{9,10},{10,1... | collective-permute-start | bytes 196616 | tf_op jit(solution)/shard_map/ppermute | solution.py:399
  50.1 0.9 %collective-permute-done.12.i2 = f32[64,256]{1,0:T(8,128)S(1)} collective-permute-done((f32[64,256]{1,0:T(8,128)S(1)}, f32[64,256]{1,0:T(8,128)S(1)}, u32[]{:S(2)}, u32[]{:S(2)}) %collective-permute-start.12) | collective-permute-done | bytes 65568 | tf_op jit(solution)/shard_map/ppermute | solution.py:399
  51.0 1.8 %collective-permute-done.11.i1 = f32[64,256]{1,0:T(8,128)S(1)} collective-permute-done((f32[64,256]{1,0:T(8,128)S(1)}, f32[64,256]{1,0:T(8,128)S(1)}, u32[]{:S(2)}, u32[]{:S(2)}) %collective-permute-start.11) | collective-permute-done | bytes 65568 | tf_op jit(solution)/shard_map/ppermute | solution.py:399
  52.8 3.1 %slope_kernel.1 = (f32[176,128]{1,0:T(8,128)S(1)}, f32[176,128]{1,0:T(8,128)S(1)}, f32[176,128]{1,0:T(8,128)S(1)}, f32[176,128]{1,0:T(8,128)S(1)}, f32[64,1024]{1,0:T(8,128)}) custom-call(f32[64,256]{1,0:T(8,128)S(1)} %get-tuple-element.27.i0, f32[64,256]{1,0:T(8,128)S(1)} %collective-permute-done.11.i1, f32[64,256]{1,0:T(8,128)S(1)} %collective-permute-done.12.i2, ...), custom_call_target="tpu_custom_call" | custom-call | flops 600000000 | bytes 1000000 | tf_op jit(solution)/shard_map/slope_kernel/pallas_call | solution.py:378
  55.9 1.4 %collective-permute-start.15 = (f32[176,128]{1,0:T(8,128)S(1)}, f32[176,128]{1,0:T(8,128)S(1)}, u32[]{:S(2)}, u32[]{:S(2)}) collective-permute-start(f32[176,128]{1,0:T(8,128)S(1)} %get-tuple-element.31), channel_id=1, source_target_pairs={{0,8},{1,9},{2,10},{3,11},{4,12},{5,13},{6,14},{7,15},{8,0},{9,1},... | collective-permute-start | bytes 270344 | tf_op jit(solution)/shard_map/ppermute | solution.py:394
  57.3 2.3 %collective-permute-start.16 = (f32[176,128]{1,0:T(8,128)S(1)}, f32[176,128]{1,0:T(8,128)S(1)}, u32[]{:S(2)}, u32[]{:S(2)}) collective-permute-start(f32[176,128]{1,0:T(8,128)S(1)} %get-tuple-element.32), channel_id=1, source_target_pairs={{0,12},{1,13},{2,14},{3,15},{4,0},{5,1},{6,2},{7,3},{8,4},{9,5},{1... | collective-permute-start | bytes 270344 | tf_op jit(solution)/shard_map/ppermute | solution.py:394
  59.6 3.0 %collective-permute-done.14.m1 = f32[176,128]{1,0:T(8,128)S(1)} collective-permute-done((f32[176,128]{1,0:T(8,128)S(1)}, f32[176,128]{1,0:T(8,128)S(1)}, u32[]{:S(2)}, u32[]{:S(2)}) %collective-permute-start.14) | collective-permute-done | bytes 90144 | tf_op jit(solution)/shard_map/ppermute | solution.py:394
  62.6 0.9 %collective-permute-done.16.m3 = f32[176,128]{1,0:T(8,128)S(1)} collective-permute-done((f32[176,128]{1,0:T(8,128)S(1)}, f32[176,128]{1,0:T(8,128)S(1)}, u32[]{:S(2)}, u32[]{:S(2)}) %collective-permute-start.16) | collective-permute-done | bytes 90144 | tf_op jit(solution)/shard_map/ppermute | solution.py:394
  63.4 1.0 %columns_kernel.1 = (f32[72,128]{1,0:T(8,128)S(1)}, f32[72,128]{1,0:T(8,128)S(1)}, f32[72,128]{1,0:T(8,128)S(1)}, f32[72,128]{1,0:T(8,128)S(1)}, f32[64,256]{1,0:T(8,128)}) custom-call(f32[176,128]{1,0:T(8,128)S(1)} %get-tuple-element.29.m0, f32[176,128]{1,0:T(8,128)S(1)} %collective-permute-done.14.m1, f32[176,128]{1,0:T(8,128)S(1)} %collective-permute-done.15.m2, ...), custom_call_target="tpu_custom_call" | custom-call | flops 10000000 | bytes 1000000 | tf_op jit(solution)/shard_map/columns_kernel/pallas_call | solution.py:378
  64.5 3.7 %collective-permute-start.17 = (f32[72,128]{1,0:T(8,128)S(1)}, f32[72,128]{1,0:T(8,128)S(1)}, u32[]{:S(2)}, u32[]{:S(2)}) collective-permute-start(f32[72,128]{1,0:T(8,128)S(1)} %get-tuple-element.35), channel_id=1, source_target_pairs={{0,1},{1,2},{2,3},{3,0},{4,5},{5,6},{6,7},{7,4},{8,9},{9,10},{10,1... | collective-permute-start | bytes 110600 | tf_op jit(solution)/shard_map/ppermute | solution.py:399
  68.1 2.7 %collective-permute-start.18 = (f32[72,128]{1,0:T(8,128)S(1)}, f32[72,128]{1,0:T(8,128)S(1)}, u32[]{:S(2)}, u32[]{:S(2)}) collective-permute-start(f32[72,128]{1,0:T(8,128)S(1)} %get-tuple-element.36), channel_id=1, source_target_pairs={{0,2},{1,3},{2,0},{3,1},{4,6},{5,7},{6,4},{7,5},{8,10},{9,11},{10,... | collective-permute-start | bytes 110600 | tf_op jit(solution)/shard_map/ppermute | solution.py:399
  70.8 0.0 collective-permute-start.19
  70.9 5.1 %collective-permute-done.18 = f32[72,128]{1,0:T(8,128)S(1)} collective-permute-done((f32[72,128]{1,0:T(8,128)S(1)}, f32[72,128]{1,0:T(8,128)S(1)}, u32[]{:S(2)}, u32[]{:S(2)}) %collective-permute-start.18) | collective-permute-done | bytes 36896 | tf_op jit(solution)/shard_map/ppermute | solution.py:399
  76.0 1.0 %collective-permute-done.19 = f32[72,128]{1,0:T(8,128)S(1)} collective-permute-done((f32[72,128]{1,0:T(8,128)S(1)}, f32[72,128]{1,0:T(8,128)S(1)}, u32[]{:S(2)}, u32[]{:S(2)}) %collective-permute-start.19) | collective-permute-done | bytes 36896 | tf_op jit(solution)/shard_map/ppermute | solution.py:399
  77.0 0.1 collective-permute-start.21
  77.1 0.5 collective-permute-start.20
  77.6 1.2 %collective-permute-done.21.below_ref = f32[72,128]{1,0:T(8,128)S(1)} collective-permute-done((f32[72,128]{1,0:T(8,128)S(1)}, f32[72,128]{1,0:T(8,128)S(1)}, u32[]{:S(2)}, u32[]{:S(2)}) %collective-permute-start.21) | collective-permute-done | bytes 36896 | tf_op jit(solution)/shard_map/ppermute | solution.py:404
  78.8 3.9 %collective-permute-done.20.above_ref = f32[72,128]{1,0:T(8,128)S(1)} collective-permute-done((f32[72,128]{1,0:T(8,128)S(1)}, f32[72,128]{1,0:T(8,128)S(1)}, u32[]{:S(2)}, u32[]{:S(2)}) %collective-permute-start.20) | collective-permute-done | bytes 36896 | tf_op jit(solution)/shard_map/ppermute | solution.py:404
  82.7 1.0 %final_kernel.1 = f32[64,256]{1,0:T(8,128)} custom-call(f32[72,128]{1,0:T(8,128)S(1)} %collective-permute-done.20.above_ref, f32[72,128]{1,0:T(8,128)S(1)} %add_add_fusion.own_ref, f32[72,128]{1,0:T(8,128)S(1)} %collective-permute-done.21.below_ref, bf16[2,144,512]{2,1,0:T(8,128)(2,1)S(1)} %copy-done.6), custom_call_target="tpu_custom_call" | custom-call | flops 10000000 | bytes 1000000 | tf_op jit(solution)/shard_map/final_kernel/pallas_call | solution.py:378
  (44 shorter events, 0.1 us)
Async XLA Ops:
  0.6 49.4 %copy-start = (s32[256,1024]{1,0:T(8,128)S(1)}, s32[256,1024]{1,0:T(8,128)}, u32[]{:S(2)}) copy-start(s32[256,1024]{1,0:T(8,128)} %param.21) | copy-start | bytes 3145732
  0.6 27.3 %copy-start.5 = (bf16[2,1024,128]{2,1,0:T(8,128)(2,1)S(1)}, bf16[2,1024,128]{2,1,0:T(8,128)(2,1)}, u32[]{:S(2)}) copy-start(bf16[2,1024,128]{2,1,0:T(8,128)(2,1)} %constant.59.clone.band_ref) | copy-start | bytes 1572868
  0.7 27.2 %collective-permute-start.7 = (f32[2,2,128,128]{3,2,1,0:T(8,128)}, f32[2,2,128,128]{3,2,1,0:T(8,128)S(1)}, u32[]{:S(2)}, u32[]{:S(2)}) collective-permute-start(f32[2,2,128,128]{3,2,1,0:T(8,128)} %h0.3), channel_id=1, source_target_pairs={{0,12},{1,13},{2,14},{3,15},{4,0},{5,1},{6,2},{7,3},{8,4},{9,5},{1... | collective-permute-start | bytes 786440 | tf_op jit(solution)/shard_map/ppermute | solution.py:394
  3.7 24.2 %collective-permute-start.6 = (f32[2,2,128,128]{3,2,1,0:T(8,128)}, f32[2,2,128,128]{3,2,1,0:T(8,128)S(1)}, u32[]{:S(2)}, u32[]{:S(2)}) collective-permute-start(f32[2,2,128,128]{3,2,1,0:T(8,128)} %h0.3), channel_id=1, source_target_pairs={{0,8},{1,9},{2,10},{3,11},{4,12},{5,13},{6,14},{7,15},{8,0},{9,1},... | collective-permute-start | bytes 786440 | tf_op jit(solution)/shard_map/ppermute | solution.py:394
  4.4 23.5 %collective-permute-start.5 = (f32[2,2,128,128]{3,2,1,0:T(8,128)}, f32[2,2,128,128]{3,2,1,0:T(8,128)S(1)}, u32[]{:S(2)}, u32[]{:S(2)}) collective-permute-start(f32[2,2,128,128]{3,2,1,0:T(8,128)} %h0.3), channel_id=1, source_target_pairs={{0,4},{1,5},{2,6},{3,7},{4,8},{5,9},{6,10},{7,11},{8,12},{9,13},{1... | collective-permute-start | bytes 786440 | tf_op jit(solution)/shard_map/ppermute | solution.py:394
  5.4 4.9 %collective-permute-start.1 = (f32[64,256]{1,0:T(8,128)}, f32[64,256]{1,0:T(8,128)S(1)}, u32[]{:S(2)}, u32[]{:S(2)}) collective-permute-start(f32[64,256]{1,0:T(8,128)} %bitcast.3), channel_id=1, source_target_pairs={{0,240},{16,0},{32,16},{48,32},{64,48},{80,64},{96,80},{112,96},{1... | collective-permute-start | bytes 196616 | tf_op jit(solution)/shard_map/ppermute | solution.py:404
  8.1 6.0 %collective-permute-start = (f32[64,256]{1,0:T(8,128)}, f32[64,256]{1,0:T(8,128)S(1)}, u32[]{:S(2)}, u32[]{:S(2)}) collective-permute-start(f32[64,256]{1,0:T(8,128)} %bitcast.4), channel_id=1, source_target_pairs={{0,16},{16,32},{32,48},{48,64},{64,80},{80,96},{96,112},{112,128},... | collective-permute-start | bytes 196616 | tf_op jit(solution)/shard_map/ppermute | solution.py:404
  14.1 1.0 %copy-start.7 = (bf16[2,144,512]{2,1,0:T(8,128)(2,1)S(1)}, bf16[2,144,512]{2,1,0:T(8,128)(2,1)}, u32[]{:S(2)}) copy-start(bf16[2,144,512]{2,1,0:T(8,128)(2,1)} %constant.57.clone.rows_ref) | copy-start | bytes 884740
  15.0 0.8 %copy-start.11 = (f32[256,64]{0,1:T(8,128)S(1)}, f32[256,64]{0,1:T(8,128)}, u32[]{:S(2)}) copy-start(f32[256,64]{0,1:T(8,128)} %param.20) | copy-start | bytes 196612
  15.9 12.0 %copy-start.15 = (f32[2]{0:T(128)S(1)}, f32[2]{0:T(128)}, u32[]{:S(2)}) copy-start(f32[2]{0:T(128)} %weight_ref.1) | copy-start | bytes 28
  15.9 23.4 %copy-start.19 = (bf16[64,72]{1,0:T(8,128)(2,1)S(1)}, bf16[64,72]{1,0:T(8,128)(2,1)}, u32[]{:S(2)}) copy-start(bf16[64,72]{1,0:T(8,128)(2,1)} %constant.65.clone.flip_ref) | copy-start | bytes 27652
  16.2 23.0 %copy-start.8 = (f32[2,2,128,128]{3,2,1,0:T(8,128)S(1)}, f32[2,2,128,128]{3,2,1,0:T(8,128)}, u32[]{:S(2)}) copy-start(f32[2,2,128,128]{3,2,1,0:T(8,128)} %h0.3) | copy-start | bytes 786436
  16.2 5.3 %collective-permute-start.4 = (f32[72,128]{1,0:T(8,128)S(1)}, f32[72,128]{1,0:T(8,128)S(1)}, u32[]{:S(2)}, u32[]{:S(2)}) collective-permute-start(f32[72,128]{1,0:T(8,128)S(1)} %window_kernel.1.r0), channel_id=1, source_target_pairs={{0,1},{1,2},{2,3},{3,0},{4,5},{5,6},{6,7},{7,4},{8,9},{9,10},{10,1... | collective-permute-start | bytes 110600 | tf_op jit(solution)/shard_map/ppermute | solution.py:399
  19.9 7.9 %collective-permute-start.3 = (f32[72,128]{1,0:T(8,128)S(1)}, f32[72,128]{1,0:T(8,128)S(1)}, u32[]{:S(2)}, u32[]{:S(2)}) collective-permute-start(f32[72,128]{1,0:T(8,128)S(1)} %window_kernel.1.r0), channel_id=1, source_target_pairs={{0,2},{1,3},{2,0},{3,1},{4,6},{5,7},{6,4},{7,5},{8,10},{9,11},{10,... | collective-permute-start | bytes 110600 | tf_op jit(solution)/shard_map/ppermute | solution.py:399
  21.5 6.4 %collective-permute-start.2 = (f32[72,128]{1,0:T(8,128)S(1)}, f32[72,128]{1,0:T(8,128)S(1)}, u32[]{:S(2)}, u32[]{:S(2)}) collective-permute-start(f32[72,128]{1,0:T(8,128)S(1)} %window_kernel.1.r0), channel_id=1, source_target_pairs={{0,3},{1,0},{2,1},{3,2},{4,7},{5,4},{6,5},{7,6},{8,11},{9,8},{10,9... | collective-permute-start | bytes 110600 | tf_op jit(solution)/shard_map/ppermute | solution.py:399
  27.9 0.8 %copy-start.12 = (bf16[2,16,1024]{2,1,0:T(8,128)(2,1)S(1)}, bf16[2,16,1024]{2,1,0:T(8,128)(2,1)}, u32[]{:S(2)}) copy-start(bf16[2,16,1024]{2,1,0:T(8,128)(2,1)} %constant.61.clone.edge_ref) | copy-start | bytes 196612
  28.8 10.5 %copy-start.17 = (bf16[2,4,128,128]{3,2,1,0:T(8,128)(2,1)S(1)}, bf16[2,4,128,128]{3,2,1,0:T(8,128)(2,1)}, u32[]{:S(2)}) copy-start(bf16[2,4,128,128]{3,2,1,0:T(8,128)(2,1)} %constant.67.clone.out_rows_ref) | copy-start | bytes 786436
  28.8 10.5 %copy-start.18 = (bf16[128,256]{1,0:T(8,128)(2,1)S(1)}, bf16[128,256]{1,0:T(8,128)(2,1)}, u32[]{:S(2)}) copy-start(bf16[128,256]{1,0:T(8,128)(2,1)} %constant.63.clone.unfold_ref) | copy-start | bytes 196612
  28.8 24.0 %copy-start.9 = (bf16[2,4,128,128]{3,2,1,0:T(8,128)(2,1)S(1)}, bf16[2,4,128,128]{3,2,1,0:T(8,128)(2,1)}, u32[]{:S(2)}) copy-start(bf16[2,4,128,128]{3,2,1,0:T(8,128)(2,1)} %constant.68.clone.out_back_ref) | copy-start | bytes 786436
  29.7 4.4 %collective-permute-start.10 = (f32[144,128]{1,0:T(8,128)S(1)}, f32[144,128]{1,0:T(8,128)S(1)}, u32[]{:S(2)}, u32[]{:S(2)}) collective-permute-start(f32[144,128]{1,0:T(8,128)S(1)} %band_kernel.1.p0), channel_id=1, source_target_pairs={{0,12},{1,13},{2,14},{3,15},{4,0},{5,1},{6,2},{7,3},{8,4},{9,5},{1... | collective-permute-start | bytes 221192 | tf_op jit(solution)/shard_map/ppermute | solution.py:394
  32.0 5.9 %collective-permute-start.9 = (f32[144,128]{1,0:T(8,128)S(1)}, f32[144,128]{1,0:T(8,128)S(1)}, u32[]{:S(2)}, u32[]{:S(2)}) collective-permute-start(f32[144,128]{1,0:T(8,128)S(1)} %band_kernel.1.p0), channel_id=1, source_target_pairs={{0,8},{1,9},{2,10},{3,11},{4,12},{5,13},{6,14},{7,15},{8,0},{9,1},... | collective-permute-start | bytes 221192 | tf_op jit(solution)/shard_map/ppermute | solution.py:394
  33.7 5.6 %collective-permute-start.8 = (f32[144,128]{1,0:T(8,128)S(1)}, f32[144,128]{1,0:T(8,128)S(1)}, u32[]{:S(2)}, u32[]{:S(2)}) collective-permute-start(f32[144,128]{1,0:T(8,128)S(1)} %band_kernel.1.p0), channel_id=1, source_target_pairs={{0,4},{1,5},{2,6},{3,7},{4,8},{5,9},{6,10},{7,11},{8,12},{9,13},{1... | collective-permute-start | bytes 221192 | tf_op jit(solution)/shard_map/ppermute | solution.py:394
  33.7 19.1 %copy-start.1 = (bf16[2,1024,256]{2,1,0:T(8,128)(2,1)S(1)}, bf16[2,1024,256]{2,1,0:T(8,128)(2,1)}, u32[]{:S(2)}) copy-start(bf16[2,1024,256]{2,1,0:T(8,128)(2,1)} %constant.72.clone.spread_back_ref) | copy-start | bytes 3145732
  33.7 19.1 %copy-start.2 = (bf16[2,256,1024]{2,1,0:T(8,128)(2,1)S(1)}, bf16[2,256,1024]{2,1,0:T(8,128)(2,1)}, u32[]{:S(2)}) copy-start(bf16[2,256,1024]{2,1,0:T(8,128)(2,1)} %constant.71.clone.spread_ref) | copy-start | bytes 3145732
  39.3 1.0 %copy-start.16 = (bf16[2,256,512]{2,1,0:T(8,128)(2,1)S(1)}, bf16[2,256,512]{2,1,0:T(8,128)(2,1)}, u32[]{:S(2)}) copy-start(bf16[2,256,512]{2,1,0:T(8,128)(2,1)} %constant.69.clone.pixels_ref) | copy-start | bytes 1572868
  40.3 12.4 %copy-start.10 = (bf16[256,128]{1,0:T(8,128)(2,1)S(1)}, bf16[256,128]{1,0:T(8,128)(2,1)}, u32[]{:S(2)}) copy-start(bf16[256,128]{1,0:T(8,128)(2,1)} %constant.64.clone.fold_ref) | copy-start | bytes 196612
  40.3 12.5 %copy-start.14 = (bf16[72,64]{1,0:T(8,128)(2,1)S(1)}, bf16[72,64]{1,0:T(8,128)(2,1)}, u32[]{:S(2)}) copy-start(bf16[72,64]{1,0:T(8,128)(2,1)} %constant.66.clone.flip_back_ref) | copy-start | bytes 27652
  41.8 11.0 %copy-start.3 = (bf16[2,512,256]{2,1,0:T(8,128)(2,1)S(1)}, bf16[2,512,256]{2,1,0:T(8,128)(2,1)}, u32[]{:S(2)}) copy-start(bf16[2,512,256]{2,1,0:T(8,128)(2,1)} %constant.70.clone.pixels_back_ref) | copy-start | bytes 1572868
  41.8 8.2 %collective-permute-start.13 = (f32[64,256]{1,0:T(8,128)S(1)}, f32[64,256]{1,0:T(8,128)S(1)}, u32[]{:S(2)}, u32[]{:S(2)}) collective-permute-start(f32[64,256]{1,0:T(8,128)S(1)} %get-tuple-element.27.i0), channel_id=1, source_target_pairs={{0,3},{1,0},{2,1},{3,2},{4,7},{5,4},{6,5},{7,6},{8,11},{9,8},{10,9... | collective-permute-start | bytes 196616 | tf_op jit(solution)/shard_map/ppermute | solution.py:399
  42.6 8.4 %collective-permute-start.12 = (f32[64,256]{1,0:T(8,128)S(1)}, f32[64,256]{1,0:T(8,128)S(1)}, u32[]{:S(2)}, u32[]{:S(2)}) collective-permute-start(f32[64,256]{1,0:T(8,128)S(1)} %get-tuple-element.27.i0), channel_id=1, source_target_pairs={{0,2},{1,3},{2,0},{3,1},{4,6},{5,7},{6,4},{7,5},{8,10},{9,11},{10,... | collective-permute-start | bytes 196616 | tf_op jit(solution)/shard_map/ppermute | solution.py:399
  47.2 5.6 %collective-permute-start.11 = (f32[64,256]{1,0:T(8,128)S(1)}, f32[64,256]{1,0:T(8,128)S(1)}, u32[]{:S(2)}, u32[]{:S(2)}) collective-permute-start(f32[64,256]{1,0:T(8,128)S(1)} %get-tuple-element.27.i0), channel_id=1, source_target_pairs={{0,1},{1,2},{2,3},{3,0},{4,5},{5,6},{6,7},{7,4},{8,9},{9,10},{10,1... | collective-permute-start | bytes 196616 | tf_op jit(solution)/shard_map/ppermute | solution.py:399
  52.8 10.7 %copy-start.4 = (bf16[2,128,1024]{2,1,0:T(8,128)(2,1)S(1)}, bf16[2,128,1024]{2,1,0:T(8,128)(2,1)}, u32[]{:S(2)}) copy-start(bf16[2,128,1024]{2,1,0:T(8,128)(2,1)} %constant.60.clone.band_back_ref) | copy-start | bytes 1572868
  52.8 10.6 %copy-start.13 = (f32[8,1024]{1,0:T(8,128)S(1)}, f32[8,1024]{1,0:T(8,128)}, u32[]{:S(2)}) copy-start(f32[8,1024]{1,0:T(8,128)} %constant.62.clone.edge_ref) | copy-start | bytes 98308
  55.9 6.7 %collective-permute-start.14 = (f32[176,128]{1,0:T(8,128)S(1)}, f32[176,128]{1,0:T(8,128)S(1)}, u32[]{:S(2)}, u32[]{:S(2)}) collective-permute-start(f32[176,128]{1,0:T(8,128)S(1)} %get-tuple-element.30), channel_id=1, source_target_pairs={{0,4},{1,5},{2,6},{3,7},{4,8},{5,9},{6,10},{7,11},{8,12},{9,13},{1... | collective-permute-start | bytes 270344 | tf_op jit(solution)/shard_map/ppermute | solution.py:394
  55.9 6.7 %collective-permute-start.15 = (f32[176,128]{1,0:T(8,128)S(1)}, f32[176,128]{1,0:T(8,128)S(1)}, u32[]{:S(2)}, u32[]{:S(2)}) collective-permute-start(f32[176,128]{1,0:T(8,128)S(1)} %get-tuple-element.31), channel_id=1, source_target_pairs={{0,8},{1,9},{2,10},{3,11},{4,12},{5,13},{6,14},{7,15},{8,0},{9,1},... | collective-permute-start | bytes 270344 | tf_op jit(solution)/shard_map/ppermute | solution.py:394
  57.3 6.1 %collective-permute-start.16 = (f32[176,128]{1,0:T(8,128)S(1)}, f32[176,128]{1,0:T(8,128)S(1)}, u32[]{:S(2)}, u32[]{:S(2)}) collective-permute-start(f32[176,128]{1,0:T(8,128)S(1)} %get-tuple-element.32), channel_id=1, source_target_pairs={{0,12},{1,13},{2,14},{3,15},{4,0},{5,1},{6,2},{7,3},{8,4},{9,5},{1... | collective-permute-start | bytes 270344 | tf_op jit(solution)/shard_map/ppermute | solution.py:394
  63.4 19.3 %copy-start.6 = (bf16[2,144,512]{2,1,0:T(8,128)(2,1)S(1)}, bf16[2,144,512]{2,1,0:T(8,128)(2,1)}, u32[]{:S(2)}) copy-start(bf16[2,144,512]{2,1,0:T(8,128)(2,1)} %constant.58.clone.rows_ref) | copy-start | bytes 884740
  64.5 6.4 %collective-permute-start.17 = (f32[72,128]{1,0:T(8,128)S(1)}, f32[72,128]{1,0:T(8,128)S(1)}, u32[]{:S(2)}, u32[]{:S(2)}) collective-permute-start(f32[72,128]{1,0:T(8,128)S(1)} %get-tuple-element.35), channel_id=1, source_target_pairs={{0,1},{1,2},{2,3},{3,0},{4,5},{5,6},{6,7},{7,4},{8,9},{9,10},{10,1... | collective-permute-start | bytes 110600 | tf_op jit(solution)/shard_map/ppermute | solution.py:399
  68.1 7.9 %collective-permute-start.18 = (f32[72,128]{1,0:T(8,128)S(1)}, f32[72,128]{1,0:T(8,128)S(1)}, u32[]{:S(2)}, u32[]{:S(2)}) collective-permute-start(f32[72,128]{1,0:T(8,128)S(1)} %get-tuple-element.36), channel_id=1, source_target_pairs={{0,2},{1,3},{2,0},{3,1},{4,6},{5,7},{6,4},{7,5},{8,10},{9,11},{10,... | collective-permute-start | bytes 110600 | tf_op jit(solution)/shard_map/ppermute | solution.py:399
  70.8 6.2 %collective-permute-start.19 = (f32[72,128]{1,0:T(8,128)S(1)}, f32[72,128]{1,0:T(8,128)S(1)}, u32[]{:S(2)}, u32[]{:S(2)}) collective-permute-start(f32[72,128]{1,0:T(8,128)S(1)} %get-tuple-element.37), channel_id=1, source_target_pairs={{0,3},{1,0},{2,1},{3,2},{4,7},{5,4},{6,5},{7,6},{8,11},{9,8},{10,9... | collective-permute-start | bytes 110600 | tf_op jit(solution)/shard_map/ppermute | solution.py:399
  77.0 1.8 %collective-permute-start.21 = (f32[72,128]{1,0:T(8,128)S(1)}, f32[72,128]{1,0:T(8,128)S(1)}, u32[]{:S(2)}, u32[]{:S(2)}) collective-permute-start(f32[72,128]{1,0:T(8,128)S(1)} %add_add_fusion.own_ref), channel_id=1, source_target_pairs={{0,240},{16,0},{32,16},{48,32},{64,48},{80,64},{96,80},{112,96},{1... | collective-permute-start | bytes 110600 | tf_op jit(solution)/shard_map/ppermute | solution.py:404
  77.1 5.6 %collective-permute-start.20 = (f32[72,128]{1,0:T(8,128)S(1)}, f32[72,128]{1,0:T(8,128)S(1)}, u32[]{:S(2)}, u32[]{:S(2)}) collective-permute-start(f32[72,128]{1,0:T(8,128)S(1)} %add_add_fusion.own_ref), channel_id=1, source_target_pairs={{0,16},{16,32},{32,48},{48,64},{64,80},{80,96},{96,112},{112,128},... | collective-permute-start | bytes 110600 | tf_op jit(solution)/shard_map/ppermute | solution.py:404

commit v3 on v2

--- a/solution.py
+++ b/solution.py
@@ -43,17 +43,19 @@
 def tables():
     freq = np.arange(FREQS) - FREQS // 2
     scale = 1.0 / math.sqrt(WINDOW * COLS)
-    win = angles(np.arange(FREQS // 2 + 1), np.arange(WINDOW), WINDOW)
-    rows = np.zeros((2, HALF, WINDOW))
+    win = angles(np.arange(FREQS // 2 + 1), HALO + np.arange(TILE), WINDOW)
+    rows = np.zeros((2, HALF, TILE))
     rows[0, : FREQS // 2 + 1] = np.cos(win) * scale
     rows[1, : FREQS // 2 + 1] = np.sin(win) * scale
-    rows = rows.reshape(2 * HALF, WINDOW)
+    rows = rows.reshape(2 * HALF, TILE)
     col = angles(np.arange(COLS), freq, COLS)
     keep = FREQS // 2
     band = np.concatenate([np.cos(col[:, keep:]), np.sin(col[:, keep:])], 1)
     band[:, keep] = np.cos(col[:, 0])
-    edge = np.zeros((16, COLS))
-    edge[0] = np.sin(col[:, 0])
+    edge = np.sin(col[:, 0])
+    wide = np.zeros((COLS // SHARD, SHARD, 2 * FREQS))
+    wide[:, :, :FREQS] = band.reshape(COLS // SHARD, SHARD, FREQS)
+    wide[:, :, FREQS] = edge.reshape(COLS // SHARD, SHARD)
     unfold = np.zeros((FREQS, 2 * FREQS))
     for place, value in enumerate(freq):
         size = abs(value)
@@ -76,11 +78,9 @@
     spread = line[gap % COLS]
     return {
         "rows": split_table(rows),
-        "rows_back": split_table(2.0 * rows),
-        "band": split_table(band),
+        "band": split_table(wide),
         "band_back": split_table(band.T),
-        "edge": split_table(edge),
-        "edge_back": edge[:8].astype(np.float32),
+        "edge_back": np.tile(edge, (8, 1)).astype(np.float32),
         "unfold": unfold.astype(ml_dtypes.bfloat16),
         "fold": unfold.T.astype(ml_dtypes.bfloat16),
         "flip": flip.astype(ml_dtypes.bfloat16),
@@ -142,27 +142,46 @@
     return total
 
 
-def window_kernel(above_ref, mask_ref, below_ref, rows_ref, out_ref):
+def pair_up(value):
+    return jnp.concatenate([value[:HALF], value[HALF:]], 1)
+
+
+def alternate(shape):
+    return 1.0 - 2.0 * (lax.broadcasted_iota(jnp.int32, shape, 0) % 2).astype(F32)
+
+
+def weight_kernel(weight_ref, out_ref):
+    row = lax.broadcasted_iota(jnp.int32, out_ref.shape, 0)
+    out_ref[...] = jnp.where(row == WEIGHT_ROW - HALF + 8, weight_ref[0], weight_ref[1])
+
+
+def window_kernel(above_ref, below_ref, mask_ref, rows_ref, heavy_ref, out_ref):
     tile = lax.axis_index("tile")
     last = lax.axis_size("tile") - 1
     above = jnp.where(tile > 0, above_ref[:, TILE - HALO :], 0.0)
     below = jnp.where(tile < last, below_ref[:, :HALO], 0.0)
-    window = jnp.concatenate([above, mask_ref[...], below], 1)
-    done = dot3(pair(rows_ref), split(window), dot_last)
-    out_ref[...] = jnp.concatenate([done[:HALF], done[HALF:]], 1)
+    sides = jnp.concatenate([below, above], 1)
+    both = split(jnp.concatenate([mask_ref[...], sides], 0))
+    done = dot3(pair(rows_ref), both, dot_last)
+    own, halo = done[:, :SHARD], done[:, SHARD:]
+    done = pair_up(own) + alternate((HALF, 2 * SHARD)) * pair_up(halo)
+    row = lax.broadcasted_iota(jnp.int32, (8, 2 * SHARD), 0) + HALF - 8
+    out_ref[: HALF - 8] = done[: HALF - 8]
+    out_ref[HALF - 8 :] = jnp.where(row < WEIGHT_ROW, done[HALF - 8 :], heavy_ref[...])
 
 
 def padded(row):
     return jnp.concatenate([row, jnp.zeros((1, FREQS - HALF), F32)], 1)
 
 
-def with_edges(value, edges, weights=()):
+def with_edges(value, edges, weights=None):
     row = lax.broadcasted_iota(jnp.int32, value.shape, 0)
     for slot, edge in enumerate(edges):
         value = jnp.where(row == EDGE_ROW + slot, padded(edge), value)
-    for slot, weight in enumerate(weights):
-        value = jnp.where(row == WEIGHT_ROW + slot, weight, value)
-    return value
+    if weights is None:
+        return value
+    heavy = jnp.concatenate([value[: HALF - 8], weights, value[HALF:]], 0)
+    return jnp.where((row >= WEIGHT_ROW) & (row < HALF), heavy, value)
 
 
 def edge_columns(value):
@@ -171,25 +190,20 @@
     return jnp.concatenate([columns[:, first : first + 1], columns[:, first + 1 : first + 2]], 0)
 
 
-def band_kernel(
-    weight_ref, r0, r1, r2, r3, band_ref, edge_ref, out_ref, order_ref
-):
+def band_kernel(r0, r1, r2, r3, band_ref, out_ref):
     kern = lax.axis_index("kern")
     at_y, at_z = kern // 4, kern % 4
-    for step, ref in enumerate((r0, r1, r2, r3)):
-        order_ref[pl.ds((at_z + step) % 4, 1)] = ref[...][None]
-    blocks = [order_ref[slot] for slot in range(4)]
+    blocks = [ref[...] for ref in (r0, r1, r2, r3)]
     cos = jnp.concatenate([block[:, :SHARD] for block in blocks], 1)
     sin = jnp.concatenate([block[:, SHARD:] for block in blocks], 1)
-    rows = split(jnp.concatenate([cos, sin], 0))
-    start = pl.multiple_of(at_y * WIDE, WIDE)
-    band = tuple(band_ref[i, pl.ds(start, WIDE), :] for i in range(2))
-    edge = tuple(edge_ref[i, :, pl.ds(start, WIDE)] for i in range(2))
-    done = dot3(rows, band)
-    edges = dot3(edge, rows, dot_last)[:1]
-    out_ref[...] = with_edges(
-        done, (edges[:, :HALF], edges[:, HALF:]), (weight_ref[0], weight_ref[1])
-    )
+    places = [4 * at_y + (at_z + step) % 4 for step in range(4)]
+    band = tuple(
+        jnp.concatenate([band_ref[i, pl.ds(place, 1)][0] for place in places], 0)
+        for i in range(2)
+    )
+    done = dot3(split(jnp.concatenate([cos, sin], 0)), band)
+    edges = [done[half : half + HALF, FREQS:].T[:1] for half in (0, HALF)]
+    out_ref[...] = with_edges(done[:, :FREQS], edges, r0[HALF - 8 :])
 
 
 def aerial_kernel(
@@ -312,7 +326,7 @@
 
 
 def columns_kernel(
-    m0, m1, m2, m3, band_back_ref, edge_ref, g0, g1, g2, g3, resist_ref, order_ref
+    m0, m1, m2, m3, band_back_ref, edge_ref, g0, g1, g2, g3, order_ref
 ):
     kern = lax.axis_index("kern")
     at_y, at_z = kern // 4, kern % 4
@@ -327,6 +341,10 @@
         order_ref[slot] = jnp.concatenate([done[:HALF, cols], done[HALF:, cols]], 1)
     for step, out in enumerate((g0, g1, g2, g3)):
         out[...] = order_ref[pl.ds((at_z + step) % 4, 1)][0]
+
+
+def resist_kernel(m0, m1, m2, m3, resist_ref):
+    at_y = lax.axis_index("kern") // 4
     pieces = []
     for message in (m0, m1, m2, m3):
         piece = message[2 * HALF :, :]
@@ -340,40 +358,33 @@
     resist_ref[...] = jnp.concatenate(spots, 1)
 
 
-def stack(value):
-    value = value.T
-    return split(value[:SHARD]), split(value[SHARD:])
-
-
 def final_kernel(above_ref, own_ref, below_ref, rows_ref, out_ref):
     tile = lax.axis_index("tile")
     last = lax.axis_size("tile") - 1
-    above = stack(jnp.where(tile > 0, above_ref[...], 0.0))
-    below = stack(jnp.where(tile < last, below_ref[...], 0.0))
-    own = stack(own_ref[...])
-
-    def rows(value, first, count):
+    own = own_ref[...]
+    sign = 2.0 * alternate(own.shape)
+    own = 2.0 * own
+    sides = (
+        own + jnp.where(tile > 0, above_ref[...], 0.0) * sign,
+        own + jnp.where(tile < last, below_ref[...], 0.0) * sign,
+    )
+    for slot, side in enumerate(sides):
+        side = split(side.T)
+        cols = slice(slot * HALO, (slot + 1) * HALO)
         total = None
         for half in range(2):
             part = dot3(
-                value[half],
-                tuple(
-                    rows_ref[i, half * HALF : (half + 1) * HALF, first : first + count]
-                    for i in range(2)
-                ),
+                (side[0][half * SHARD : (half + 1) * SHARD], side[1][half * SHARD : (half + 1) * SHARD]),
+                tuple(rows_ref[i, half * HALF : (half + 1) * HALF, cols] for i in range(2)),
             )
             total = part if total is None else total + part
-        return total
-
-    out_ref[:, :HALO] = rows(own, HALO, HALO) + rows(above, WINDOW - HALO, HALO)
-    out_ref[:, HALO:] = rows(own, 2 * HALO, HALO) + rows(below, 0, HALO)
-
-
-def call(kernel, shapes, *operands, flops=10**7, smem=(), scratch=()):
+        out_ref[:, cols] = total
+
+
+def call(kernel, shapes, *operands, flops=4 * 10**9, smem=(), hbm=(), scratch=()):
     many = isinstance(shapes, list)
-    spec = lambda i: pl.BlockSpec(
-        memory_space=pltpu.SMEM if i in smem else pltpu.VMEM
-    )
+    space = lambda i: pltpu.SMEM if i in smem else pltpu.HBM if i in hbm else pltpu.VMEM
+    spec = lambda i: pl.BlockSpec(memory_space=space(i))
     out = [jax.ShapeDtypeStruct(shape, F32) for shape in (shapes if many else [shapes])]
     return pl.pallas_call(
         kernel,
@@ -411,38 +422,40 @@
     mask_field = mask_field.T
     above = shift_tile(mask_field, 1)
     below = shift_tile(mask_field, -1)
+    heavy = call(weight_kernel, (8, 2 * SHARD), kernel_weight, smem=(0,))
+    kernel_spectra, heavy = lax.optimization_barrier((kernel_spectra, heavy))
     kernels = [kernel_spectra] + [shift_y(kernel_spectra, step) for step in (1, 2, 3)]
 
     rows = call(
-        window_kernel, (HALF, 2 * SHARD), above, mask_field, below, table["rows"]
+        window_kernel, (HALF, 2 * SHARD), above, below, mask_field, table["rows"], heavy
     )
     rows = [rows] + [shift_z(rows, -step) for step in (1, 2, 3)]
-    *rows, h1, h2, h3 = lax.optimization_barrier((*rows, *kernels[1:]))
-    kernels = [kernel_spectra, h1, h2, h3]
+    *rows, h1, h3 = lax.optimization_barrier((*rows, kernels[1], kernels[3]))
+    kernels = [kernel_spectra, h1, kernels[2], h3]
     part = call(
-        band_kernel, (2 * HALF, FREQS), kernel_weight, *rows, table["band"],
-        table["edge"], smem=(0,), scratch=order,
+        band_kernel, (2 * HALF, FREQS), *rows, table["band"]
     )
     parts = [part] + [shift_y(part, step) for step in (1, 2, 3)]
     field, image = call(
         aerial_kernel,
         [(COUNT * QUARTER, 2 * SAMPLES), (QUARTER, SAMPLES)],
         *parts, *kernels, table["unfold"], table["flip"], table["out"],
-        table["pixels"], flops=6 * 10**8,
+        table["pixels"], flops=4 * 10**9,
     )
     images = [image] + [shift_z(image, step) for step in (1, 2, 3)]
     goal = lax.dynamic_slice_in_dim(target, at_y * QUARTER, QUARTER, 0)
-    *messages, _ = call(
+    messages = call(
         slope_kernel,
-        [(2 * HALF + EXTRA, FREQS)] * 4 + [(QUARTER, COLS)],
+        [(2 * HALF + EXTRA, FREQS)] * 4,
         *images, goal, field, *kernels, table["spread"], table["spread_back"],
         table["pixels_back"], table["out_back"], table["flip_back"], table["fold"],
-        flops=6 * 10**8,
+        scratch=[pltpu.VMEM((QUARTER, COLS), F32)],
     )
     messages = [messages[0]] + [shift_y(messages[step], step) for step in (1, 2, 3)]
-    *grads, resist = call(
+    resist = call(resist_kernel, (SHARD, TILE), *messages)
+    grads = call(
         columns_kernel,
-        [(HALF, 2 * SHARD)] * 4 + [(SHARD, TILE)],
+        [(HALF, 2 * SHARD)] * 4,
         *messages, table["band_back"], table["edge_back"], scratch=order,
     )
     grad = grads[0]
@@ -450,7 +463,7 @@
         grad = grad + shift_z(grads[step], step)
     mask_grad = call(
         final_kernel, (SHARD, TILE), shift_tile(grad, 1), grad, shift_tile(grad, -1),
-        table["rows_back"],
+        table["rows"],
     )
     return (resist.T, mask_grad.T)
 

time: 83.9 us -> 74.7 us (0.89)
  waiting for transfers between devices: 34.1 us -> 24 us
  starting transfers between devices: 37.2 us -> 42.2 us
  local copies, waits for them, and re-layouts: 3.77 us -> 0.13 us
    ppermute x9, waiting for transfers between devices: 13.6 us -> 8.94 us  [shift_z(): return lax.ppermute(value, 'kern', route)]
    ppermute x4, waiting for transfers between devices: 11.1 us -> 6.62 us  [shift_tile(): lax.ppermute(value, 'tile', [(i, (i + step) % peers) for i in range(peers)])]
    unnamed x40 -> x36, local copies, waits for them, and re-layouts: 3.75 us -> 0.11 us
    ppermute x9, starting transfers between devices: 12.4 us -> 15.2 us  [shift_y(): return lax.ppermute(value, 'kern', route)]
    ppermute x9, starting transfers between devices: 21.5 us -> 22.7 us  [shift_z(): return lax.ppermute(value, 'kern', route)]
    ppermute x9, waiting for transfers between devices: 9.41 us -> 8.4 us  [shift_y(): return lax.ppermute(value, 'kern', route)]
    ppermute x4, starting transfers between devices: 3.29 us -> 4.21 us  [shift_tile(): lax.ppermute(value, 'tile', [(i, (i + step) % peers) for i in range(peers)])]
    pallas_call x6 -> x8, Pallas kernels: 7.77 us -> 7.46 us  [call(): pl.pallas_call(kernel, scratch_shapes=list(scratch), out_shape=out if man...]
  transfers between devices with their start and end apart: 22 -> 22, of which waited for: 16 -> 14; matrix products, arithmetic and copies ran while one was open for 0% -> 0% of each run, Pallas kernels for 0% -> 3%
where the time goes in v3:
time: 74.7 us; the launch traced here: 74.6 us
  starting transfers between devices  42.2 us (56%)
  waiting for transfers between devices  24 us (32%)
  Pallas kernels  7.46 us (10%)
  between operations  0.9 us (1%)
    ppermute x9, starting transfers between devices, shift_z(): return lax.ppermute(value, 'kern', route)  22.7 us
    ppermute x9, starting transfers between devices, shift_y(): return lax.ppermute(value, 'kern', route)  15.2 us
    ppermute x9, waiting for transfers between devices, shift_z(): return lax.ppermute(value, 'kern', route)  8.94 us
    ppermute x9, waiting for transfers between devices, shift_y(): return lax.ppermute(value, 'kern', route)  8.4 us
    pallas_call x8, Pallas kernels, call(): pl.pallas_call(kernel, scratch_shapes=list(scratch), out_shape=out if man...  7.46 us
    ppermute x4, waiting for transfers between devices, shift_tile(): lax.ppermute(value, 'tile', [(i, (i + step) % peers) for i in range(peers)])  6.62 us
    ppermute x4, starting transfers between devices, shift_tile(): lax.ppermute(value, 'tile', [(i, (i + step) % peers) for i in range(peers)])  4.21 us
  transfers between devices with their start and end apart: 22, of which 14 were waited for; matrix products, arithmetic and copies ran while one was open for 0% of the time, Pallas kernels for 3%

profile of v3, /device:TPU:64, one launch (start us, length us, event | category | flops | bytes accessed | tf_op | source)
XLA Modules:
  0.0 74.6 jit_solution(1938530521189821170)
XLA Ops:
  0.6 0.0 copy-start
  0.7 0.0 copy-start.12
  0.7 3.6 %collective-permute-start.1 = (f32[64,256]{1,0:T(8,128)}, f32[64,256]{1,0:T(8,128)S(1)}, u32[]{:S(2)}, u32[]{:S(2)}) collective-permute-start(f32[64,256]{1,0:T(8,128)} %bitcast.3), channel_id=1, source_target_pairs={{0,240},{16,0},{32,16},{48,32},{64,48},{80,64},{96,80},{112,96},{1... | collective-permute-start | bytes 196616 | tf_op jit(solution)/shard_map/ppermute | solution.py:415
  4.3 0.5 weight_kernel.1.heavy_ref
  4.9 0.0 copy-start.6
  4.9 3.1 %collective-permute-start.6 = (f32[2,2,128,128]{3,2,1,0:T(8,128)S(1)}, f32[2,2,128,128]{3,2,1,0:T(8,128)S(1)}, u32[]{:S(2)}, u32[]{:S(2)}) collective-permute-start(f32[2,2,128,128]{3,2,1,0:T(8,128)S(1)} %copy-done.1), channel_id=1, source_target_pairs={{0,12},{1,13},{2,14},{3,15},{4,0},{5,1},{6,2},{7,3},{8,4},{9,5},{1... | collective-permute-start | bytes 786440 | tf_op jit(solution)/shard_map/ppermute | solution.py:405
  8.0 2.3 %collective-permute-done.above_ref = f32[64,256]{1,0:T(8,128)S(1)} collective-permute-done((f32[64,256]{1,0:T(8,128)}, f32[64,256]{1,0:T(8,128)S(1)}, u32[]{:S(2)}, u32[]{:S(2)}) %collective-permute-start) | collective-permute-done | bytes 65568 | tf_op jit(solution)/shard_map/ppermute | solution.py:415
  10.3 0.3 window_kernel.1.r0
  10.6 0.0 copy-start.9
  10.6 0.0 copy-start.11
  10.7 0.0 copy-start.14
  10.7 3.7 %collective-permute-start.4 = (f32[72,128]{1,0:T(8,128)S(1)}, f32[72,128]{1,0:T(8,128)S(1)}, u32[]{:S(2)}, u32[]{:S(2)}) collective-permute-start(f32[72,128]{1,0:T(8,128)S(1)} %window_kernel.1.r0), channel_id=1, source_target_pairs={{0,1},{1,2},{2,3},{3,0},{4,5},{5,6},{6,7},{7,4},{8,9},{9,10},{10,1... | collective-permute-start | bytes 110600 | tf_op jit(solution)/shard_map/ppermute | solution.py:410
  14.3 1.0 %collective-permute-start.3 = (f32[72,128]{1,0:T(8,128)S(1)}, f32[72,128]{1,0:T(8,128)S(1)}, u32[]{:S(2)}, u32[]{:S(2)}) collective-permute-start(f32[72,128]{1,0:T(8,128)S(1)} %window_kernel.1.r0), channel_id=1, source_target_pairs={{0,2},{1,3},{2,0},{3,1},{4,6},{5,7},{6,4},{7,5},{8,10},{9,11},{10,... | collective-permute-start | bytes 110600 | tf_op jit(solution)/shard_map/ppermute | solution.py:410
  15.3 2.8 %collective-permute-start.2 = (f32[72,128]{1,0:T(8,128)S(1)}, f32[72,128]{1,0:T(8,128)S(1)}, u32[]{:S(2)}, u32[]{:S(2)}) collective-permute-start(f32[72,128]{1,0:T(8,128)S(1)} %window_kernel.1.r0), channel_id=1, source_target_pairs={{0,3},{1,0},{2,1},{3,2},{4,7},{5,4},{6,5},{7,6},{8,11},{9,8},{10,9... | collective-permute-start | bytes 110600 | tf_op jit(solution)/shard_map/ppermute | solution.py:410
  18.2 3.2 %collective-permute-start.10 = (f32[2,2,128,128]{3,2,1,0:T(8,128)S(1)}, f32[2,2,128,128]{3,2,1,0:T(8,128)S(1)}, u32[]{:S(2)}, u32[]{:S(2)}) collective-permute-start(f32[2,2,128,128]{3,2,1,0:T(8,128)S(1)} %copy-done.1), channel_id=1, source_target_pairs={{0,8},{1,9},{2,10},{3,11},{4,12},{5,13},{6,14},{7,15},{8,0},{9,1},... | collective-permute-start | bytes 786440 | tf_op jit(solution)/shard_map/ppermute | solution.py:405
  21.4 0.8 %collective-permute-done.3.r2 = f32[72,128]{1,0:T(8,128)S(1)} collective-permute-done((f32[72,128]{1,0:T(8,128)S(1)}, f32[72,128]{1,0:T(8,128)S(1)}, u32[]{:S(2)}, u32[]{:S(2)}) %collective-permute-start.3) | collective-permute-done | bytes 36896 | tf_op jit(solution)/shard_map/ppermute | solution.py:410
  22.2 0.3 band_kernel.1.p0
  22.5 3.1 %collective-permute-start.9 = (f32[144,128]{1,0:T(8,128)S(1)}, f32[144,128]{1,0:T(8,128)S(1)}, u32[]{:S(2)}, u32[]{:S(2)}) collective-permute-start(f32[144,128]{1,0:T(8,128)S(1)} %band_kernel.1.p0), channel_id=1, source_target_pairs={{0,12},{1,13},{2,14},{3,15},{4,0},{5,1},{6,2},{7,3},{8,4},{9,5},{1... | collective-permute-start | bytes 221192 | tf_op jit(solution)/shard_map/ppermute | solution.py:405
  25.6 0.6 collective-permute-start.8
  26.2 1.0 %collective-permute-start.7 = (f32[144,128]{1,0:T(8,128)S(1)}, f32[144,128]{1,0:T(8,128)S(1)}, u32[]{:S(2)}, u32[]{:S(2)}) collective-permute-start(f32[144,128]{1,0:T(8,128)S(1)} %band_kernel.1.p0), channel_id=1, source_target_pairs={{0,4},{1,5},{2,6},{3,7},{4,8},{5,9},{6,10},{7,11},{8,12},{9,13},{1... | collective-permute-start | bytes 221192 | tf_op jit(solution)/shard_map/ppermute | solution.py:405
  27.2 0.3 collective-permute-done.10.h2
  27.5 0.1 collective-permute-done.9.p3
  27.6 3.9 %collective-permute-done.8.p2 = f32[144,128]{1,0:T(8,128)S(1)} collective-permute-done((f32[144,128]{1,0:T(8,128)S(1)}, f32[144,128]{1,0:T(8,128)S(1)}, u32[]{:S(2)}, u32[]{:S(2)}) %collective-permute-start.8) | collective-permute-done | bytes 73760 | tf_op jit(solution)/shard_map/ppermute | solution.py:405
  31.5 0.7 collective-permute-done.7.p1
  32.3 0.0 copy-start.10
  32.3 1.5 %aerial_kernel.1 = (f32[512,512]{1,0:T(8,128)S(1)}, f32[64,256]{1,0:T(8,128)S(1)}) custom-call(f32[144,128]{1,0:T(8,128)S(1)} %band_kernel.1.p0, f32[144,128]{1,0:T(8,128)S(1)} %collective-permute-done.7.p1, f32[144,128]{1,0:T(8,128)S(1)} %collective-permute-done.8.p2, f32[144,128]{1,0:T(8,128)S(1)} %collective-permute-done.9.p3, ...), custom_call_target="tpu_custom_call" | custom-call | flops 4000000000 | bytes 1000000 | tf_op jit(solution)/shard_map/aerial_kernel/pallas_call | solution.py:389
  33.8 0.9 %collective-permute-start.13 = (f32[64,256]{1,0:T(8,128)S(1)}, f32[64,256]{1,0:T(8,128)S(1)}, u32[]{:S(2)}, u32[]{:S(2)}) collective-permute-start(f32[64,256]{1,0:T(8,128)S(1)} %get-tuple-element.28.i0), channel_id=1, source_target_pairs={{0,3},{1,0},{2,1},{3,2},{4,7},{5,4},{6,5},{7,6},{8,11},{9,8},{10,9... | collective-permute-start | bytes 196616 | tf_op jit(solution)/shard_map/ppermute | solution.py:410
  34.7 3.4 %collective-permute-start.12 = (f32[64,256]{1,0:T(8,128)S(1)}, f32[64,256]{1,0:T(8,128)S(1)}, u32[]{:S(2)}, u32[]{:S(2)}) collective-permute-start(f32[64,256]{1,0:T(8,128)S(1)} %get-tuple-element.28.i0), channel_id=1, source_target_pairs={{0,2},{1,3},{2,0},{3,1},{4,6},{5,7},{6,4},{7,5},{8,10},{9,11},{10,... | collective-permute-start | bytes 196616 | tf_op jit(solution)/shard_map/ppermute | solution.py:410
  38.1 4.0 %collective-permute-start.11 = (f32[64,256]{1,0:T(8,128)S(1)}, f32[64,256]{1,0:T(8,128)S(1)}, u32[]{:S(2)}, u32[]{:S(2)}) collective-permute-start(f32[64,256]{1,0:T(8,128)S(1)} %get-tuple-element.28.i0), channel_id=1, source_target_pairs={{0,1},{1,2},{2,3},{3,0},{4,5},{5,6},{6,7},{7,4},{8,9},{9,10},{10,1... | collective-permute-start | bytes 196616 | tf_op jit(solution)/shard_map/ppermute | solution.py:410
  42.2 0.7 collective-permute-done.12.i2
  42.9 1.3 %collective-permute-done.11.i1 = f32[64,256]{1,0:T(8,128)S(1)} collective-permute-done((f32[64,256]{1,0:T(8,128)S(1)}, f32[64,256]{1,0:T(8,128)S(1)}, u32[]{:S(2)}, u32[]{:S(2)}) %collective-permute-start.11) | collective-permute-done | bytes 65568 | tf_op jit(solution)/shard_map/ppermute | solution.py:410
  44.3 2.8 %slope_kernel.1 = (f32[176,128]{1,0:T(8,128)S(1)}, f32[176,128]{1,0:T(8,128)S(1)}, f32[176,128]{1,0:T(8,128)S(1)}, f32[176,128]{1,0:T(8,128)S(1)}) custom-call(f32[64,256]{1,0:T(8,128)S(1)} %get-tuple-element.28.i0, f32[64,256]{1,0:T(8,128)S(1)} %collective-permute-done.11.i1, f32[64,256]{1,0:T(8,128)S(1)} %collective-permute-done.12.i2, ...), custom_call_target="tpu_custom_call" | custom-call | flops 4000000000 | bytes 1000000 | tf_op jit(solution)/shard_map/slope_kernel/pallas_call | solution.py:389
  47.1 0.1 collective-permute-start.14
  47.2 2.5 %collective-permute-start.15 = (f32[176,128]{1,0:T(8,128)S(1)}, f32[176,128]{1,0:T(8,128)S(1)}, u32[]{:S(2)}, u32[]{:S(2)}) collective-permute-start(f32[176,128]{1,0:T(8,128)S(1)} %get-tuple-element.32), channel_id=1, source_target_pairs={{0,8},{1,9},{2,10},{3,11},{4,12},{5,13},{6,14},{7,15},{8,0},{9,1},... | collective-permute-start | bytes 270344 | tf_op jit(solution)/shard_map/ppermute | solution.py:405
  49.7 1.7 %collective-permute-start.16 = (f32[176,128]{1,0:T(8,128)S(1)}, f32[176,128]{1,0:T(8,128)S(1)}, u32[]{:S(2)}, u32[]{:S(2)}) collective-permute-start(f32[176,128]{1,0:T(8,128)S(1)} %get-tuple-element.33), channel_id=1, source_target_pairs={{0,12},{1,13},{2,14},{3,15},{4,0},{5,1},{6,2},{7,3},{8,4},{9,5},{1... | collective-permute-start | bytes 270344 | tf_op jit(solution)/shard_map/ppermute | solution.py:405
  51.4 2.5 %collective-permute-done.14.m1 = f32[176,128]{1,0:T(8,128)S(1)} collective-permute-done((f32[176,128]{1,0:T(8,128)S(1)}, f32[176,128]{1,0:T(8,128)S(1)}, u32[]{:S(2)}, u32[]{:S(2)}) %collective-permute-start.14) | collective-permute-done | bytes 90144 | tf_op jit(solution)/shard_map/ppermute | solution.py:405
  53.9 0.9 %collective-permute-done.16.m3 = f32[176,128]{1,0:T(8,128)S(1)} collective-permute-done((f32[176,128]{1,0:T(8,128)S(1)}, f32[176,128]{1,0:T(8,128)S(1)}, u32[]{:S(2)}, u32[]{:S(2)}) %collective-permute-start.16) | collective-permute-done | bytes 90144 | tf_op jit(solution)/shard_map/ppermute | solution.py:405
  54.7 0.3 columns_kernel.1
  55.1 4.4 %collective-permute-start.17 = (f32[72,128]{1,0:T(8,128)S(1)}, f32[72,128]{1,0:T(8,128)S(1)}, u32[]{:S(2)}, u32[]{:S(2)}) collective-permute-start(f32[72,128]{1,0:T(8,128)S(1)} %get-tuple-element.35), channel_id=1, source_target_pairs={{0,1},{1,2},{2,3},{3,0},{4,5},{5,6},{6,7},{7,4},{8,9},{9,10},{10,1... | collective-permute-start | bytes 110600 | tf_op jit(solution)/shard_map/ppermute | solution.py:410
  59.5 2.5 %collective-permute-start.18 = (f32[72,128]{1,0:T(8,128)S(1)}, f32[72,128]{1,0:T(8,128)S(1)}, u32[]{:S(2)}, u32[]{:S(2)}) collective-permute-start(f32[72,128]{1,0:T(8,128)S(1)} %get-tuple-element.36), channel_id=1, source_target_pairs={{0,2},{1,3},{2,0},{3,1},{4,6},{5,7},{6,4},{7,5},{8,10},{9,11},{10,... | collective-permute-start | bytes 110600 | tf_op jit(solution)/shard_map/ppermute | solution.py:410
  62.0 5.3 %collective-permute-done.18 = f32[72,128]{1,0:T(8,128)S(1)} collective-permute-done((f32[72,128]{1,0:T(8,128)S(1)}, f32[72,128]{1,0:T(8,128)S(1)}, u32[]{:S(2)}, u32[]{:S(2)}) %collective-permute-start.18) | collective-permute-done | bytes 36896 | tf_op jit(solution)/shard_map/ppermute | solution.py:410
  67.3 0.7 collective-permute-done.19
  68.0 0.1 collective-permute-start.21
  68.1 0.5 collective-permute-start.20
  68.6 0.8 %resist_kernel.1 = f32[64,256]{1,0:T(8,128)} custom-call(f32[176,128]{1,0:T(8,128)S(1)} %get-tuple-element.30.m0, f32[176,128]{1,0:T(8,128)S(1)} %collective-permute-done.14.m1, f32[176,128]{1,0:T(8,128)S(1)} %collective-permute-done.15.m2, f32[176,128]{1,0:T(8,128)S(1)} %collective-permute-done.16.m3), custom_call_target="tpu_custom_call" | custom-call | flops 4000000000 | bytes 1000000 | tf_op jit(solution)/shard_map/resist_kernel/pallas_call | solution.py:389
  69.4 0.4 collective-permute-done.21.below_ref
  69.8 3.9 %collective-permute-done.20.above_ref = f32[72,128]{1,0:T(8,128)S(1)} collective-permute-done((f32[72,128]{1,0:T(8,128)S(1)}, f32[72,128]{1,0:T(8,128)S(1)}, u32[]{:S(2)}, u32[]{:S(2)}) %collective-permute-start.20) | collective-permute-done | bytes 36896 | tf_op jit(solution)/shard_map/ppermute | solution.py:415
  73.7 0.9 %final_kernel.1 = f32[64,256]{1,0:T(8,128)} custom-call(f32[72,128]{1,0:T(8,128)S(1)} %collective-permute-done.20.above_ref, f32[72,128]{1,0:T(8,128)S(1)} %add_add_fusion.own_ref, f32[72,128]{1,0:T(8,128)S(1)} %collective-permute-done.21.below_ref, bf16[2,144,256]{2,1,0:T(8,128)(2,1)S(1)} %copy-done.12), custom_call_target="tpu_custom_call" | custom-call | flops 4000000000 | bytes 1000000 | tf_op jit(solution)/shard_map/final_kernel/pallas_call | solution.py:389
  (42 shorter events, 0.1 us)
Async XLA Ops:
  0.6 41.5 %copy-start = (s32[256,1024]{1,0:T(8,128)S(1)}, s32[256,1024]{1,0:T(8,128)}, u32[]{:S(2)}) copy-start(s32[256,1024]{1,0:T(8,128)} %param.19) | copy-start | bytes 3145732
  0.6 3.7 %copy-start.3 = (f32[2]{0:T(128)S(1)}, f32[2]{0:T(128)}, u32[]{:S(2)}) copy-start(f32[2]{0:T(128)} %weight_ref.1) | copy-start | bytes 28
  0.7 4.2 %copy-start.1 = (f32[2,2,128,128]{3,2,1,0:T(8,128)S(1)}, f32[2,2,128,128]{3,2,1,0:T(8,128)}, u32[]{:S(2)}) copy-start(f32[2,2,128,128]{3,2,1,0:T(8,128)} %h0.1) | copy-start | bytes 786436
  0.7 9.7 %copy-start.2 = (f32[256,64]{0,1:T(8,128)S(1)}, f32[256,64]{0,1:T(8,128)}, u32[]{:S(2)}) copy-start(f32[256,64]{0,1:T(8,128)} %param.18) | copy-start | bytes 196612
  0.7 9.7 %copy-start.12 = (bf16[2,144,256]{2,1,0:T(8,128)(2,1)S(1)}, bf16[2,144,256]{2,1,0:T(8,128)(2,1)}, u32[]{:S(2)}) copy-start(bf16[2,144,256]{2,1,0:T(8,128)(2,1)} %constant.53.clone.rows_ref) | copy-start | bytes 442372
  0.7 7.3 %collective-permute-start.1 = (f32[64,256]{1,0:T(8,128)}, f32[64,256]{1,0:T(8,128)S(1)}, u32[]{:S(2)}, u32[]{:S(2)}) collective-permute-start(f32[64,256]{1,0:T(8,128)} %bitcast.3), channel_id=1, source_target_pairs={{0,240},{16,0},{32,16},{48,32},{64,48},{80,64},{96,80},{112,96},{1... | collective-permute-start | bytes 196616 | tf_op jit(solution)/shard_map/ppermute | solution.py:415
  4.3 6.0 %collective-permute-start = (f32[64,256]{1,0:T(8,128)}, f32[64,256]{1,0:T(8,128)S(1)}, u32[]{:S(2)}, u32[]{:S(2)}) collective-permute-start(f32[64,256]{1,0:T(8,128)} %bitcast.4), channel_id=1, source_target_pairs={{0,16},{16,32},{32,48},{48,64},{64,80},{80,96},{96,112},{112,128},... | collective-permute-start | bytes 196616 | tf_op jit(solution)/shard_map/ppermute | solution.py:415
  4.9 17.3 %copy-start.6 = (bf16[2,16,64,256]{3,2,1,0:T(8,128)(2,1)S(1)}, bf16[2,16,64,256]{3,2,1,0:T(8,128)(2,1)}, u32[]{:S(2)}) copy-start(bf16[2,16,64,256]{3,2,1,0:T(8,128)(2,1)} %constant.54.clone.band_ref) | copy-start | bytes 3145732
  4.9 17.3 %collective-permute-start.6 = (f32[2,2,128,128]{3,2,1,0:T(8,128)S(1)}, f32[2,2,128,128]{3,2,1,0:T(8,128)S(1)}, u32[]{:S(2)}, u32[]{:S(2)}) collective-permute-start(f32[2,2,128,128]{3,2,1,0:T(8,128)S(1)} %copy-done.1), channel_id=1, source_target_pairs={{0,12},{1,13},{2,14},{3,15},{4,0},{5,1},{6,2},{7,3},{8,4},{9,5},{1... | collective-permute-start | bytes 786440 | tf_op jit(solution)/shard_map/ppermute | solution.py:405
  8.0 14.2 %collective-permute-start.5 = (f32[2,2,128,128]{3,2,1,0:T(8,128)S(1)}, f32[2,2,128,128]{3,2,1,0:T(8,128)S(1)}, u32[]{:S(2)}, u32[]{:S(2)}) collective-permute-start(f32[2,2,128,128]{3,2,1,0:T(8,128)S(1)} %copy-done.1), channel_id=1, source_target_pairs={{0,4},{1,5},{2,6},{3,7},{4,8},{5,9},{6,10},{7,11},{8,12},{9,13},{1... | collective-permute-start | bytes 786440 | tf_op jit(solution)/shard_map/ppermute | solution.py:405
  10.6 21.6 %copy-start.9 = (bf16[2,256,512]{2,1,0:T(8,128)(2,1)S(1)}, bf16[2,256,512]{2,1,0:T(8,128)(2,1)}, u32[]{:S(2)}) copy-start(bf16[2,256,512]{2,1,0:T(8,128)(2,1)} %constant.63.clone.pixels_ref) | copy-start | bytes 1572868
  10.6 21.6 %copy-start.11 = (bf16[2,4,128,128]{3,2,1,0:T(8,128)(2,1)S(1)}, bf16[2,4,128,128]{3,2,1,0:T(8,128)(2,1)}, u32[]{:S(2)}) copy-start(bf16[2,4,128,128]{3,2,1,0:T(8,128)(2,1)} %constant.61.clone.out_rows_ref) | copy-start | bytes 786436
  10.7 21.6 %copy-start.14 = (bf16[128,256]{1,0:T(8,128)(2,1)S(1)}, bf16[128,256]{1,0:T(8,128)(2,1)}, u32[]{:S(2)}) copy-start(bf16[128,256]{1,0:T(8,128)(2,1)} %constant.57.clone.unfold_ref) | copy-start | bytes 196612
  10.7 7.5 %collective-permute-start.4 = (f32[72,128]{1,0:T(8,128)S(1)}, f32[72,128]{1,0:T(8,128)S(1)}, u32[]{:S(2)}, u32[]{:S(2)}) collective-permute-start(f32[72,128]{1,0:T(8,128)S(1)} %window_kernel.1.r0), channel_id=1, source_target_pairs={{0,1},{1,2},{2,3},{3,0},{4,5},{5,6},{6,7},{7,4},{8,9},{9,10},{10,1... | collective-permute-start | bytes 110600 | tf_op jit(solution)/shard_map/ppermute | solution.py:410
  14.3 7.9 %collective-permute-start.3 = (f32[72,128]{1,0:T(8,128)S(1)}, f32[72,128]{1,0:T(8,128)S(1)}, u32[]{:S(2)}, u32[]{:S(2)}) collective-permute-start(f32[72,128]{1,0:T(8,128)S(1)} %window_kernel.1.r0), channel_id=1, source_target_pairs={{0,2},{1,3},{2,0},{3,1},{4,6},{5,7},{6,4},{7,5},{8,10},{9,11},{10,... | collective-permute-start | bytes 110600 | tf_op jit(solution)/shard_map/ppermute | solution.py:410
  15.3 6.9 %collective-permute-start.2 = (f32[72,128]{1,0:T(8,128)S(1)}, f32[72,128]{1,0:T(8,128)S(1)}, u32[]{:S(2)}, u32[]{:S(2)}) collective-permute-start(f32[72,128]{1,0:T(8,128)S(1)} %window_kernel.1.r0), channel_id=1, source_target_pairs={{0,3},{1,0},{2,1},{3,2},{4,7},{5,4},{6,5},{7,6},{8,11},{9,8},{10,9... | collective-permute-start | bytes 110600 | tf_op jit(solution)/shard_map/ppermute | solution.py:410
  18.2 9.3 %collective-permute-start.10 = (f32[2,2,128,128]{3,2,1,0:T(8,128)S(1)}, f32[2,2,128,128]{3,2,1,0:T(8,128)S(1)}, u32[]{:S(2)}, u32[]{:S(2)}) collective-permute-start(f32[2,2,128,128]{3,2,1,0:T(8,128)S(1)} %copy-done.1), channel_id=1, source_target_pairs={{0,8},{1,9},{2,10},{3,11},{4,12},{5,13},{6,14},{7,15},{8,0},{9,1},... | collective-permute-start | bytes 786440 | tf_op jit(solution)/shard_map/ppermute | solution.py:405
  22.5 5.0 %collective-permute-start.9 = (f32[144,128]{1,0:T(8,128)S(1)}, f32[144,128]{1,0:T(8,128)S(1)}, u32[]{:S(2)}, u32[]{:S(2)}) collective-permute-start(f32[144,128]{1,0:T(8,128)S(1)} %band_kernel.1.p0), channel_id=1, source_target_pairs={{0,12},{1,13},{2,14},{3,15},{4,0},{5,1},{6,2},{7,3},{8,4},{9,5},{1... | collective-permute-start | bytes 221192 | tf_op jit(solution)/shard_map/ppermute | solution.py:405
  25.6 5.9 %collective-permute-start.8 = (f32[144,128]{1,0:T(8,128)S(1)}, f32[144,128]{1,0:T(8,128)S(1)}, u32[]{:S(2)}, u32[]{:S(2)}) collective-permute-start(f32[144,128]{1,0:T(8,128)S(1)} %band_kernel.1.p0), channel_id=1, source_target_pairs={{0,8},{1,9},{2,10},{3,11},{4,12},{5,13},{6,14},{7,15},{8,0},{9,1},... | collective-permute-start | bytes 221192 | tf_op jit(solution)/shard_map/ppermute | solution.py:405
  26.2 6.0 %collective-permute-start.7 = (f32[144,128]{1,0:T(8,128)S(1)}, f32[144,128]{1,0:T(8,128)S(1)}, u32[]{:S(2)}, u32[]{:S(2)}) collective-permute-start(f32[144,128]{1,0:T(8,128)S(1)} %band_kernel.1.p0), channel_id=1, source_target_pairs={{0,4},{1,5},{2,6},{3,7},{4,8},{5,9},{6,10},{7,11},{8,12},{9,13},{1... | collective-permute-start | bytes 221192 | tf_op jit(solution)/shard_map/ppermute | solution.py:405
  27.2 5.1 %copy-start.17 = (bf16[64,72]{1,0:T(8,128)(2,1)S(1)}, bf16[64,72]{1,0:T(8,128)(2,1)}, u32[]{:S(2)}) copy-start(bf16[64,72]{1,0:T(8,128)(2,1)} %constant.59.clone.flip_ref) | copy-start | bytes 27652
  27.2 17.0 %copy-start.4 = (bf16[2,1024,256]{2,1,0:T(8,128)(2,1)S(1)}, bf16[2,1024,256]{2,1,0:T(8,128)(2,1)}, u32[]{:S(2)}) copy-start(bf16[2,1024,256]{2,1,0:T(8,128)(2,1)} %constant.66.clone.spread_back_ref) | copy-start | bytes 3145732
  27.2 17.0 %copy-start.5 = (bf16[2,256,1024]{2,1,0:T(8,128)(2,1)S(1)}, bf16[2,256,1024]{2,1,0:T(8,128)(2,1)}, u32[]{:S(2)}) copy-start(bf16[2,256,1024]{2,1,0:T(8,128)(2,1)} %constant.65.clone.spread_ref) | copy-start | bytes 3145732
  32.3 12.0 %copy-start.10 = (bf16[2,4,128,128]{3,2,1,0:T(8,128)(2,1)S(1)}, bf16[2,4,128,128]{3,2,1,0:T(8,128)(2,1)}, u32[]{:S(2)}) copy-start(bf16[2,4,128,128]{3,2,1,0:T(8,128)(2,1)} %constant.62.clone.out_back_ref) | copy-start | bytes 786436
  32.3 12.0 %copy-start.13 = (bf16[256,128]{1,0:T(8,128)(2,1)S(1)}, bf16[256,128]{1,0:T(8,128)(2,1)}, u32[]{:S(2)}) copy-start(bf16[256,128]{1,0:T(8,128)(2,1)} %constant.58.clone.fold_ref) | copy-start | bytes 196612
  32.3 11.9 %copy-start.16 = (bf16[72,64]{1,0:T(8,128)(2,1)S(1)}, bf16[72,64]{1,0:T(8,128)(2,1)}, u32[]{:S(2)}) copy-start(bf16[72,64]{1,0:T(8,128)(2,1)} %constant.60.clone.flip_back_ref) | copy-start | bytes 27652
  33.8 10.4 %copy-start.8 = (bf16[2,512,256]{2,1,0:T(8,128)(2,1)S(1)}, bf16[2,512,256]{2,1,0:T(8,128)(2,1)}, u32[]{:S(2)}) copy-start(bf16[2,512,256]{2,1,0:T(8,128)(2,1)} %constant.64.clone.pixels_back_ref) | copy-start | bytes 1572868
  33.8 8.4 %collective-permute-start.13 = (f32[64,256]{1,0:T(8,128)S(1)}, f32[64,256]{1,0:T(8,128)S(1)}, u32[]{:S(2)}, u32[]{:S(2)}) collective-permute-start(f32[64,256]{1,0:T(8,128)S(1)} %get-tuple-element.28.i0), channel_id=1, source_target_pairs={{0,3},{1,0},{2,1},{3,2},{4,7},{5,4},{6,5},{7,6},{8,11},{9,8},{10,9... | collective-permute-start | bytes 196616 | tf_op jit(solution)/shard_map/ppermute | solution.py:410
  34.7 8.2 %collective-permute-start.12 = (f32[64,256]{1,0:T(8,128)S(1)}, f32[64,256]{1,0:T(8,128)S(1)}, u32[]{:S(2)}, u32[]{:S(2)}) collective-permute-start(f32[64,256]{1,0:T(8,128)S(1)} %get-tuple-element.28.i0), channel_id=1, source_target_pairs={{0,2},{1,3},{2,0},{3,1},{4,6},{5,7},{6,4},{7,5},{8,10},{9,11},{10,... | collective-permute-start | bytes 196616 | tf_op jit(solution)/shard_map/ppermute | solution.py:410
  38.1 6.1 %collective-permute-start.11 = (f32[64,256]{1,0:T(8,128)S(1)}, f32[64,256]{1,0:T(8,128)S(1)}, u32[]{:S(2)}, u32[]{:S(2)}) collective-permute-start(f32[64,256]{1,0:T(8,128)S(1)} %get-tuple-element.28.i0), channel_id=1, source_target_pairs={{0,1},{1,2},{2,3},{3,0},{4,5},{5,6},{6,7},{7,4},{8,9},{9,10},{10,1... | collective-permute-start | bytes 196616 | tf_op jit(solution)/shard_map/ppermute | solution.py:410
  44.3 10.5 %copy-start.7 = (bf16[2,128,1024]{2,1,0:T(8,128)(2,1)S(1)}, bf16[2,128,1024]{2,1,0:T(8,128)(2,1)}, u32[]{:S(2)}) copy-start(bf16[2,128,1024]{2,1,0:T(8,128)(2,1)} %constant.55.clone.band_back_ref) | copy-start | bytes 1572868
  44.3 10.4 %copy-start.15 = (f32[8,1024]{1,0:T(8,128)S(1)}, f32[8,1024]{1,0:T(8,128)}, u32[]{:S(2)}) copy-start(f32[8,1024]{1,0:T(8,128)} %constant.56.clone.edge_ref) | copy-start | bytes 98308
  47.1 6.8 %collective-permute-start.14 = (f32[176,128]{1,0:T(8,128)S(1)}, f32[176,128]{1,0:T(8,128)S(1)}, u32[]{:S(2)}, u32[]{:S(2)}) collective-permute-start(f32[176,128]{1,0:T(8,128)S(1)} %get-tuple-element.31), channel_id=1, source_target_pairs={{0,4},{1,5},{2,6},{3,7},{4,8},{5,9},{6,10},{7,11},{8,12},{9,13},{1... | collective-permute-start | bytes 270344 | tf_op jit(solution)/shard_map/ppermute | solution.py:405
  47.2 6.7 %collective-permute-start.15 = (f32[176,128]{1,0:T(8,128)S(1)}, f32[176,128]{1,0:T(8,128)S(1)}, u32[]{:S(2)}, u32[]{:S(2)}) collective-permute-start(f32[176,128]{1,0:T(8,128)S(1)} %get-tuple-element.32), channel_id=1, source_target_pairs={{0,8},{1,9},{2,10},{3,11},{4,12},{5,13},{6,14},{7,15},{8,0},{9,1},... | collective-permute-start | bytes 270344 | tf_op jit(solution)/shard_map/ppermute | solution.py:405
  49.7 5.0 %collective-permute-start.16 = (f32[176,128]{1,0:T(8,128)S(1)}, f32[176,128]{1,0:T(8,128)S(1)}, u32[]{:S(2)}, u32[]{:S(2)}) collective-permute-start(f32[176,128]{1,0:T(8,128)S(1)} %get-tuple-element.33), channel_id=1, source_target_pairs={{0,12},{1,13},{2,14},{3,15},{4,0},{5,1},{6,2},{7,3},{8,4},{9,5},{1... | collective-permute-start | bytes 270344 | tf_op jit(solution)/shard_map/ppermute | solution.py:405
  55.1 6.9 %collective-permute-start.17 = (f32[72,128]{1,0:T(8,128)S(1)}, f32[72,128]{1,0:T(8,128)S(1)}, u32[]{:S(2)}, u32[]{:S(2)}) collective-permute-start(f32[72,128]{1,0:T(8,128)S(1)} %get-tuple-element.35), channel_id=1, source_target_pairs={{0,1},{1,2},{2,3},{3,0},{4,5},{5,6},{6,7},{7,4},{8,9},{9,10},{10,1... | collective-permute-start | bytes 110600 | tf_op jit(solution)/shard_map/ppermute | solution.py:410
  59.5 7.9 %collective-permute-start.18 = (f32[72,128]{1,0:T(8,128)S(1)}, f32[72,128]{1,0:T(8,128)S(1)}, u32[]{:S(2)}, u32[]{:S(2)}) collective-permute-start(f32[72,128]{1,0:T(8,128)S(1)} %get-tuple-element.36), channel_id=1, source_target_pairs={{0,2},{1,3},{2,0},{3,1},{4,6},{5,7},{6,4},{7,5},{8,10},{9,11},{10,... | collective-permute-start | bytes 110600 | tf_op jit(solution)/shard_map/ppermute | solution.py:410
  62.0 6.1 %collective-permute-start.19 = (f32[72,128]{1,0:T(8,128)S(1)}, f32[72,128]{1,0:T(8,128)S(1)}, u32[]{:S(2)}, u32[]{:S(2)}) collective-permute-start(f32[72,128]{1,0:T(8,128)S(1)} %get-tuple-element.37), channel_id=1, source_target_pairs={{0,3},{1,0},{2,1},{3,2},{4,7},{5,4},{6,5},{7,6},{8,11},{9,8},{10,9... | collective-permute-start | bytes 110600 | tf_op jit(solution)/shard_map/ppermute | solution.py:410
  68.0 1.8 %collective-permute-start.21 = (f32[72,128]{1,0:T(8,128)S(1)}, f32[72,128]{1,0:T(8,128)S(1)}, u32[]{:S(2)}, u32[]{:S(2)}) collective-permute-start(f32[72,128]{1,0:T(8,128)S(1)} %add_add_fusion.own_ref), channel_id=1, source_target_pairs={{0,240},{16,0},{32,16},{48,32},{64,48},{80,64},{96,80},{112,96},{1... | collective-permute-start | bytes 110600 | tf_op jit(solution)/shard_map/ppermute | solution.py:415
  68.1 5.6 %collective-permute-start.20 = (f32[72,128]{1,0:T(8,128)S(1)}, f32[72,128]{1,0:T(8,128)S(1)}, u32[]{:S(2)}, u32[]{:S(2)}) collective-permute-start(f32[72,128]{1,0:T(8,128)S(1)} %add_add_fusion.own_ref), channel_id=1, source_target_pairs={{0,16},{16,32},{32,48},{48,64},{64,80},{80,96},{96,112},{112,128},... | collective-permute-start | bytes 110600 | tf_op jit(solution)/shard_map/ppermute | solution.py:415

commit v4 on v3

--- a/solution.py
+++ b/solution.py
@@ -118,28 +118,23 @@
     )
 
 
+def dot3_deep(former, latter):
+    twice = jnp.concatenate([former[0], former[0]], 1)
+    return dot(twice, jnp.concatenate(latter, 0)) + dot(former[1], latter[0])
+
+
 def pair(ref):
     return ref[0], ref[1]
 
 
 def moved(flip, value):
-    high, rest = value.astype(BF16), value
-    total = dot(flip, high)
-    for _ in range(2):
-        rest = rest - high.astype(F32)
-        high = rest.astype(BF16)
-        total = total + dot(flip, high)
-    return total
+    high, low = split(value)
+    return dot(flip, high) + dot(flip, low)
 
 
 def moved_right(value, flip):
-    high, rest = value.astype(BF16), value
-    total = dot(high, flip)
-    for _ in range(2):
-        rest = rest - high.astype(F32)
-        high = rest.astype(BF16)
-        total = total + dot(high, flip)
-    return total
+    high, low = split(value)
+    return dot(high, flip) + dot(low, flip)
 
 
 def pair_up(value):
@@ -155,11 +150,17 @@
     out_ref[...] = jnp.where(row == WEIGHT_ROW - HALF + 8, weight_ref[0], weight_ref[1])
 
 
-def window_kernel(above_ref, below_ref, mask_ref, rows_ref, heavy_ref, out_ref):
+def neighbours(outer, inner):
     tile = lax.axis_index("tile")
     last = lax.axis_size("tile") - 1
-    above = jnp.where(tile > 0, above_ref[:, TILE - HALO :], 0.0)
-    below = jnp.where(tile < last, below_ref[:, :HALO], 0.0)
+    outer = jnp.where((tile > 0) & (tile < last), outer, 0.0)
+    odd = tile % 2 == 1
+    return jnp.where(odd, inner, outer), jnp.where(odd, outer, inner)
+
+
+def window_kernel(outer_ref, inner_ref, mask_ref, rows_ref, heavy_ref, out_ref):
+    above, below = neighbours(outer_ref[...], inner_ref[...])
+    above, below = above[:, TILE - HALO :], below[:, :HALO]
     sides = jnp.concatenate([below, above], 1)
     both = split(jnp.concatenate([mask_ref[...], sides], 0))
     done = dot3(pair(rows_ref), both, dot_last)
@@ -196,7 +197,7 @@
     blocks = [ref[...] for ref in (r0, r1, r2, r3)]
     cos = jnp.concatenate([block[:, :SHARD] for block in blocks], 1)
     sin = jnp.concatenate([block[:, SHARD:] for block in blocks], 1)
-    places = [4 * at_y + (at_z + step) % 4 for step in range(4)]
+    places = [4 * at_y + (at_z ^ step) for step in range(4)]
     band = tuple(
         jnp.concatenate([band_ref[i, pl.ds(place, 1)][0] for place in places], 0)
         for i in range(2)
@@ -239,7 +240,7 @@
                 ],
                 1,
             )
-            quads = dot3(out_rows, split(band))
+            quads = dot3_deep(out_rows, split(band))
             upper, lower = quads[:QUARTER], quads[QUARTER:]
             mids.append(
                 jnp.concatenate(
@@ -277,10 +278,17 @@
     slope = slope.astype(BF16)
     slope = dot(slope, spread_back_ref[0]) + dot(slope, spread_back_ref[1])
     slope = jnp.concatenate([slope, slope], 1)
-    weighted = jnp.concatenate(
-        [slope * field_ref[slot * QUARTER : (slot + 1) * QUARTER, :] for slot in range(COUNT)], 0
-    )
-    freqs = dot3(split(weighted), pair(pixels_back_ref))
+    freqs = []
+    for first in range(0, COUNT, 2):
+        weighted = jnp.concatenate(
+            [
+                slope * field_ref[slot * QUARTER : (slot + 1) * QUARTER, :]
+                for slot in range(first, first + 2)
+            ],
+            0,
+        )
+        freqs.append(dot3(split(weighted), pair(pixels_back_ref)))
+    freqs = jnp.concatenate(freqs, 0)
     out_back = (
         out_back_ref[0, pl.ds(at_y, 1)][0],
         out_back_ref[1, pl.ds(at_y, 1)][0],
@@ -293,7 +301,7 @@
         block = jnp.concatenate(
             [part, jnp.concatenate([part[:, FREQS:], -part[:, :FREQS]], 1)], 0
         )
-        adjoint = dot3(out_back, split(block))
+        adjoint = dot3_deep(out_back, split(block))
         adj_re, adj_im = adjoint[:, :FREQS], adjoint[:, FREQS:]
         term_re = kern_re * adj_re + kern_im * adj_im
         term_im = kern_re * adj_im - kern_im * adj_re
@@ -318,7 +326,7 @@
     resist_ref[...] = resist
     for step, message in enumerate((m0, m1, m2, m3)):
         message[: 2 * HALF, :] = done
-        block = 4 * ((at_y + step) % 4) + at_z
+        block = 4 * (at_y ^ step) + at_z
         start = pl.multiple_of((block // 2) * 2 * SHARD, 2 * SHARD)
         wide = resist_ref[:, pl.ds(start, 2 * SHARD)].T
         piece = jnp.where(block % 2 == 0, wide[:SHARD], wide[SHARD:])
@@ -340,7 +348,7 @@
         cols = slice(slot * SHARD, (slot + 1) * SHARD)
         order_ref[slot] = jnp.concatenate([done[:HALF, cols], done[HALF:, cols]], 1)
     for step, out in enumerate((g0, g1, g2, g3)):
-        out[...] = order_ref[pl.ds((at_z + step) % 4, 1)][0]
+        out[...] = order_ref[pl.ds(at_z ^ step, 1)][0]
 
 
 def resist_kernel(m0, m1, m2, m3, resist_ref):
@@ -353,20 +361,19 @@
     for slot in range(4):
         spot = pieces[0]
         for step in (1, 2, 3):
-            spot = jnp.where((at_y - step + 4) % 4 == slot, pieces[step], spot)
+            spot = jnp.where((at_y ^ step) == slot, pieces[step], spot)
         spots.append(spot)
     resist_ref[...] = jnp.concatenate(spots, 1)
 
 
-def final_kernel(above_ref, own_ref, below_ref, rows_ref, out_ref):
-    tile = lax.axis_index("tile")
-    last = lax.axis_size("tile") - 1
+def final_kernel(inner_ref, outer_ref, own_ref, rows_ref, out_ref):
+    above, below = neighbours(outer_ref[...], inner_ref[...])
     own = own_ref[...]
     sign = 2.0 * alternate(own.shape)
     own = 2.0 * own
     sides = (
-        own + jnp.where(tile > 0, above_ref[...], 0.0) * sign,
-        own + jnp.where(tile < last, below_ref[...], 0.0) * sign,
+        own + above * sign,
+        own + below * sign,
     )
     for slot, side in enumerate(sides):
         side = split(side.T)
@@ -400,19 +407,20 @@
     )(*operands)
 
 
-def shift_y(value, step):
-    route = [(4 * y + z, 4 * ((y + step) % 4) + z) for y in range(4) for z in range(4)]
-    return lax.ppermute(value, "kern", route)
-
-
-def shift_z(value, step):
-    route = [(4 * y + z, 4 * y + (z + step) % 4) for y in range(4) for z in range(4)]
-    return lax.ppermute(value, "kern", route)
-
-
-def shift_tile(value, step):
-    peers = lax.axis_size("tile")
-    return lax.ppermute(value, "tile", [(i, (i + step) % peers) for i in range(peers)])
+def swap_y(value, step):
+    return lax.ppermute(value, "kern", [(i, i ^ (4 * step)) for i in range(16)])
+
+
+def swap_z(value, step):
+    return lax.ppermute(value, "kern", [(i, i ^ step) for i in range(16)])
+
+
+def swap_inner(value):
+    return lax.ppermute(value, "tile", [(i, i ^ 1) for i in range(16)])
+
+
+def swap_outer(value):
+    return lax.ppermute(value, "tile", [(i, ((i + 1) ^ 1) - 1 & 15) for i in range(16)])
 
 
 def per_device(mask_field, target, kernel_spectra, kernel_weight):
@@ -420,29 +428,28 @@
     at_y = lax.axis_index("kern") // 4
     order = [pltpu.VMEM((4, HALF, 2 * SHARD), F32)]
     mask_field = mask_field.T
-    above = shift_tile(mask_field, 1)
-    below = shift_tile(mask_field, -1)
+    inner, outer = swap_inner(mask_field), swap_outer(mask_field)
     heavy = call(weight_kernel, (8, 2 * SHARD), kernel_weight, smem=(0,))
     kernel_spectra, heavy = lax.optimization_barrier((kernel_spectra, heavy))
-    kernels = [kernel_spectra] + [shift_y(kernel_spectra, step) for step in (1, 2, 3)]
+    kernels = [kernel_spectra] + [swap_y(kernel_spectra, step) for step in (1, 2, 3)]
 
     rows = call(
-        window_kernel, (HALF, 2 * SHARD), above, below, mask_field, table["rows"], heavy
-    )
-    rows = [rows] + [shift_z(rows, -step) for step in (1, 2, 3)]
+        window_kernel, (HALF, 2 * SHARD), outer, inner, mask_field, table["rows"], heavy
+    )
+    rows = [rows] + [swap_z(rows, step) for step in (1, 2, 3)]
     *rows, h1, h3 = lax.optimization_barrier((*rows, kernels[1], kernels[3]))
     kernels = [kernel_spectra, h1, kernels[2], h3]
     part = call(
         band_kernel, (2 * HALF, FREQS), *rows, table["band"]
     )
-    parts = [part] + [shift_y(part, step) for step in (1, 2, 3)]
+    parts = [part] + [swap_y(part, step) for step in (1, 2, 3)]
     field, image = call(
         aerial_kernel,
         [(COUNT * QUARTER, 2 * SAMPLES), (QUARTER, SAMPLES)],
         *parts, *kernels, table["unfold"], table["flip"], table["out"],
         table["pixels"], flops=4 * 10**9,
     )
-    images = [image] + [shift_z(image, step) for step in (1, 2, 3)]
+    images = [image] + [swap_z(image, step) for step in (1, 2, 3)]
     goal = lax.dynamic_slice_in_dim(target, at_y * QUARTER, QUARTER, 0)
     messages = call(
         slope_kernel,
@@ -451,7 +458,7 @@
         table["pixels_back"], table["out_back"], table["flip_back"], table["fold"],
         scratch=[pltpu.VMEM((QUARTER, COLS), F32)],
     )
-    messages = [messages[0]] + [shift_y(messages[step], step) for step in (1, 2, 3)]
+    messages = [messages[0]] + [swap_y(messages[step], step) for step in (1, 2, 3)]
     resist = call(resist_kernel, (SHARD, TILE), *messages)
     grads = call(
         columns_kernel,
@@ -460,9 +467,9 @@
     )
     grad = grads[0]
     for step in (1, 2, 3):
-        grad = grad + shift_z(grads[step], step)
+        grad = grad + swap_z(grads[step], step)
     mask_grad = call(
-        final_kernel, (SHARD, TILE), shift_tile(grad, 1), grad, shift_tile(grad, -1),
+        final_kernel, (SHARD, TILE), swap_inner(grad), swap_outer(grad), grad,
         table["rows"],
     )
     return (resist.T, mask_grad.T)

time: 74.7 us -> 71.9 us (0.963)
  starting transfers between devices: 42.2 us -> 38.3 us
  waiting for transfers between devices: 24 us -> 25.7 us
  Pallas kernels: 7.46 us -> 6.6 us
    ppermute x22, starting transfers between devices: 42.2 us -> 38.3 us  [the longest x9 19.7 us: swap_z(): return lax.ppermute(value, 'kern', [(i, i ^ step) for i in range(16)])]
    ppermute x22, waiting for transfers between devices: 24 us -> 25.7 us  [the longest x9 12.1 us: swap_z(): return lax.ppermute(value, 'kern', [(i, i ^ step) for i in range(16)])]
    pallas_call x8, Pallas kernels: 7.46 us -> 6.6 us  [call(): pl.pallas_call(kernel, scratch_shapes=list(scratch), out_shape=out if man...]
  transfers between devices with their start and end apart: 22 -> 22, of which waited for: 14 -> 11; matrix products, arithmetic and copies ran while one was open for 0% -> 0% of each run, Pallas kernels for 3% -> 3%
where the time goes in v4:
time: 71.9 us; the launch traced here: 71.7 us
  starting transfers between devices  38.3 us (53%)
  waiting for transfers between devices  25.7 us (36%)
  Pallas kernels  6.6 us (9%)
  between operations  0.92 us (1%)
    ppermute x9, starting transfers between devices, swap_z(): return lax.ppermute(value, 'kern', [(i, i ^ step) for i in range(16)])  19.7 us
    ppermute x9, starting transfers between devices, swap_y(): return lax.ppermute(value, 'kern', [(i, i ^ 4 * step) for i in range(16)])  14.1 us
    ppermute x9, waiting for transfers between devices, swap_z(): return lax.ppermute(value, 'kern', [(i, i ^ step) for i in range(16)])  12.1 us
    ppermute x9, waiting for transfers between devices, swap_y(): return lax.ppermute(value, 'kern', [(i, i ^ 4 * step) for i in range(16)])  8.96 us
    pallas_call x8, Pallas kernels, call(): pl.pallas_call(kernel, scratch_shapes=list(scratch), out_shape=out if man...  6.6 us
    ppermute x2, waiting for transfers between devices, swap_outer(): lax.ppermute(value, 'tile', [(i, (i + 1 ^ 1) - 1 & 15) for i in range(16)])  4.59 us
    ppermute x2, starting transfers between devices, swap_outer(): lax.ppermute(value, 'tile', [(i, (i + 1 ^ 1) - 1 & 15) for i in range(16)])  4.31 us
  transfers between devices with their start and end apart: 22, of which 11 were waited for; matrix products, arithmetic and copies ran while one was open for 0% of the time, Pallas kernels for 3%

profile of v4, /device:TPU:64, one launch (start us, length us, event | category | flops | bytes accessed | tf_op | source)
XLA Modules:
  0.0 71.7 jit_solution(2070194337307165037)
XLA Ops:
  0.6 0.0 copy-start
  0.7 0.0 copy-start.12
  0.7 0.1 collective-permute-start.1
  0.8 4.2 %collective-permute-start = (f32[64,256]{1,0:T(8,128)}, f32[64,256]{1,0:T(8,128)S(1)}, u32[]{:S(2)}, u32[]{:S(2)}) collective-permute-start(f32[64,256]{1,0:T(8,128)} %bitcast.4), channel_id=1, source_target_pairs={{0,240},{16,32},{32,16},{48,64},{64,48},{80,96},{96,80},{112,128},... | collective-permute-start | bytes 196616 | tf_op jit(solution)/shard_map/ppermute | solution.py:423
  5.0 0.5 weight_kernel.1.heavy_ref
  5.6 0.0 copy-start.6
  5.6 3.1 %collective-permute-start.6 = (f32[2,2,128,128]{3,2,1,0:T(8,128)S(1)}, f32[2,2,128,128]{3,2,1,0:T(8,128)S(1)}, u32[]{:S(2)}, u32[]{:S(2)}) collective-permute-start(f32[2,2,128,128]{3,2,1,0:T(8,128)S(1)} %copy-done.1), channel_id=1, source_target_pairs={{0,12},{1,13},{2,14},{3,15},{4,8},{5,9},{6,10},{7,11},{8,4},{9,5},... | collective-permute-start | bytes 786440 | tf_op jit(solution)/shard_map/ppermute | solution.py:411
  8.7 0.1 collective-permute-start.5
  8.8 0.3 window_kernel.1.r0
  9.1 0.0 copy-start.9
  9.2 0.0 copy-start.11
  9.2 0.0 copy-start.14
  9.2 3.7 %collective-permute-start.4 = (f32[72,128]{1,0:T(8,128)S(1)}, f32[72,128]{1,0:T(8,128)S(1)}, u32[]{:S(2)}, u32[]{:S(2)}) collective-permute-start(f32[72,128]{1,0:T(8,128)S(1)} %window_kernel.1.r0), channel_id=1, source_target_pairs={{0,3},{1,2},{2,1},{3,0},{4,7},{5,6},{6,5},{7,4},{8,11},{9,10},{10,... | collective-permute-start | bytes 110600 | tf_op jit(solution)/shard_map/ppermute | solution.py:415
  12.8 1.0 %collective-permute-start.3 = (f32[72,128]{1,0:T(8,128)S(1)}, f32[72,128]{1,0:T(8,128)S(1)}, u32[]{:S(2)}, u32[]{:S(2)}) collective-permute-start(f32[72,128]{1,0:T(8,128)S(1)} %window_kernel.1.r0), channel_id=1, source_target_pairs={{0,2},{1,3},{2,0},{3,1},{4,6},{5,7},{6,4},{7,5},{8,10},{9,11},{10,... | collective-permute-start | bytes 110600 | tf_op jit(solution)/shard_map/ppermute | solution.py:415
  13.9 1.9 %collective-permute-start.2 = (f32[72,128]{1,0:T(8,128)S(1)}, f32[72,128]{1,0:T(8,128)S(1)}, u32[]{:S(2)}, u32[]{:S(2)}) collective-permute-start(f32[72,128]{1,0:T(8,128)S(1)} %window_kernel.1.r0), channel_id=1, source_target_pairs={{0,1},{1,0},{2,3},{3,2},{4,5},{5,4},{6,7},{7,6},{8,9},{9,8},{10,11... | collective-permute-start | bytes 110600 | tf_op jit(solution)/shard_map/ppermute | solution.py:415
  15.8 1.9 %collective-permute-start.10 = (f32[2,2,128,128]{3,2,1,0:T(8,128)S(1)}, f32[2,2,128,128]{3,2,1,0:T(8,128)S(1)}, u32[]{:S(2)}, u32[]{:S(2)}) collective-permute-start(f32[2,2,128,128]{3,2,1,0:T(8,128)S(1)} %copy-done.1), channel_id=1, source_target_pairs={{0,8},{1,9},{2,10},{3,11},{4,12},{5,13},{6,14},{7,15},{8,0},{9,1},... | collective-permute-start | bytes 786440 | tf_op jit(solution)/shard_map/ppermute | solution.py:411
  17.7 3.2 %collective-permute-done.3.r2 = f32[72,128]{1,0:T(8,128)S(1)} collective-permute-done((f32[72,128]{1,0:T(8,128)S(1)}, f32[72,128]{1,0:T(8,128)S(1)}, u32[]{:S(2)}, u32[]{:S(2)}) %collective-permute-start.3) | collective-permute-done | bytes 36896 | tf_op jit(solution)/shard_map/ppermute | solution.py:415
  20.8 0.3 band_kernel.1.p0
  21.2 3.0 %collective-permute-start.9 = (f32[144,128]{1,0:T(8,128)S(1)}, f32[144,128]{1,0:T(8,128)S(1)}, u32[]{:S(2)}, u32[]{:S(2)}) collective-permute-start(f32[144,128]{1,0:T(8,128)S(1)} %band_kernel.1.p0), channel_id=1, source_target_pairs={{0,12},{1,13},{2,14},{3,15},{4,8},{5,9},{6,10},{7,11},{8,4},{9,5},... | collective-permute-start | bytes 221192 | tf_op jit(solution)/shard_map/ppermute | solution.py:411
  24.1 1.0 %collective-permute-start.8 = (f32[144,128]{1,0:T(8,128)S(1)}, f32[144,128]{1,0:T(8,128)S(1)}, u32[]{:S(2)}, u32[]{:S(2)}) collective-permute-start(f32[144,128]{1,0:T(8,128)S(1)} %band_kernel.1.p0), channel_id=1, source_target_pairs={{0,8},{1,9},{2,10},{3,11},{4,12},{5,13},{6,14},{7,15},{8,0},{9,1},... | collective-permute-start | bytes 221192 | tf_op jit(solution)/shard_map/ppermute | solution.py:411
  25.2 0.1 collective-permute-start.7
  25.3 1.5 %collective-permute-done.9.p3 = f32[144,128]{1,0:T(8,128)S(1)} collective-permute-done((f32[144,128]{1,0:T(8,128)S(1)}, f32[144,128]{1,0:T(8,128)S(1)}, u32[]{:S(2)}, u32[]{:S(2)}) %collective-permute-start.9) | collective-permute-done | bytes 73760 | tf_op jit(solution)/shard_map/ppermute | solution.py:411
  26.8 3.2 %collective-permute-done.8.p2 = f32[144,128]{1,0:T(8,128)S(1)} collective-permute-done((f32[144,128]{1,0:T(8,128)S(1)}, f32[144,128]{1,0:T(8,128)S(1)}, u32[]{:S(2)}, u32[]{:S(2)}) %collective-permute-start.8) | collective-permute-done | bytes 73760 | tf_op jit(solution)/shard_map/ppermute | solution.py:411
  30.0 0.0 copy-start.10
  30.1 1.3 %aerial_kernel.1 = (f32[512,512]{1,0:T(8,128)S(1)}, f32[64,256]{1,0:T(8,128)S(1)}) custom-call(f32[144,128]{1,0:T(8,128)S(1)} %band_kernel.1.p0, f32[144,128]{1,0:T(8,128)S(1)} %collective-permute-done.7.p1, f32[144,128]{1,0:T(8,128)S(1)} %collective-permute-done.8.p2, f32[144,128]{1,0:T(8,128)S(1)} %collective-permute-done.9.p3, ...), custom_call_target="tpu_custom_call" | custom-call | flops 4000000000 | bytes 1000000 | tf_op jit(solution)/shard_map/aerial_kernel/pallas_call | solution.py:396
  31.4 1.5 %collective-permute-start.13 = (f32[64,256]{1,0:T(8,128)S(1)}, f32[64,256]{1,0:T(8,128)S(1)}, u32[]{:S(2)}, u32[]{:S(2)}) collective-permute-start(f32[64,256]{1,0:T(8,128)S(1)} %get-tuple-element.28.i0), channel_id=1, source_target_pairs={{0,3},{1,2},{2,1},{3,0},{4,7},{5,6},{6,5},{7,4},{8,11},{9,10},{10,... | collective-permute-start | bytes 196616 | tf_op jit(solution)/shard_map/ppermute | solution.py:415
  32.9 3.1 %collective-permute-start.12 = (f32[64,256]{1,0:T(8,128)S(1)}, f32[64,256]{1,0:T(8,128)S(1)}, u32[]{:S(2)}, u32[]{:S(2)}) collective-permute-start(f32[64,256]{1,0:T(8,128)S(1)} %get-tuple-element.28.i0), channel_id=1, source_target_pairs={{0,2},{1,3},{2,0},{3,1},{4,6},{5,7},{6,4},{7,5},{8,10},{9,11},{10,... | collective-permute-start | bytes 196616 | tf_op jit(solution)/shard_map/ppermute | solution.py:415
  36.0 2.0 %collective-permute-start.11 = (f32[64,256]{1,0:T(8,128)S(1)}, f32[64,256]{1,0:T(8,128)S(1)}, u32[]{:S(2)}, u32[]{:S(2)}) collective-permute-start(f32[64,256]{1,0:T(8,128)S(1)} %get-tuple-element.28.i0), channel_id=1, source_target_pairs={{0,1},{1,0},{2,3},{3,2},{4,5},{5,4},{6,7},{7,6},{8,9},{9,8},{10,11... | collective-permute-start | bytes 196616 | tf_op jit(solution)/shard_map/ppermute | solution.py:415
  38.0 1.7 %collective-permute-done.13.i3 = f32[64,256]{1,0:T(8,128)S(1)} collective-permute-done((f32[64,256]{1,0:T(8,128)S(1)}, f32[64,256]{1,0:T(8,128)S(1)}, u32[]{:S(2)}, u32[]{:S(2)}) %collective-permute-start.13) | collective-permute-done | bytes 65568 | tf_op jit(solution)/shard_map/ppermute | solution.py:415
  39.7 1.4 %collective-permute-done.12.i2 = f32[64,256]{1,0:T(8,128)S(1)} collective-permute-done((f32[64,256]{1,0:T(8,128)S(1)}, f32[64,256]{1,0:T(8,128)S(1)}, u32[]{:S(2)}, u32[]{:S(2)}) %collective-permute-start.12) | collective-permute-done | bytes 65568 | tf_op jit(solution)/shard_map/ppermute | solution.py:415
  41.1 0.6 collective-permute-done.11.i1
  41.8 2.1 %slope_kernel.1 = (f32[176,128]{1,0:T(8,128)S(1)}, f32[176,128]{1,0:T(8,128)S(1)}, f32[176,128]{1,0:T(8,128)S(1)}, f32[176,128]{1,0:T(8,128)S(1)}) custom-call(f32[64,256]{1,0:T(8,128)S(1)} %get-tuple-element.28.i0, f32[64,256]{1,0:T(8,128)S(1)} %collective-permute-done.11.i1, f32[64,256]{1,0:T(8,128)S(1)} %collective-permute-done.12.i2, ...), custom_call_target="tpu_custom_call" | custom-call | flops 4000000000 | bytes 1000000 | tf_op jit(solution)/shard_map/slope_kernel/pallas_call | solution.py:396
  44.0 2.0 %collective-permute-start.14 = (f32[176,128]{1,0:T(8,128)S(1)}, f32[176,128]{1,0:T(8,128)S(1)}, u32[]{:S(2)}, u32[]{:S(2)}) collective-permute-start(f32[176,128]{1,0:T(8,128)S(1)} %get-tuple-element.31), channel_id=1, source_target_pairs={{0,4},{1,5},{2,6},{3,7},{4,0},{5,1},{6,2},{7,3},{8,12},{9,13},{10,... | collective-permute-start | bytes 270344 | tf_op jit(solution)/shard_map/ppermute | solution.py:411
  46.0 1.3 %collective-permute-start.15 = (f32[176,128]{1,0:T(8,128)S(1)}, f32[176,128]{1,0:T(8,128)S(1)}, u32[]{:S(2)}, u32[]{:S(2)}) collective-permute-start(f32[176,128]{1,0:T(8,128)S(1)} %get-tuple-element.32), channel_id=1, source_target_pairs={{0,8},{1,9},{2,10},{3,11},{4,12},{5,13},{6,14},{7,15},{8,0},{9,1},... | collective-permute-start | bytes 270344 | tf_op jit(solution)/shard_map/ppermute | solution.py:411
  47.3 1.5 %collective-permute-start.16 = (f32[176,128]{1,0:T(8,128)S(1)}, f32[176,128]{1,0:T(8,128)S(1)}, u32[]{:S(2)}, u32[]{:S(2)}) collective-permute-start(f32[176,128]{1,0:T(8,128)S(1)} %get-tuple-element.33), channel_id=1, source_target_pairs={{0,12},{1,13},{2,14},{3,15},{4,8},{5,9},{6,10},{7,11},{8,4},{9,5},... | collective-permute-start | bytes 270344 | tf_op jit(solution)/shard_map/ppermute | solution.py:411
  48.8 3.3 %collective-permute-done.15.m2 = f32[176,128]{1,0:T(8,128)S(1)} collective-permute-done((f32[176,128]{1,0:T(8,128)S(1)}, f32[176,128]{1,0:T(8,128)S(1)}, u32[]{:S(2)}, u32[]{:S(2)}) %collective-permute-start.15) | collective-permute-done | bytes 90144 | tf_op jit(solution)/shard_map/ppermute | solution.py:411
  52.0 1.0 %collective-permute-done.16.m3 = f32[176,128]{1,0:T(8,128)S(1)} collective-permute-done((f32[176,128]{1,0:T(8,128)S(1)}, f32[176,128]{1,0:T(8,128)S(1)}, u32[]{:S(2)}, u32[]{:S(2)}) %collective-permute-start.16) | collective-permute-done | bytes 90144 | tf_op jit(solution)/shard_map/ppermute | solution.py:411
  53.0 0.3 columns_kernel.1
  53.4 2.1 %collective-permute-start.17 = (f32[72,128]{1,0:T(8,128)S(1)}, f32[72,128]{1,0:T(8,128)S(1)}, u32[]{:S(2)}, u32[]{:S(2)}) collective-permute-start(f32[72,128]{1,0:T(8,128)S(1)} %get-tuple-element.35), channel_id=1, source_target_pairs={{0,1},{1,0},{2,3},{3,2},{4,5},{5,4},{6,7},{7,6},{8,9},{9,8},{10,11... | collective-permute-start | bytes 110600 | tf_op jit(solution)/shard_map/ppermute | solution.py:415
  55.5 3.6 %collective-permute-start.18 = (f32[72,128]{1,0:T(8,128)S(1)}, f32[72,128]{1,0:T(8,128)S(1)}, u32[]{:S(2)}, u32[]{:S(2)}) collective-permute-start(f32[72,128]{1,0:T(8,128)S(1)} %get-tuple-element.36), channel_id=1, source_target_pairs={{0,2},{1,3},{2,0},{3,1},{4,6},{5,7},{6,4},{7,5},{8,10},{9,11},{10,... | collective-permute-start | bytes 110600 | tf_op jit(solution)/shard_map/ppermute | solution.py:415
  59.1 0.9 %collective-permute-start.19 = (f32[72,128]{1,0:T(8,128)S(1)}, f32[72,128]{1,0:T(8,128)S(1)}, u32[]{:S(2)}, u32[]{:S(2)}) collective-permute-start(f32[72,128]{1,0:T(8,128)S(1)} %get-tuple-element.37), channel_id=1, source_target_pairs={{0,3},{1,2},{2,1},{3,0},{4,7},{5,6},{6,5},{7,4},{8,11},{9,10},{10,... | collective-permute-start | bytes 110600 | tf_op jit(solution)/shard_map/ppermute | solution.py:415
  60.0 3.3 %collective-permute-done.18 = f32[72,128]{1,0:T(8,128)S(1)} collective-permute-done((f32[72,128]{1,0:T(8,128)S(1)}, f32[72,128]{1,0:T(8,128)S(1)}, u32[]{:S(2)}, u32[]{:S(2)}) %collective-permute-start.18) | collective-permute-done | bytes 36896 | tf_op jit(solution)/shard_map/ppermute | solution.py:415
  63.3 1.8 %collective-permute-done.19 = f32[72,128]{1,0:T(8,128)S(1)} collective-permute-done((f32[72,128]{1,0:T(8,128)S(1)}, f32[72,128]{1,0:T(8,128)S(1)}, u32[]{:S(2)}, u32[]{:S(2)}) %collective-permute-start.19) | collective-permute-done | bytes 36896 | tf_op jit(solution)/shard_map/ppermute | solution.py:415
  65.2 0.1 collective-permute-start.21
  65.3 0.1 collective-permute-start.20
  65.4 0.8 %resist_kernel.1 = f32[64,256]{1,0:T(8,128)} custom-call(f32[176,128]{1,0:T(8,128)S(1)} %get-tuple-element.30.m0, f32[176,128]{1,0:T(8,128)S(1)} %collective-permute-done.14.m1, f32[176,128]{1,0:T(8,128)S(1)} %collective-permute-done.15.m2, f32[176,128]{1,0:T(8,128)S(1)} %collective-permute-done.16.m3), custom_call_target="tpu_custom_call" | custom-call | flops 4000000000 | bytes 1000000 | tf_op jit(solution)/shard_map/resist_kernel/pallas_call | solution.py:396
  66.1 4.6 %collective-permute-done.21.outer_ref = f32[72,128]{1,0:T(8,128)S(1)} collective-permute-done((f32[72,128]{1,0:T(8,128)S(1)}, f32[72,128]{1,0:T(8,128)S(1)}, u32[]{:S(2)}, u32[]{:S(2)}) %collective-permute-start.21) | collective-permute-done | bytes 36896 | tf_op jit(solution)/shard_map/ppermute | solution.py:423
  70.7 0.9 %final_kernel.1 = f32[64,256]{1,0:T(8,128)} custom-call(f32[72,128]{1,0:T(8,128)S(1)} %collective-permute-done.20.inner_ref, f32[72,128]{1,0:T(8,128)S(1)} %collective-permute-done.21.outer_ref, f32[72,128]{1,0:T(8,128)S(1)} %add_add_fusion.own_ref, bf16[2,144,256]{2,1,0:T(8,128)(2,1)S(1)} %copy-done.12), custom_call_target="tpu_custom_call" | custom-call | flops 4000000000 | bytes 1000000 | tf_op jit(solution)/shard_map/final_kernel/pallas_call | solution.py:396
  (42 shorter events, 0.1 us)
Async XLA Ops:
  0.6 37.3 %copy-start = (s32[256,1024]{1,0:T(8,128)S(1)}, s32[256,1024]{1,0:T(8,128)}, u32[]{:S(2)}) copy-start(s32[256,1024]{1,0:T(8,128)} %param.19) | copy-start | bytes 3145732
  0.6 4.4 %copy-start.3 = (f32[2]{0:T(128)S(1)}, f32[2]{0:T(128)}, u32[]{:S(2)}) copy-start(f32[2]{0:T(128)} %weight_ref.1) | copy-start | bytes 28
  0.7 4.9 %copy-start.1 = (f32[2,2,128,128]{3,2,1,0:T(8,128)S(1)}, f32[2,2,128,128]{3,2,1,0:T(8,128)}, u32[]{:S(2)}) copy-start(f32[2,2,128,128]{3,2,1,0:T(8,128)} %h0.1) | copy-start | bytes 786436
  0.7 8.2 %copy-start.2 = (f32[256,64]{0,1:T(8,128)S(1)}, f32[256,64]{0,1:T(8,128)}, u32[]{:S(2)}) copy-start(f32[256,64]{0,1:T(8,128)} %param.18) | copy-start | bytes 196612
  0.7 8.2 %copy-start.12 = (bf16[2,144,256]{2,1,0:T(8,128)(2,1)S(1)}, bf16[2,144,256]{2,1,0:T(8,128)(2,1)}, u32[]{:S(2)}) copy-start(bf16[2,144,256]{2,1,0:T(8,128)(2,1)} %constant.53.clone.rows_ref) | copy-start | bytes 442372
  0.7 8.1 %collective-permute-start.1 = (f32[64,256]{1,0:T(8,128)}, f32[64,256]{1,0:T(8,128)S(1)}, u32[]{:S(2)}, u32[]{:S(2)}) collective-permute-start(f32[64,256]{1,0:T(8,128)} %bitcast.3), channel_id=1, source_target_pairs={{0,16},{16,0},{32,48},{48,32},{64,80},{80,64},{96,112},{112,96},{1... | collective-permute-start | bytes 196616 | tf_op jit(solution)/shard_map/ppermute | solution.py:419
  0.8 8.0 %collective-permute-start = (f32[64,256]{1,0:T(8,128)}, f32[64,256]{1,0:T(8,128)S(1)}, u32[]{:S(2)}, u32[]{:S(2)}) collective-permute-start(f32[64,256]{1,0:T(8,128)} %bitcast.4), channel_id=1, source_target_pairs={{0,240},{16,32},{32,16},{48,64},{64,48},{80,96},{96,80},{112,128},... | collective-permute-start | bytes 196616 | tf_op jit(solution)/shard_map/ppermute | solution.py:423
  5.6 15.3 %copy-start.6 = (bf16[2,16,64,256]{3,2,1,0:T(8,128)(2,1)S(1)}, bf16[2,16,64,256]{3,2,1,0:T(8,128)(2,1)}, u32[]{:S(2)}) copy-start(bf16[2,16,64,256]{3,2,1,0:T(8,128)(2,1)} %constant.54.clone.band_ref) | copy-start | bytes 3145732
  5.6 15.2 %collective-permute-start.6 = (f32[2,2,128,128]{3,2,1,0:T(8,128)S(1)}, f32[2,2,128,128]{3,2,1,0:T(8,128)S(1)}, u32[]{:S(2)}, u32[]{:S(2)}) collective-permute-start(f32[2,2,128,128]{3,2,1,0:T(8,128)S(1)} %copy-done.1), channel_id=1, source_target_pairs={{0,12},{1,13},{2,14},{3,15},{4,8},{5,9},{6,10},{7,11},{8,4},{9,5},... | collective-permute-start | bytes 786440 | tf_op jit(solution)/shard_map/ppermute | solution.py:411
  8.7 12.1 %collective-permute-start.5 = (f32[2,2,128,128]{3,2,1,0:T(8,128)S(1)}, f32[2,2,128,128]{3,2,1,0:T(8,128)S(1)}, u32[]{:S(2)}, u32[]{:S(2)}) collective-permute-start(f32[2,2,128,128]{3,2,1,0:T(8,128)S(1)} %copy-done.1), channel_id=1, source_target_pairs={{0,4},{1,5},{2,6},{3,7},{4,0},{5,1},{6,2},{7,3},{8,12},{9,13},{10,... | collective-permute-start | bytes 786440 | tf_op jit(solution)/shard_map/ppermute | solution.py:411
  9.1 20.9 %copy-start.9 = (bf16[2,256,512]{2,1,0:T(8,128)(2,1)S(1)}, bf16[2,256,512]{2,1,0:T(8,128)(2,1)}, u32[]{:S(2)}) copy-start(bf16[2,256,512]{2,1,0:T(8,128)(2,1)} %constant.63.clone.pixels_ref) | copy-start | bytes 1572868
  9.2 20.9 %copy-start.11 = (bf16[2,4,128,128]{3,2,1,0:T(8,128)(2,1)S(1)}, bf16[2,4,128,128]{3,2,1,0:T(8,128)(2,1)}, u32[]{:S(2)}) copy-start(bf16[2,4,128,128]{3,2,1,0:T(8,128)(2,1)} %constant.61.clone.out_rows_ref) | copy-start | bytes 786436
  9.2 20.9 %copy-start.14 = (bf16[128,256]{1,0:T(8,128)(2,1)S(1)}, bf16[128,256]{1,0:T(8,128)(2,1)}, u32[]{:S(2)}) copy-start(bf16[128,256]{1,0:T(8,128)(2,1)} %constant.57.clone.unfold_ref) | copy-start | bytes 196612
  9.2 6.6 %collective-permute-start.4 = (f32[72,128]{1,0:T(8,128)S(1)}, f32[72,128]{1,0:T(8,128)S(1)}, u32[]{:S(2)}, u32[]{:S(2)}) collective-permute-start(f32[72,128]{1,0:T(8,128)S(1)} %window_kernel.1.r0), channel_id=1, source_target_pairs={{0,3},{1,2},{2,1},{3,0},{4,7},{5,6},{6,5},{7,4},{8,11},{9,10},{10,... | collective-permute-start | bytes 110600 | tf_op jit(solution)/shard_map/ppermute | solution.py:415
  12.8 8.0 %collective-permute-start.3 = (f32[72,128]{1,0:T(8,128)S(1)}, f32[72,128]{1,0:T(8,128)S(1)}, u32[]{:S(2)}, u32[]{:S(2)}) collective-permute-start(f32[72,128]{1,0:T(8,128)S(1)} %window_kernel.1.r0), channel_id=1, source_target_pairs={{0,2},{1,3},{2,0},{3,1},{4,6},{5,7},{6,4},{7,5},{8,10},{9,11},{10,... | collective-permute-start | bytes 110600 | tf_op jit(solution)/shard_map/ppermute | solution.py:415
  13.9 7.0 %collective-permute-start.2 = (f32[72,128]{1,0:T(8,128)S(1)}, f32[72,128]{1,0:T(8,128)S(1)}, u32[]{:S(2)}, u32[]{:S(2)}) collective-permute-start(f32[72,128]{1,0:T(8,128)S(1)} %window_kernel.1.r0), channel_id=1, source_target_pairs={{0,1},{1,0},{2,3},{3,2},{4,5},{5,4},{6,7},{7,6},{8,9},{9,8},{10,11... | collective-permute-start | bytes 110600 | tf_op jit(solution)/shard_map/ppermute | solution.py:415
  15.8 9.6 %collective-permute-start.10 = (f32[2,2,128,128]{3,2,1,0:T(8,128)S(1)}, f32[2,2,128,128]{3,2,1,0:T(8,128)S(1)}, u32[]{:S(2)}, u32[]{:S(2)}) collective-permute-start(f32[2,2,128,128]{3,2,1,0:T(8,128)S(1)} %copy-done.1), channel_id=1, source_target_pairs={{0,8},{1,9},{2,10},{3,11},{4,12},{5,13},{6,14},{7,15},{8,0},{9,1},... | collective-permute-start | bytes 786440 | tf_op jit(solution)/shard_map/ppermute | solution.py:411
  21.2 5.6 %collective-permute-start.9 = (f32[144,128]{1,0:T(8,128)S(1)}, f32[144,128]{1,0:T(8,128)S(1)}, u32[]{:S(2)}, u32[]{:S(2)}) collective-permute-start(f32[144,128]{1,0:T(8,128)S(1)} %band_kernel.1.p0), channel_id=1, source_target_pairs={{0,12},{1,13},{2,14},{3,15},{4,8},{5,9},{6,10},{7,11},{8,4},{9,5},... | collective-permute-start | bytes 221192 | tf_op jit(solution)/shard_map/ppermute | solution.py:411
  24.1 5.9 %collective-permute-start.8 = (f32[144,128]{1,0:T(8,128)S(1)}, f32[144,128]{1,0:T(8,128)S(1)}, u32[]{:S(2)}, u32[]{:S(2)}) collective-permute-start(f32[144,128]{1,0:T(8,128)S(1)} %band_kernel.1.p0), channel_id=1, source_target_pairs={{0,8},{1,9},{2,10},{3,11},{4,12},{5,13},{6,14},{7,15},{8,0},{9,1},... | collective-permute-start | bytes 221192 | tf_op jit(solution)/shard_map/ppermute | solution.py:411
  25.2 4.8 %collective-permute-start.7 = (f32[144,128]{1,0:T(8,128)S(1)}, f32[144,128]{1,0:T(8,128)S(1)}, u32[]{:S(2)}, u32[]{:S(2)}) collective-permute-start(f32[144,128]{1,0:T(8,128)S(1)} %band_kernel.1.p0), channel_id=1, source_target_pairs={{0,4},{1,5},{2,6},{3,7},{4,0},{5,1},{6,2},{7,3},{8,12},{9,13},{10,... | collective-permute-start | bytes 221192 | tf_op jit(solution)/shard_map/ppermute | solution.py:411
  25.3 4.7 %copy-start.17 = (bf16[64,72]{1,0:T(8,128)(2,1)S(1)}, bf16[64,72]{1,0:T(8,128)(2,1)}, u32[]{:S(2)}) copy-start(bf16[64,72]{1,0:T(8,128)(2,1)} %constant.59.clone.flip_ref) | copy-start | bytes 27652
  25.3 16.5 %copy-start.4 = (bf16[2,1024,256]{2,1,0:T(8,128)(2,1)S(1)}, bf16[2,1024,256]{2,1,0:T(8,128)(2,1)}, u32[]{:S(2)}) copy-start(bf16[2,1024,256]{2,1,0:T(8,128)(2,1)} %constant.66.clone.spread_back_ref) | copy-start | bytes 3145732
  25.3 16.5 %copy-start.5 = (bf16[2,256,1024]{2,1,0:T(8,128)(2,1)S(1)}, bf16[2,256,1024]{2,1,0:T(8,128)(2,1)}, u32[]{:S(2)}) copy-start(bf16[2,256,1024]{2,1,0:T(8,128)(2,1)} %constant.65.clone.spread_ref) | copy-start | bytes 3145732
  30.0 11.7 %copy-start.10 = (bf16[2,4,128,128]{3,2,1,0:T(8,128)(2,1)S(1)}, bf16[2,4,128,128]{3,2,1,0:T(8,128)(2,1)}, u32[]{:S(2)}) copy-start(bf16[2,4,128,128]{3,2,1,0:T(8,128)(2,1)} %constant.62.clone.out_back_ref) | copy-start | bytes 786436
  30.0 11.7 %copy-start.13 = (bf16[256,128]{1,0:T(8,128)(2,1)S(1)}, bf16[256,128]{1,0:T(8,128)(2,1)}, u32[]{:S(2)}) copy-start(bf16[256,128]{1,0:T(8,128)(2,1)} %constant.58.clone.fold_ref) | copy-start | bytes 196612
  30.1 11.7 %copy-start.16 = (bf16[72,64]{1,0:T(8,128)(2,1)S(1)}, bf16[72,64]{1,0:T(8,128)(2,1)}, u32[]{:S(2)}) copy-start(bf16[72,64]{1,0:T(8,128)(2,1)} %constant.60.clone.flip_back_ref) | copy-start | bytes 27652
  31.4 10.4 %copy-start.8 = (bf16[2,512,256]{2,1,0:T(8,128)(2,1)S(1)}, bf16[2,512,256]{2,1,0:T(8,128)(2,1)}, u32[]{:S(2)}) copy-start(bf16[2,512,256]{2,1,0:T(8,128)(2,1)} %constant.64.clone.pixels_back_ref) | copy-start | bytes 1572868
  31.4 8.3 %collective-permute-start.13 = (f32[64,256]{1,0:T(8,128)S(1)}, f32[64,256]{1,0:T(8,128)S(1)}, u32[]{:S(2)}, u32[]{:S(2)}) collective-permute-start(f32[64,256]{1,0:T(8,128)S(1)} %get-tuple-element.28.i0), channel_id=1, source_target_pairs={{0,3},{1,2},{2,1},{3,0},{4,7},{5,6},{6,5},{7,4},{8,11},{9,10},{10,... | collective-permute-start | bytes 196616 | tf_op jit(solution)/shard_map/ppermute | solution.py:415
  32.9 8.2 %collective-permute-start.12 = (f32[64,256]{1,0:T(8,128)S(1)}, f32[64,256]{1,0:T(8,128)S(1)}, u32[]{:S(2)}, u32[]{:S(2)}) collective-permute-start(f32[64,256]{1,0:T(8,128)S(1)} %get-tuple-element.28.i0), channel_id=1, source_target_pairs={{0,2},{1,3},{2,0},{3,1},{4,6},{5,7},{6,4},{7,5},{8,10},{9,11},{10,... | collective-permute-start | bytes 196616 | tf_op jit(solution)/shard_map/ppermute | solution.py:415
  36.0 5.8 %collective-permute-start.11 = (f32[64,256]{1,0:T(8,128)S(1)}, f32[64,256]{1,0:T(8,128)S(1)}, u32[]{:S(2)}, u32[]{:S(2)}) collective-permute-start(f32[64,256]{1,0:T(8,128)S(1)} %get-tuple-element.28.i0), channel_id=1, source_target_pairs={{0,1},{1,0},{2,3},{3,2},{4,5},{5,4},{6,7},{7,6},{8,9},{9,8},{10,11... | collective-permute-start | bytes 196616 | tf_op jit(solution)/shard_map/ppermute | solution.py:415
  41.8 11.2 %copy-start.7 = (bf16[2,128,1024]{2,1,0:T(8,128)(2,1)S(1)}, bf16[2,128,1024]{2,1,0:T(8,128)(2,1)}, u32[]{:S(2)}) copy-start(bf16[2,128,1024]{2,1,0:T(8,128)(2,1)} %constant.55.clone.band_back_ref) | copy-start | bytes 1572868
  41.8 11.2 %copy-start.15 = (f32[8,1024]{1,0:T(8,128)S(1)}, f32[8,1024]{1,0:T(8,128)}, u32[]{:S(2)}) copy-start(f32[8,1024]{1,0:T(8,128)} %constant.56.clone.edge_ref) | copy-start | bytes 98308
  44.0 4.8 %collective-permute-start.14 = (f32[176,128]{1,0:T(8,128)S(1)}, f32[176,128]{1,0:T(8,128)S(1)}, u32[]{:S(2)}, u32[]{:S(2)}) collective-permute-start(f32[176,128]{1,0:T(8,128)S(1)} %get-tuple-element.31), channel_id=1, source_target_pairs={{0,4},{1,5},{2,6},{3,7},{4,0},{5,1},{6,2},{7,3},{8,12},{9,13},{10,... | collective-permute-start | bytes 270344 | tf_op jit(solution)/shard_map/ppermute | solution.py:411
  46.0 6.0 %collective-permute-start.15 = (f32[176,128]{1,0:T(8,128)S(1)}, f32[176,128]{1,0:T(8,128)S(1)}, u32[]{:S(2)}, u32[]{:S(2)}) collective-permute-start(f32[176,128]{1,0:T(8,128)S(1)} %get-tuple-element.32), channel_id=1, source_target_pairs={{0,8},{1,9},{2,10},{3,11},{4,12},{5,13},{6,14},{7,15},{8,0},{9,1},... | collective-permute-start | bytes 270344 | tf_op jit(solution)/shard_map/ppermute | solution.py:411
  47.3 5.7 %collective-permute-start.16 = (f32[176,128]{1,0:T(8,128)S(1)}, f32[176,128]{1,0:T(8,128)S(1)}, u32[]{:S(2)}, u32[]{:S(2)}) collective-permute-start(f32[176,128]{1,0:T(8,128)S(1)} %get-tuple-element.33), channel_id=1, source_target_pairs={{0,12},{1,13},{2,14},{3,15},{4,8},{5,9},{6,10},{7,11},{8,4},{9,5},... | collective-permute-start | bytes 270344 | tf_op jit(solution)/shard_map/ppermute | solution.py:411
  53.4 6.6 %collective-permute-start.17 = (f32[72,128]{1,0:T(8,128)S(1)}, f32[72,128]{1,0:T(8,128)S(1)}, u32[]{:S(2)}, u32[]{:S(2)}) collective-permute-start(f32[72,128]{1,0:T(8,128)S(1)} %get-tuple-element.35), channel_id=1, source_target_pairs={{0,1},{1,0},{2,3},{3,2},{4,5},{5,4},{6,7},{7,6},{8,9},{9,8},{10,11... | collective-permute-start | bytes 110600 | tf_op jit(solution)/shard_map/ppermute | solution.py:415
  55.5 7.9 %collective-permute-start.18 = (f32[72,128]{1,0:T(8,128)S(1)}, f32[72,128]{1,0:T(8,128)S(1)}, u32[]{:S(2)}, u32[]{:S(2)}) collective-permute-start(f32[72,128]{1,0:T(8,128)S(1)} %get-tuple-element.36), channel_id=1, source_target_pairs={{0,2},{1,3},{2,0},{3,1},{4,6},{5,7},{6,4},{7,5},{8,10},{9,11},{10,... | collective-permute-start | bytes 110600 | tf_op jit(solution)/shard_map/ppermute | solution.py:415
  59.1 6.1 %collective-permute-start.19 = (f32[72,128]{1,0:T(8,128)S(1)}, f32[72,128]{1,0:T(8,128)S(1)}, u32[]{:S(2)}, u32[]{:S(2)}) collective-permute-start(f32[72,128]{1,0:T(8,128)S(1)} %get-tuple-element.37), channel_id=1, source_target_pairs={{0,3},{1,2},{2,1},{3,0},{4,7},{5,6},{6,5},{7,4},{8,11},{9,10},{10,... | collective-permute-start | bytes 110600 | tf_op jit(solution)/shard_map/ppermute | solution.py:415
  65.2 5.6 %collective-permute-start.21 = (f32[72,128]{1,0:T(8,128)S(1)}, f32[72,128]{1,0:T(8,128)S(1)}, u32[]{:S(2)}, u32[]{:S(2)}) collective-permute-start(f32[72,128]{1,0:T(8,128)S(1)} %add_add_fusion.own_ref), channel_id=1, source_target_pairs={{0,240},{16,32},{32,16},{48,64},{64,48},{80,96},{96,80},{112,128},... | collective-permute-start | bytes 110600 | tf_op jit(solution)/shard_map/ppermute | solution.py:423
  65.3 5.5 %collective-permute-start.20 = (f32[72,128]{1,0:T(8,128)S(1)}, f32[72,128]{1,0:T(8,128)S(1)}, u32[]{:S(2)}, u32[]{:S(2)}) collective-permute-start(f32[72,128]{1,0:T(8,128)S(1)} %add_add_fusion.own_ref), channel_id=1, source_target_pairs={{0,16},{16,0},{32,48},{48,32},{64,80},{80,64},{96,112},{112,96},{1... | collective-permute-start | bytes 110600 | tf_op jit(solution)/shard_map/ppermute | solution.py:419

commit v5 on v4

--- a/solution.py
+++ b/solution.py
@@ -442,14 +442,15 @@
     part = call(
         band_kernel, (2 * HALF, FREQS), *rows, table["band"]
     )
-    parts = [part] + [swap_y(part, step) for step in (1, 2, 3)]
+    near, far, middle = [swap_y(part, step) for step in (1, 3, 2)]
+    parts = [part, near, middle, far]
     field, image = call(
         aerial_kernel,
         [(COUNT * QUARTER, 2 * SAMPLES), (QUARTER, SAMPLES)],
         *parts, *kernels, table["unfold"], table["flip"], table["out"],
         table["pixels"], flops=4 * 10**9,
     )
-    images = [image] + [swap_z(image, step) for step in (1, 2, 3)]
+    images = [image] + [swap_z(image, step) for step in (1, 3, 2)]
     goal = lax.dynamic_slice_in_dim(target, at_y * QUARTER, QUARTER, 0)
     messages = call(
         slope_kernel,

time: 71.9 us -> 71.6 us (level)
  waiting for transfers between devices: 25.7 us -> 24.7 us
  transfers between devices with their start and end apart: 22 -> 22, of which waited for: 11 -> 10; matrix products, arithmetic and copies ran while one was open for 0% -> 0% of each run, Pallas kernels for 3% -> 3%
where the time goes in v5:
time: 71.6 us; the launch traced here: 70.9 us
  starting transfers between devices  38.6 us (54%)
  waiting for transfers between devices  24.7 us (34%)
  Pallas kernels  6.6 us (9%)
  between operations  0.91 us (1%)
    ppermute x9, starting transfers between devices, swap_z(): return lax.ppermute(value, 'kern', [(i, i ^ step) for i in range(16)])  19.7 us
    ppermute x9, starting transfers between devices, swap_y(): return lax.ppermute(value, 'kern', [(i, i ^ 4 * step) for i in range(16)])  14.1 us
    ppermute x9, waiting for transfers between devices, swap_z(): return lax.ppermute(value, 'kern', [(i, i ^ step) for i in range(16)])  11.9 us
    ppermute x9, waiting for transfers between devices, swap_y(): return lax.ppermute(value, 'kern', [(i, i ^ 4 * step) for i in range(16)])  8.46 us
    pallas_call x8, Pallas kernels, call(): pl.pallas_call(kernel, scratch_shapes=list(scratch), out_shape=out if man...  6.6 us
    ppermute x2, waiting for transfers between devices, swap_outer(): lax.ppermute(value, 'tile', [(i, (i + 1 ^ 1) - 1 & 15) for i in range(16)])  4.34 us
    ppermute x2, starting transfers between devices, swap_outer(): lax.ppermute(value, 'tile', [(i, (i + 1 ^ 1) - 1 & 15) for i in range(16)])  4.31 us
  transfers between devices with their start and end apart: 22, of which 10 were waited for; matrix products, arithmetic and copies ran while one was open for 0% of the time, Pallas kernels for 3%

profile of v5, /device:TPU:64, one launch (start us, length us, event | category | flops | bytes accessed | tf_op | source)
XLA Modules:
  0.0 70.9 jit_solution(11050397589081281048)
XLA Ops:
  0.6 0.0 copy-start
  0.7 0.0 copy-start.12
  0.7 0.1 collective-permute-start.1
  0.8 4.2 %collective-permute-start = (f32[64,256]{1,0:T(8,128)}, f32[64,256]{1,0:T(8,128)S(1)}, u32[]{:S(2)}, u32[]{:S(2)}) collective-permute-start(f32[64,256]{1,0:T(8,128)} %bitcast.4), channel_id=1, source_target_pairs={{0,240},{16,32},{32,16},{48,64},{64,48},{80,96},{96,80},{112,128},... | collective-permute-start | bytes 196616 | tf_op jit(solution)/shard_map/ppermute | solution.py:423
  5.0 0.5 weight_kernel.1.heavy_ref
  5.6 0.0 copy-start.6
  5.6 3.1 %collective-permute-start.6 = (f32[2,2,128,128]{3,2,1,0:T(8,128)S(1)}, f32[2,2,128,128]{3,2,1,0:T(8,128)S(1)}, u32[]{:S(2)}, u32[]{:S(2)}) collective-permute-start(f32[2,2,128,128]{3,2,1,0:T(8,128)S(1)} %copy-done.1), channel_id=1, source_target_pairs={{0,12},{1,13},{2,14},{3,15},{4,8},{5,9},{6,10},{7,11},{8,4},{9,5},... | collective-permute-start | bytes 786440 | tf_op jit(solution)/shard_map/ppermute | solution.py:411
  8.7 0.1 collective-permute-start.5
  8.8 0.3 window_kernel.1.r0
  9.1 0.0 copy-start.9
  9.2 0.0 copy-start.11
  9.2 3.7 %collective-permute-start.4 = (f32[72,128]{1,0:T(8,128)S(1)}, f32[72,128]{1,0:T(8,128)S(1)}, u32[]{:S(2)}, u32[]{:S(2)}) collective-permute-start(f32[72,128]{1,0:T(8,128)S(1)} %window_kernel.1.r0), channel_id=1, source_target_pairs={{0,3},{1,2},{2,1},{3,0},{4,7},{5,6},{6,5},{7,4},{8,11},{9,10},{10,... | collective-permute-start | bytes 110600 | tf_op jit(solution)/shard_map/ppermute | solution.py:415
  12.8 1.0 %collective-permute-start.3 = (f32[72,128]{1,0:T(8,128)S(1)}, f32[72,128]{1,0:T(8,128)S(1)}, u32[]{:S(2)}, u32[]{:S(2)}) collective-permute-start(f32[72,128]{1,0:T(8,128)S(1)} %window_kernel.1.r0), channel_id=1, source_target_pairs={{0,2},{1,3},{2,0},{3,1},{4,6},{5,7},{6,4},{7,5},{8,10},{9,11},{10,... | collective-permute-start | bytes 110600 | tf_op jit(solution)/shard_map/ppermute | solution.py:415
  13.9 1.9 %collective-permute-start.2 = (f32[72,128]{1,0:T(8,128)S(1)}, f32[72,128]{1,0:T(8,128)S(1)}, u32[]{:S(2)}, u32[]{:S(2)}) collective-permute-start(f32[72,128]{1,0:T(8,128)S(1)} %window_kernel.1.r0), channel_id=1, source_target_pairs={{0,1},{1,0},{2,3},{3,2},{4,5},{5,4},{6,7},{7,6},{8,9},{9,8},{10,11... | collective-permute-start | bytes 110600 | tf_op jit(solution)/shard_map/ppermute | solution.py:415
  15.8 1.9 %collective-permute-start.10 = (f32[2,2,128,128]{3,2,1,0:T(8,128)S(1)}, f32[2,2,128,128]{3,2,1,0:T(8,128)S(1)}, u32[]{:S(2)}, u32[]{:S(2)}) collective-permute-start(f32[2,2,128,128]{3,2,1,0:T(8,128)S(1)} %copy-done.1), channel_id=1, source_target_pairs={{0,8},{1,9},{2,10},{3,11},{4,12},{5,13},{6,14},{7,15},{8,0},{9,1},... | collective-permute-start | bytes 786440 | tf_op jit(solution)/shard_map/ppermute | solution.py:411
  17.7 3.2 %collective-permute-done.3.r2 = f32[72,128]{1,0:T(8,128)S(1)} collective-permute-done((f32[72,128]{1,0:T(8,128)S(1)}, f32[72,128]{1,0:T(8,128)S(1)}, u32[]{:S(2)}, u32[]{:S(2)}) %collective-permute-start.3) | collective-permute-done | bytes 36896 | tf_op jit(solution)/shard_map/ppermute | solution.py:415
  20.8 0.3 band_kernel.1.p0
  21.2 3.0 %collective-permute-start.9 = (f32[144,128]{1,0:T(8,128)S(1)}, f32[144,128]{1,0:T(8,128)S(1)}, u32[]{:S(2)}, u32[]{:S(2)}) collective-permute-start(f32[144,128]{1,0:T(8,128)S(1)} %band_kernel.1.p0), channel_id=1, source_target_pairs={{0,12},{1,13},{2,14},{3,15},{4,8},{5,9},{6,10},{7,11},{8,4},{9,5},... | collective-permute-start | bytes 221192 | tf_op jit(solution)/shard_map/ppermute | solution.py:411
  24.1 1.0 %collective-permute-start.8 = (f32[144,128]{1,0:T(8,128)S(1)}, f32[144,128]{1,0:T(8,128)S(1)}, u32[]{:S(2)}, u32[]{:S(2)}) collective-permute-start(f32[144,128]{1,0:T(8,128)S(1)} %band_kernel.1.p0), channel_id=1, source_target_pairs={{0,8},{1,9},{2,10},{3,11},{4,12},{5,13},{6,14},{7,15},{8,0},{9,1},... | collective-permute-start | bytes 221192 | tf_op jit(solution)/shard_map/ppermute | solution.py:411
  25.2 0.1 collective-permute-start.7
  25.3 1.5 %collective-permute-done.9.p3 = f32[144,128]{1,0:T(8,128)S(1)} collective-permute-done((f32[144,128]{1,0:T(8,128)S(1)}, f32[144,128]{1,0:T(8,128)S(1)}, u32[]{:S(2)}, u32[]{:S(2)}) %collective-permute-start.9) | collective-permute-done | bytes 73760 | tf_op jit(solution)/shard_map/ppermute | solution.py:411
  26.8 3.2 %collective-permute-done.8.p2 = f32[144,128]{1,0:T(8,128)S(1)} collective-permute-done((f32[144,128]{1,0:T(8,128)S(1)}, f32[144,128]{1,0:T(8,128)S(1)}, u32[]{:S(2)}, u32[]{:S(2)}) %collective-permute-start.8) | collective-permute-done | bytes 73760 | tf_op jit(solution)/shard_map/ppermute | solution.py:411
  30.0 0.0 copy-start.10
  30.0 0.0 copy-start.13
  30.1 0.0 copy-start.16
  30.1 1.3 %aerial_kernel.1 = (f32[512,512]{1,0:T(8,128)S(1)}, f32[64,256]{1,0:T(8,128)S(1)}) custom-call(f32[144,128]{1,0:T(8,128)S(1)} %band_kernel.1.p0, f32[144,128]{1,0:T(8,128)S(1)} %collective-permute-done.7.p1, f32[144,128]{1,0:T(8,128)S(1)} %collective-permute-done.8.p2, f32[144,128]{1,0:T(8,128)S(1)} %collective-permute-done.9.p3, ...), custom_call_target="tpu_custom_call" | custom-call | flops 4000000000 | bytes 1000000 | tf_op jit(solution)/shard_map/aerial_kernel/pallas_call | solution.py:396
  31.4 2.4 %collective-permute-start.13 = (f32[64,256]{1,0:T(8,128)S(1)}, f32[64,256]{1,0:T(8,128)S(1)}, u32[]{:S(2)}, u32[]{:S(2)}) collective-permute-start(f32[64,256]{1,0:T(8,128)S(1)} %get-tuple-element.28.i0), channel_id=1, source_target_pairs={{0,2},{1,3},{2,0},{3,1},{4,6},{5,7},{6,4},{7,5},{8,10},{9,11},{10,... | collective-permute-start | bytes 196616 | tf_op jit(solution)/shard_map/ppermute | solution.py:415
  33.8 2.2 %collective-permute-start.12 = (f32[64,256]{1,0:T(8,128)S(1)}, f32[64,256]{1,0:T(8,128)S(1)}, u32[]{:S(2)}, u32[]{:S(2)}) collective-permute-start(f32[64,256]{1,0:T(8,128)S(1)} %get-tuple-element.28.i0), channel_id=1, source_target_pairs={{0,3},{1,2},{2,1},{3,0},{4,7},{5,6},{6,5},{7,4},{8,11},{9,10},{10,... | collective-permute-start | bytes 196616 | tf_op jit(solution)/shard_map/ppermute | solution.py:415
  36.0 2.0 %collective-permute-start.11 = (f32[64,256]{1,0:T(8,128)S(1)}, f32[64,256]{1,0:T(8,128)S(1)}, u32[]{:S(2)}, u32[]{:S(2)}) collective-permute-start(f32[64,256]{1,0:T(8,128)S(1)} %get-tuple-element.28.i0), channel_id=1, source_target_pairs={{0,1},{1,0},{2,3},{3,2},{4,5},{5,4},{6,7},{7,6},{8,9},{9,8},{10,11... | collective-permute-start | bytes 196616 | tf_op jit(solution)/shard_map/ppermute | solution.py:415
  38.0 2.7 %collective-permute-done.13.i3 = f32[64,256]{1,0:T(8,128)S(1)} collective-permute-done((f32[64,256]{1,0:T(8,128)S(1)}, f32[64,256]{1,0:T(8,128)S(1)}, u32[]{:S(2)}, u32[]{:S(2)}) %collective-permute-start.13) | collective-permute-done | bytes 65568 | tf_op jit(solution)/shard_map/ppermute | solution.py:415
  40.7 0.8 %collective-permute-done.11.i1 = f32[64,256]{1,0:T(8,128)S(1)} collective-permute-done((f32[64,256]{1,0:T(8,128)S(1)}, f32[64,256]{1,0:T(8,128)S(1)}, u32[]{:S(2)}, u32[]{:S(2)}) %collective-permute-start.11) | collective-permute-done | bytes 65568 | tf_op jit(solution)/shard_map/ppermute | solution.py:415
  41.5 2.1 %slope_kernel.1 = (f32[176,128]{1,0:T(8,128)S(1)}, f32[176,128]{1,0:T(8,128)S(1)}, f32[176,128]{1,0:T(8,128)S(1)}, f32[176,128]{1,0:T(8,128)S(1)}) custom-call(f32[64,256]{1,0:T(8,128)S(1)} %get-tuple-element.28.i0, f32[64,256]{1,0:T(8,128)S(1)} %collective-permute-done.11.i1, f32[64,256]{1,0:T(8,128)S(1)} %collective-permute-done.12.i2, ...), custom_call_target="tpu_custom_call" | custom-call | flops 4000000000 | bytes 1000000 | tf_op jit(solution)/shard_map/slope_kernel/pallas_call | solution.py:396
  43.6 0.6 collective-permute-start.14
  44.2 2.3 %collective-permute-start.15 = (f32[176,128]{1,0:T(8,128)S(1)}, f32[176,128]{1,0:T(8,128)S(1)}, u32[]{:S(2)}, u32[]{:S(2)}) collective-permute-start(f32[176,128]{1,0:T(8,128)S(1)} %get-tuple-element.32), channel_id=1, source_target_pairs={{0,8},{1,9},{2,10},{3,11},{4,12},{5,13},{6,14},{7,15},{8,0},{9,1},... | collective-permute-start | bytes 270344 | tf_op jit(solution)/shard_map/ppermute | solution.py:411
  46.5 2.0 %collective-permute-start.16 = (f32[176,128]{1,0:T(8,128)S(1)}, f32[176,128]{1,0:T(8,128)S(1)}, u32[]{:S(2)}, u32[]{:S(2)}) collective-permute-start(f32[176,128]{1,0:T(8,128)S(1)} %get-tuple-element.33), channel_id=1, source_target_pairs={{0,12},{1,13},{2,14},{3,15},{4,8},{5,9},{6,10},{7,11},{8,4},{9,5},... | collective-permute-start | bytes 270344 | tf_op jit(solution)/shard_map/ppermute | solution.py:411
  48.4 1.8 %collective-permute-done.15.m2 = f32[176,128]{1,0:T(8,128)S(1)} collective-permute-done((f32[176,128]{1,0:T(8,128)S(1)}, f32[176,128]{1,0:T(8,128)S(1)}, u32[]{:S(2)}, u32[]{:S(2)}) %collective-permute-start.15) | collective-permute-done | bytes 90144 | tf_op jit(solution)/shard_map/ppermute | solution.py:411
  50.2 2.0 %collective-permute-done.16.m3 = f32[176,128]{1,0:T(8,128)S(1)} collective-permute-done((f32[176,128]{1,0:T(8,128)S(1)}, f32[176,128]{1,0:T(8,128)S(1)}, u32[]{:S(2)}, u32[]{:S(2)}) %collective-permute-start.16) | collective-permute-done | bytes 90144 | tf_op jit(solution)/shard_map/ppermute | solution.py:411
  52.2 0.3 columns_kernel.1
  52.6 2.1 %collective-permute-start.17 = (f32[72,128]{1,0:T(8,128)S(1)}, f32[72,128]{1,0:T(8,128)S(1)}, u32[]{:S(2)}, u32[]{:S(2)}) collective-permute-start(f32[72,128]{1,0:T(8,128)S(1)} %get-tuple-element.35), channel_id=1, source_target_pairs={{0,1},{1,0},{2,3},{3,2},{4,5},{5,4},{6,7},{7,6},{8,9},{9,8},{10,11... | collective-permute-start | bytes 110600 | tf_op jit(solution)/shard_map/ppermute | solution.py:415
  54.6 3.0 %collective-permute-start.18 = (f32[72,128]{1,0:T(8,128)S(1)}, f32[72,128]{1,0:T(8,128)S(1)}, u32[]{:S(2)}, u32[]{:S(2)}) collective-permute-start(f32[72,128]{1,0:T(8,128)S(1)} %get-tuple-element.36), channel_id=1, source_target_pairs={{0,2},{1,3},{2,0},{3,1},{4,6},{5,7},{6,4},{7,5},{8,10},{9,11},{10,... | collective-permute-start | bytes 110600 | tf_op jit(solution)/shard_map/ppermute | solution.py:415
  57.6 1.5 %collective-permute-start.19 = (f32[72,128]{1,0:T(8,128)S(1)}, f32[72,128]{1,0:T(8,128)S(1)}, u32[]{:S(2)}, u32[]{:S(2)}) collective-permute-start(f32[72,128]{1,0:T(8,128)S(1)} %get-tuple-element.37), channel_id=1, source_target_pairs={{0,3},{1,2},{2,1},{3,0},{4,7},{5,6},{6,5},{7,4},{8,11},{9,10},{10,... | collective-permute-start | bytes 110600 | tf_op jit(solution)/shard_map/ppermute | solution.py:415
  59.1 3.4 %collective-permute-done.18 = f32[72,128]{1,0:T(8,128)S(1)} collective-permute-done((f32[72,128]{1,0:T(8,128)S(1)}, f32[72,128]{1,0:T(8,128)S(1)}, u32[]{:S(2)}, u32[]{:S(2)}) %collective-permute-start.18) | collective-permute-done | bytes 36896 | tf_op jit(solution)/shard_map/ppermute | solution.py:415
  62.5 1.9 %collective-permute-done.19 = f32[72,128]{1,0:T(8,128)S(1)} collective-permute-done((f32[72,128]{1,0:T(8,128)S(1)}, f32[72,128]{1,0:T(8,128)S(1)}, u32[]{:S(2)}, u32[]{:S(2)}) %collective-permute-start.19) | collective-permute-done | bytes 36896 | tf_op jit(solution)/shard_map/ppermute | solution.py:415
  64.4 0.1 collective-permute-start.21
  64.5 0.4 collective-permute-start.20
  64.9 0.8 %resist_kernel.1 = f32[64,256]{1,0:T(8,128)} custom-call(f32[176,128]{1,0:T(8,128)S(1)} %get-tuple-element.30.m0, f32[176,128]{1,0:T(8,128)S(1)} %collective-permute-done.14.m1, f32[176,128]{1,0:T(8,128)S(1)} %collective-permute-done.15.m2, f32[176,128]{1,0:T(8,128)S(1)} %collective-permute-done.16.m3), custom_call_target="tpu_custom_call" | custom-call | flops 4000000000 | bytes 1000000 | tf_op jit(solution)/shard_map/resist_kernel/pallas_call | solution.py:396
  65.7 4.3 %collective-permute-done.21.outer_ref = f32[72,128]{1,0:T(8,128)S(1)} collective-permute-done((f32[72,128]{1,0:T(8,128)S(1)}, f32[72,128]{1,0:T(8,128)S(1)}, u32[]{:S(2)}, u32[]{:S(2)}) %collective-permute-start.21) | collective-permute-done | bytes 36896 | tf_op jit(solution)/shard_map/ppermute | solution.py:423
  70.0 0.9 %final_kernel.1 = f32[64,256]{1,0:T(8,128)} custom-call(f32[72,128]{1,0:T(8,128)S(1)} %collective-permute-done.20.inner_ref, f32[72,128]{1,0:T(8,128)S(1)} %collective-permute-done.21.outer_ref, f32[72,128]{1,0:T(8,128)S(1)} %add_add_fusion.own_ref, bf16[2,144,256]{2,1,0:T(8,128)(2,1)S(1)} %copy-done.12), custom_call_target="tpu_custom_call" | custom-call | flops 4000000000 | bytes 1000000 | tf_op jit(solution)/shard_map/final_kernel/pallas_call | solution.py:396
  (42 shorter events, 0.1 us)
Async XLA Ops:
  0.6 37.3 %copy-start = (s32[256,1024]{1,0:T(8,128)S(1)}, s32[256,1024]{1,0:T(8,128)}, u32[]{:S(2)}) copy-start(s32[256,1024]{1,0:T(8,128)} %param.19) | copy-start | bytes 3145732
  0.6 4.4 %copy-start.3 = (f32[2]{0:T(128)S(1)}, f32[2]{0:T(128)}, u32[]{:S(2)}) copy-start(f32[2]{0:T(128)} %weight_ref.1) | copy-start | bytes 28
  0.7 4.9 %copy-start.1 = (f32[2,2,128,128]{3,2,1,0:T(8,128)S(1)}, f32[2,2,128,128]{3,2,1,0:T(8,128)}, u32[]{:S(2)}) copy-start(f32[2,2,128,128]{3,2,1,0:T(8,128)} %h0.1) | copy-start | bytes 786436
  0.7 8.2 %copy-start.2 = (f32[256,64]{0,1:T(8,128)S(1)}, f32[256,64]{0,1:T(8,128)}, u32[]{:S(2)}) copy-start(f32[256,64]{0,1:T(8,128)} %param.18) | copy-start | bytes 196612
  0.7 8.2 %copy-start.12 = (bf16[2,144,256]{2,1,0:T(8,128)(2,1)S(1)}, bf16[2,144,256]{2,1,0:T(8,128)(2,1)}, u32[]{:S(2)}) copy-start(bf16[2,144,256]{2,1,0:T(8,128)(2,1)} %constant.53.clone.rows_ref) | copy-start | bytes 442372
  0.7 8.1 %collective-permute-start.1 = (f32[64,256]{1,0:T(8,128)}, f32[64,256]{1,0:T(8,128)S(1)}, u32[]{:S(2)}, u32[]{:S(2)}) collective-permute-start(f32[64,256]{1,0:T(8,128)} %bitcast.3), channel_id=1, source_target_pairs={{0,16},{16,0},{32,48},{48,32},{64,80},{80,64},{96,112},{112,96},{1... | collective-permute-start | bytes 196616 | tf_op jit(solution)/shard_map/ppermute | solution.py:419
  0.8 8.0 %collective-permute-start = (f32[64,256]{1,0:T(8,128)}, f32[64,256]{1,0:T(8,128)S(1)}, u32[]{:S(2)}, u32[]{:S(2)}) collective-permute-start(f32[64,256]{1,0:T(8,128)} %bitcast.4), channel_id=1, source_target_pairs={{0,240},{16,32},{32,16},{48,64},{64,48},{80,96},{96,80},{112,128},... | collective-permute-start | bytes 196616 | tf_op jit(solution)/shard_map/ppermute | solution.py:423
  5.6 15.3 %copy-start.6 = (bf16[2,16,64,256]{3,2,1,0:T(8,128)(2,1)S(1)}, bf16[2,16,64,256]{3,2,1,0:T(8,128)(2,1)}, u32[]{:S(2)}) copy-start(bf16[2,16,64,256]{3,2,1,0:T(8,128)(2,1)} %constant.54.clone.band_ref) | copy-start | bytes 3145732
  5.6 15.2 %collective-permute-start.6 = (f32[2,2,128,128]{3,2,1,0:T(8,128)S(1)}, f32[2,2,128,128]{3,2,1,0:T(8,128)S(1)}, u32[]{:S(2)}, u32[]{:S(2)}) collective-permute-start(f32[2,2,128,128]{3,2,1,0:T(8,128)S(1)} %copy-done.1), channel_id=1, source_target_pairs={{0,12},{1,13},{2,14},{3,15},{4,8},{5,9},{6,10},{7,11},{8,4},{9,5},... | collective-permute-start | bytes 786440 | tf_op jit(solution)/shard_map/ppermute | solution.py:411
  8.7 12.1 %collective-permute-start.5 = (f32[2,2,128,128]{3,2,1,0:T(8,128)S(1)}, f32[2,2,128,128]{3,2,1,0:T(8,128)S(1)}, u32[]{:S(2)}, u32[]{:S(2)}) collective-permute-start(f32[2,2,128,128]{3,2,1,0:T(8,128)S(1)} %copy-done.1), channel_id=1, source_target_pairs={{0,4},{1,5},{2,6},{3,7},{4,0},{5,1},{6,2},{7,3},{8,12},{9,13},{10,... | collective-permute-start | bytes 786440 | tf_op jit(solution)/shard_map/ppermute | solution.py:411
  9.1 20.9 %copy-start.9 = (bf16[2,256,512]{2,1,0:T(8,128)(2,1)S(1)}, bf16[2,256,512]{2,1,0:T(8,128)(2,1)}, u32[]{:S(2)}) copy-start(bf16[2,256,512]{2,1,0:T(8,128)(2,1)} %constant.63.clone.pixels_ref) | copy-start | bytes 1572868
  9.2 20.9 %copy-start.11 = (bf16[2,4,128,128]{3,2,1,0:T(8,128)(2,1)S(1)}, bf16[2,4,128,128]{3,2,1,0:T(8,128)(2,1)}, u32[]{:S(2)}) copy-start(bf16[2,4,128,128]{3,2,1,0:T(8,128)(2,1)} %constant.61.clone.out_rows_ref) | copy-start | bytes 786436
  9.2 20.9 %copy-start.14 = (bf16[128,256]{1,0:T(8,128)(2,1)S(1)}, bf16[128,256]{1,0:T(8,128)(2,1)}, u32[]{:S(2)}) copy-start(bf16[128,256]{1,0:T(8,128)(2,1)} %constant.57.clone.unfold_ref) | copy-start | bytes 196612
  9.2 6.6 %collective-permute-start.4 = (f32[72,128]{1,0:T(8,128)S(1)}, f32[72,128]{1,0:T(8,128)S(1)}, u32[]{:S(2)}, u32[]{:S(2)}) collective-permute-start(f32[72,128]{1,0:T(8,128)S(1)} %window_kernel.1.r0), channel_id=1, source_target_pairs={{0,3},{1,2},{2,1},{3,0},{4,7},{5,6},{6,5},{7,4},{8,11},{9,10},{10,... | collective-permute-start | bytes 110600 | tf_op jit(solution)/shard_map/ppermute | solution.py:415
  12.8 8.0 %collective-permute-start.3 = (f32[72,128]{1,0:T(8,128)S(1)}, f32[72,128]{1,0:T(8,128)S(1)}, u32[]{:S(2)}, u32[]{:S(2)}) collective-permute-start(f32[72,128]{1,0:T(8,128)S(1)} %window_kernel.1.r0), channel_id=1, source_target_pairs={{0,2},{1,3},{2,0},{3,1},{4,6},{5,7},{6,4},{7,5},{8,10},{9,11},{10,... | collective-permute-start | bytes 110600 | tf_op jit(solution)/shard_map/ppermute | solution.py:415
  13.9 7.0 %collective-permute-start.2 = (f32[72,128]{1,0:T(8,128)S(1)}, f32[72,128]{1,0:T(8,128)S(1)}, u32[]{:S(2)}, u32[]{:S(2)}) collective-permute-start(f32[72,128]{1,0:T(8,128)S(1)} %window_kernel.1.r0), channel_id=1, source_target_pairs={{0,1},{1,0},{2,3},{3,2},{4,5},{5,4},{6,7},{7,6},{8,9},{9,8},{10,11... | collective-permute-start | bytes 110600 | tf_op jit(solution)/shard_map/ppermute | solution.py:415
  15.8 9.6 %collective-permute-start.10 = (f32[2,2,128,128]{3,2,1,0:T(8,128)S(1)}, f32[2,2,128,128]{3,2,1,0:T(8,128)S(1)}, u32[]{:S(2)}, u32[]{:S(2)}) collective-permute-start(f32[2,2,128,128]{3,2,1,0:T(8,128)S(1)} %copy-done.1), channel_id=1, source_target_pairs={{0,8},{1,9},{2,10},{3,11},{4,12},{5,13},{6,14},{7,15},{8,0},{9,1},... | collective-permute-start | bytes 786440 | tf_op jit(solution)/shard_map/ppermute | solution.py:411
  21.2 5.6 %collective-permute-start.9 = (f32[144,128]{1,0:T(8,128)S(1)}, f32[144,128]{1,0:T(8,128)S(1)}, u32[]{:S(2)}, u32[]{:S(2)}) collective-permute-start(f32[144,128]{1,0:T(8,128)S(1)} %band_kernel.1.p0), channel_id=1, source_target_pairs={{0,12},{1,13},{2,14},{3,15},{4,8},{5,9},{6,10},{7,11},{8,4},{9,5},... | collective-permute-start | bytes 221192 | tf_op jit(solution)/shard_map/ppermute | solution.py:411
  24.1 5.9 %collective-permute-start.8 = (f32[144,128]{1,0:T(8,128)S(1)}, f32[144,128]{1,0:T(8,128)S(1)}, u32[]{:S(2)}, u32[]{:S(2)}) collective-permute-start(f32[144,128]{1,0:T(8,128)S(1)} %band_kernel.1.p0), channel_id=1, source_target_pairs={{0,8},{1,9},{2,10},{3,11},{4,12},{5,13},{6,14},{7,15},{8,0},{9,1},... | collective-permute-start | bytes 221192 | tf_op jit(solution)/shard_map/ppermute | solution.py:411
  25.2 4.8 %collective-permute-start.7 = (f32[144,128]{1,0:T(8,128)S(1)}, f32[144,128]{1,0:T(8,128)S(1)}, u32[]{:S(2)}, u32[]{:S(2)}) collective-permute-start(f32[144,128]{1,0:T(8,128)S(1)} %band_kernel.1.p0), channel_id=1, source_target_pairs={{0,4},{1,5},{2,6},{3,7},{4,0},{5,1},{6,2},{7,3},{8,12},{9,13},{10,... | collective-permute-start | bytes 221192 | tf_op jit(solution)/shard_map/ppermute | solution.py:411
  25.3 4.7 %copy-start.17 = (bf16[64,72]{1,0:T(8,128)(2,1)S(1)}, bf16[64,72]{1,0:T(8,128)(2,1)}, u32[]{:S(2)}) copy-start(bf16[64,72]{1,0:T(8,128)(2,1)} %constant.59.clone.flip_ref) | copy-start | bytes 27652
  25.3 16.1 %copy-start.4 = (bf16[2,1024,256]{2,1,0:T(8,128)(2,1)S(1)}, bf16[2,1024,256]{2,1,0:T(8,128)(2,1)}, u32[]{:S(2)}) copy-start(bf16[2,1024,256]{2,1,0:T(8,128)(2,1)} %constant.66.clone.spread_back_ref) | copy-start | bytes 3145732
  25.3 16.1 %copy-start.5 = (bf16[2,256,1024]{2,1,0:T(8,128)(2,1)S(1)}, bf16[2,256,1024]{2,1,0:T(8,128)(2,1)}, u32[]{:S(2)}) copy-start(bf16[2,256,1024]{2,1,0:T(8,128)(2,1)} %constant.65.clone.spread_ref) | copy-start | bytes 3145732
  30.0 11.4 %copy-start.10 = (bf16[2,4,128,128]{3,2,1,0:T(8,128)(2,1)S(1)}, bf16[2,4,128,128]{3,2,1,0:T(8,128)(2,1)}, u32[]{:S(2)}) copy-start(bf16[2,4,128,128]{3,2,1,0:T(8,128)(2,1)} %constant.62.clone.out_back_ref) | copy-start | bytes 786436
  30.0 11.4 %copy-start.13 = (bf16[256,128]{1,0:T(8,128)(2,1)S(1)}, bf16[256,128]{1,0:T(8,128)(2,1)}, u32[]{:S(2)}) copy-start(bf16[256,128]{1,0:T(8,128)(2,1)} %constant.58.clone.fold_ref) | copy-start | bytes 196612
  30.1 11.4 %copy-start.16 = (bf16[72,64]{1,0:T(8,128)(2,1)S(1)}, bf16[72,64]{1,0:T(8,128)(2,1)}, u32[]{:S(2)}) copy-start(bf16[72,64]{1,0:T(8,128)(2,1)} %constant.60.clone.flip_back_ref) | copy-start | bytes 27652
  31.4 10.1 %copy-start.8 = (bf16[2,512,256]{2,1,0:T(8,128)(2,1)S(1)}, bf16[2,512,256]{2,1,0:T(8,128)(2,1)}, u32[]{:S(2)}) copy-start(bf16[2,512,256]{2,1,0:T(8,128)(2,1)} %constant.64.clone.pixels_back_ref) | copy-start | bytes 1572868
  31.4 9.3 %collective-permute-start.13 = (f32[64,256]{1,0:T(8,128)S(1)}, f32[64,256]{1,0:T(8,128)S(1)}, u32[]{:S(2)}, u32[]{:S(2)}) collective-permute-start(f32[64,256]{1,0:T(8,128)S(1)} %get-tuple-element.28.i0), channel_id=1, source_target_pairs={{0,2},{1,3},{2,0},{3,1},{4,6},{5,7},{6,4},{7,5},{8,10},{9,11},{10,... | collective-permute-start | bytes 196616 | tf_op jit(solution)/shard_map/ppermute | solution.py:415
  33.8 6.9 %collective-permute-start.12 = (f32[64,256]{1,0:T(8,128)S(1)}, f32[64,256]{1,0:T(8,128)S(1)}, u32[]{:S(2)}, u32[]{:S(2)}) collective-permute-start(f32[64,256]{1,0:T(8,128)S(1)} %get-tuple-element.28.i0), channel_id=1, source_target_pairs={{0,3},{1,2},{2,1},{3,0},{4,7},{5,6},{6,5},{7,4},{8,11},{9,10},{10,... | collective-permute-start | bytes 196616 | tf_op jit(solution)/shard_map/ppermute | solution.py:415
  36.0 5.5 %collective-permute-start.11 = (f32[64,256]{1,0:T(8,128)S(1)}, f32[64,256]{1,0:T(8,128)S(1)}, u32[]{:S(2)}, u32[]{:S(2)}) collective-permute-start(f32[64,256]{1,0:T(8,128)S(1)} %get-tuple-element.28.i0), channel_id=1, source_target_pairs={{0,1},{1,0},{2,3},{3,2},{4,5},{5,4},{6,7},{7,6},{8,9},{9,8},{10,11... | collective-permute-start | bytes 196616 | tf_op jit(solution)/shard_map/ppermute | solution.py:415
  41.5 10.7 %copy-start.7 = (bf16[2,128,1024]{2,1,0:T(8,128)(2,1)S(1)}, bf16[2,128,1024]{2,1,0:T(8,128)(2,1)}, u32[]{:S(2)}) copy-start(bf16[2,128,1024]{2,1,0:T(8,128)(2,1)} %constant.55.clone.band_back_ref) | copy-start | bytes 1572868
  41.5 10.7 %copy-start.15 = (f32[8,1024]{1,0:T(8,128)S(1)}, f32[8,1024]{1,0:T(8,128)}, u32[]{:S(2)}) copy-start(f32[8,1024]{1,0:T(8,128)} %constant.56.clone.edge_ref) | copy-start | bytes 98308
  43.6 4.8 %collective-permute-start.14 = (f32[176,128]{1,0:T(8,128)S(1)}, f32[176,128]{1,0:T(8,128)S(1)}, u32[]{:S(2)}, u32[]{:S(2)}) collective-permute-start(f32[176,128]{1,0:T(8,128)S(1)} %get-tuple-element.31), channel_id=1, source_target_pairs={{0,4},{1,5},{2,6},{3,7},{4,0},{5,1},{6,2},{7,3},{8,12},{9,13},{10,... | collective-permute-start | bytes 270344 | tf_op jit(solution)/shard_map/ppermute | solution.py:411
  44.2 6.0 %collective-permute-start.15 = (f32[176,128]{1,0:T(8,128)S(1)}, f32[176,128]{1,0:T(8,128)S(1)}, u32[]{:S(2)}, u32[]{:S(2)}) collective-permute-start(f32[176,128]{1,0:T(8,128)S(1)} %get-tuple-element.32), channel_id=1, source_target_pairs={{0,8},{1,9},{2,10},{3,11},{4,12},{5,13},{6,14},{7,15},{8,0},{9,1},... | collective-permute-start | bytes 270344 | tf_op jit(solution)/shard_map/ppermute | solution.py:411
  46.5 5.7 %collective-permute-start.16 = (f32[176,128]{1,0:T(8,128)S(1)}, f32[176,128]{1,0:T(8,128)S(1)}, u32[]{:S(2)}, u32[]{:S(2)}) collective-permute-start(f32[176,128]{1,0:T(8,128)S(1)} %get-tuple-element.33), channel_id=1, source_target_pairs={{0,12},{1,13},{2,14},{3,15},{4,8},{5,9},{6,10},{7,11},{8,4},{9,5},... | collective-permute-start | bytes 270344 | tf_op jit(solution)/shard_map/ppermute | solution.py:411
  52.6 6.6 %collective-permute-start.17 = (f32[72,128]{1,0:T(8,128)S(1)}, f32[72,128]{1,0:T(8,128)S(1)}, u32[]{:S(2)}, u32[]{:S(2)}) collective-permute-start(f32[72,128]{1,0:T(8,128)S(1)} %get-tuple-element.35), channel_id=1, source_target_pairs={{0,1},{1,0},{2,3},{3,2},{4,5},{5,4},{6,7},{7,6},{8,9},{9,8},{10,11... | collective-permute-start | bytes 110600 | tf_op jit(solution)/shard_map/ppermute | solution.py:415
  54.6 7.9 %collective-permute-start.18 = (f32[72,128]{1,0:T(8,128)S(1)}, f32[72,128]{1,0:T(8,128)S(1)}, u32[]{:S(2)}, u32[]{:S(2)}) collective-permute-start(f32[72,128]{1,0:T(8,128)S(1)} %get-tuple-element.36), channel_id=1, source_target_pairs={{0,2},{1,3},{2,0},{3,1},{4,6},{5,7},{6,4},{7,5},{8,10},{9,11},{10,... | collective-permute-start | bytes 110600 | tf_op jit(solution)/shard_map/ppermute | solution.py:415
  57.6 6.8 %collective-permute-start.19 = (f32[72,128]{1,0:T(8,128)S(1)}, f32[72,128]{1,0:T(8,128)S(1)}, u32[]{:S(2)}, u32[]{:S(2)}) collective-permute-start(f32[72,128]{1,0:T(8,128)S(1)} %get-tuple-element.37), channel_id=1, source_target_pairs={{0,3},{1,2},{2,1},{3,0},{4,7},{5,6},{6,5},{7,4},{8,11},{9,10},{10,... | collective-permute-start | bytes 110600 | tf_op jit(solution)/shard_map/ppermute | solution.py:415
  64.4 5.6 %collective-permute-start.21 = (f32[72,128]{1,0:T(8,128)S(1)}, f32[72,128]{1,0:T(8,128)S(1)}, u32[]{:S(2)}, u32[]{:S(2)}) collective-permute-start(f32[72,128]{1,0:T(8,128)S(1)} %add_add_fusion.own_ref), channel_id=1, source_target_pairs={{0,240},{16,32},{32,16},{48,64},{64,48},{80,96},{96,80},{112,128},... | collective-permute-start | bytes 110600 | tf_op jit(solution)/shard_map/ppermute | solution.py:423
  64.5 5.5 %collective-permute-start.20 = (f32[72,128]{1,0:T(8,128)S(1)}, f32[72,128]{1,0:T(8,128)S(1)}, u32[]{:S(2)}, u32[]{:S(2)}) collective-permute-start(f32[72,128]{1,0:T(8,128)S(1)} %add_add_fusion.own_ref), channel_id=1, source_target_pairs={{0,16},{16,0},{32,48},{48,32},{64,80},{80,64},{96,112},{112,96},{1... | collective-permute-start | bytes 110600 | tf_op jit(solution)/shard_map/ppermute | solution.py:419

commit v6 on v5

--- a/solution.py
+++ b/solution.py
@@ -19,6 +19,7 @@
 QUARTER = 64
 COUNT = 8
 HALF = 72
+ROOM = 80
 EDGE_ROW = 65
 WEIGHT_ROW = 67
 EXTRA = 32
@@ -40,14 +41,20 @@
     return np.stack([high, low])
 
 
+def split_table3(value):
+    pair = split_table(value)
+    rest = value - pair.astype(np.float64).sum(0)
+    return np.concatenate([pair, rest.astype(ml_dtypes.bfloat16)[None]])
+
+
 def tables():
     freq = np.arange(FREQS) - FREQS // 2
     scale = 1.0 / math.sqrt(WINDOW * COLS)
     win = angles(np.arange(FREQS // 2 + 1), HALO + np.arange(TILE), WINDOW)
-    rows = np.zeros((2, HALF, TILE))
+    rows = np.zeros((2, ROOM, TILE))
     rows[0, : FREQS // 2 + 1] = np.cos(win) * scale
     rows[1, : FREQS // 2 + 1] = np.sin(win) * scale
-    rows = rows.reshape(2 * HALF, TILE)
+    rows = rows.reshape(2 * ROOM, TILE)
     col = angles(np.arange(COLS), freq, COLS)
     keep = FREQS // 2
     band = np.concatenate([np.cos(col[:, keep:]), np.sin(col[:, keep:])], 1)
@@ -89,7 +96,7 @@
         "out_back": split_table(out_rows.transpose(0, 2, 1)),
         "pixels": split_table(pixels),
         "pixels_back": split_table(pixels.T),
-        "spread": split_table(spread),
+        "spread": split_table3(spread),
         "spread_back": split_table(spread.T),
     }
 
@@ -123,6 +130,16 @@
     return dot(twice, jnp.concatenate(latter, 0)) + dot(former[1], latter[0])
 
 
+def dot6(former, latter):
+    high, mid = split(former)
+    low = ((former - high.astype(F32)) - mid.astype(F32)).astype(BF16)
+    count = former.shape[0]
+    most = dot(jnp.concatenate([high, mid, low], 0), latter[0])
+    some = dot(jnp.concatenate([high, mid], 0), latter[1])
+    small = dot(high, latter[2]) + some[count:] + most[2 * count :]
+    return small + some[:count] + most[count : 2 * count] + most[:count]
+
+
 def pair(ref):
     return ref[0], ref[1]
 
@@ -138,7 +155,7 @@
 
 
 def pair_up(value):
-    return jnp.concatenate([value[:HALF], value[HALF:]], 1)
+    return jnp.concatenate([value[:HALF], value[ROOM : ROOM + HALF]], 1)
 
 
 def alternate(shape):
@@ -271,7 +288,7 @@
     kern = lax.axis_index("kern")
     at_y, at_z = kern // 4, kern % 4
     image = (i0[...] + i1[...]) + (i2[...] + i3[...])
-    image = dot3(split(image), pair(spread_ref))
+    image = dot6(image, spread_ref)
     resist = 1.0 / (1.0 + jnp.exp(-STEEPNESS * (image - THRESHOLD)))
     goal = goal_ref[...].astype(F32)
     slope = 2.0 * STEEPNESS * (resist - goal) * resist * (1.0 - resist)
@@ -376,13 +393,13 @@
         own + below * sign,
     )
     for slot, side in enumerate(sides):
-        side = split(side.T)
+        side = split(jnp.concatenate([side, jnp.zeros((ROOM - HALF, 2 * SHARD), F32)], 0).T)
         cols = slice(slot * HALO, (slot + 1) * HALO)
         total = None
         for half in range(2):
             part = dot3(
                 (side[0][half * SHARD : (half + 1) * SHARD], side[1][half * SHARD : (half + 1) * SHARD]),
-                tuple(rows_ref[i, half * HALF : (half + 1) * HALF, cols] for i in range(2)),
+                tuple(rows_ref[i, half * ROOM : (half + 1) * ROOM, cols] for i in range(2)),
             )
             total = part if total is None else total + part
         out_ref[:, cols] = total

time: 71.6 us -> 71.6 us (level)
  transfers between devices with their start and end apart: 22 -> 22, of which waited for: 10 -> 11; matrix products, arithmetic and copies ran while one was open for 0% -> 0% of each run, Pallas kernels for 3% -> 3%
where the time goes in v6:
time: 71.6 us; the launch traced here: 70.7 us
  starting transfers between devices  38.2 us (53%)
  waiting for transfers between devices  24.3 us (34%)
  Pallas kernels  6.66 us (9%)
  between operations  0.88 us (1%)
  local copies, waits for them, and re-layouts  0.77 us (1%)
    ppermute x9, starting transfers between devices, swap_z(): return lax.ppermute(value, 'kern', [(i, i ^ step) for i in range(16)])  19.7 us
    ppermute x9, starting transfers between devices, swap_y(): return lax.ppermute(value, 'kern', [(i, i ^ 4 * step) for i in range(16)])  13.7 us
    ppermute x9, waiting for transfers between devices, swap_z(): return lax.ppermute(value, 'kern', [(i, i ^ step) for i in range(16)])  11.8 us
    ppermute x9, waiting for transfers between devices, swap_y(): return lax.ppermute(value, 'kern', [(i, i ^ 4 * step) for i in range(16)])  8.1 us
    pallas_call x8, Pallas kernels, call(): pl.pallas_call(kernel, scratch_shapes=list(scratch), out_shape=out if man...  6.66 us
    ppermute x2, starting transfers between devices, swap_outer(): lax.ppermute(value, 'tile', [(i, (i + 1 ^ 1) - 1 & 15) for i in range(16)])  4.43 us
    ppermute x2, waiting for transfers between devices, swap_outer(): lax.ppermute(value, 'tile', [(i, (i + 1 ^ 1) - 1 & 15) for i in range(16)])  4.41 us
  transfers between devices with their start and end apart: 22, of which 11 were waited for; matrix products, arithmetic and copies ran while one was open for 0% of the time, Pallas kernels for 3%

profile of v6, /device:TPU:64, one launch (start us, length us, event | category | flops | bytes accessed | tf_op | source)
XLA Modules:
  0.0 70.7 jit_solution(13162355392026783526)
XLA Ops:
  0.6 0.0 copy-start
  0.7 0.1 collective-permute-start.1
  0.8 4.2 %collective-permute-start = (f32[64,256]{1,0:T(8,128)}, f32[64,256]{1,0:T(8,128)S(1)}, u32[]{:S(2)}, u32[]{:S(2)}) collective-permute-start(f32[64,256]{1,0:T(8,128)} %bitcast.4), channel_id=1, source_target_pairs={{0,240},{16,32},{32,16},{48,64},{64,48},{80,96},{96,80},{112,128},... | collective-permute-start | bytes 196616 | tf_op jit(solution)/shard_map/ppermute | solution.py:440
  5.0 0.7 copy-done.3
  5.6 0.5 weight_kernel.1.heavy_ref
  6.2 0.0 copy-start.6
  6.2 3.1 %collective-permute-start.6 = (f32[2,2,128,128]{3,2,1,0:T(8,128)S(1)}, f32[2,2,128,128]{3,2,1,0:T(8,128)S(1)}, u32[]{:S(2)}, u32[]{:S(2)}) collective-permute-start(f32[2,2,128,128]{3,2,1,0:T(8,128)S(1)} %copy-done.1), channel_id=1, source_target_pairs={{0,12},{1,13},{2,14},{3,15},{4,8},{5,9},{6,10},{7,11},{8,4},{9,5},... | collective-permute-start | bytes 786440 | tf_op jit(solution)/shard_map/ppermute | solution.py:428
  9.3 0.1 collective-permute-start.5
  9.5 0.3 window_kernel.1.r0
  9.8 0.0 copy-start.9
  9.8 0.0 copy-start.11
  9.8 0.0 copy-start.17
  9.8 3.7 %collective-permute-start.4 = (f32[72,128]{1,0:T(8,128)S(1)}, f32[72,128]{1,0:T(8,128)S(1)}, u32[]{:S(2)}, u32[]{:S(2)}) collective-permute-start(f32[72,128]{1,0:T(8,128)S(1)} %window_kernel.1.r0), channel_id=1, source_target_pairs={{0,3},{1,2},{2,1},{3,0},{4,7},{5,6},{6,5},{7,4},{8,11},{9,10},{10,... | collective-permute-start | bytes 110600 | tf_op jit(solution)/shard_map/ppermute | solution.py:432
  13.5 1.0 %collective-permute-start.3 = (f32[72,128]{1,0:T(8,128)S(1)}, f32[72,128]{1,0:T(8,128)S(1)}, u32[]{:S(2)}, u32[]{:S(2)}) collective-permute-start(f32[72,128]{1,0:T(8,128)S(1)} %window_kernel.1.r0), channel_id=1, source_target_pairs={{0,2},{1,3},{2,0},{3,1},{4,6},{5,7},{6,4},{7,5},{8,10},{9,11},{10,... | collective-permute-start | bytes 110600 | tf_op jit(solution)/shard_map/ppermute | solution.py:432
  14.5 1.9 %collective-permute-start.2 = (f32[72,128]{1,0:T(8,128)S(1)}, f32[72,128]{1,0:T(8,128)S(1)}, u32[]{:S(2)}, u32[]{:S(2)}) collective-permute-start(f32[72,128]{1,0:T(8,128)S(1)} %window_kernel.1.r0), channel_id=1, source_target_pairs={{0,1},{1,0},{2,3},{3,2},{4,5},{5,4},{6,7},{7,6},{8,9},{9,8},{10,11... | collective-permute-start | bytes 110600 | tf_op jit(solution)/shard_map/ppermute | solution.py:432
  16.4 1.5 %collective-permute-start.10 = (f32[2,2,128,128]{3,2,1,0:T(8,128)S(1)}, f32[2,2,128,128]{3,2,1,0:T(8,128)S(1)}, u32[]{:S(2)}, u32[]{:S(2)}) collective-permute-start(f32[2,2,128,128]{3,2,1,0:T(8,128)S(1)} %copy-done.1), channel_id=1, source_target_pairs={{0,8},{1,9},{2,10},{3,11},{4,12},{5,13},{6,14},{7,15},{8,0},{9,1},... | collective-permute-start | bytes 786440 | tf_op jit(solution)/shard_map/ppermute | solution.py:428
  18.0 3.5 %collective-permute-done.3.r2 = f32[72,128]{1,0:T(8,128)S(1)} collective-permute-done((f32[72,128]{1,0:T(8,128)S(1)}, f32[72,128]{1,0:T(8,128)S(1)}, u32[]{:S(2)}, u32[]{:S(2)}) %collective-permute-start.3) | collective-permute-done | bytes 36896 | tf_op jit(solution)/shard_map/ppermute | solution.py:432
  21.5 0.3 band_kernel.1.p0
  21.8 2.3 %collective-permute-start.9 = (f32[144,128]{1,0:T(8,128)S(1)}, f32[144,128]{1,0:T(8,128)S(1)}, u32[]{:S(2)}, u32[]{:S(2)}) collective-permute-start(f32[144,128]{1,0:T(8,128)S(1)} %band_kernel.1.p0), channel_id=1, source_target_pairs={{0,12},{1,13},{2,14},{3,15},{4,8},{5,9},{6,10},{7,11},{8,4},{9,5},... | collective-permute-start | bytes 221192 | tf_op jit(solution)/shard_map/ppermute | solution.py:428
  24.1 1.7 %collective-permute-start.8 = (f32[144,128]{1,0:T(8,128)S(1)}, f32[144,128]{1,0:T(8,128)S(1)}, u32[]{:S(2)}, u32[]{:S(2)}) collective-permute-start(f32[144,128]{1,0:T(8,128)S(1)} %band_kernel.1.p0), channel_id=1, source_target_pairs={{0,8},{1,9},{2,10},{3,11},{4,12},{5,13},{6,14},{7,15},{8,0},{9,1},... | collective-permute-start | bytes 221192 | tf_op jit(solution)/shard_map/ppermute | solution.py:428
  25.8 0.1 collective-permute-start.7
  26.0 0.0 copy-start.16
  26.0 1.4 %collective-permute-done.9.p3 = f32[144,128]{1,0:T(8,128)S(1)} collective-permute-done((f32[144,128]{1,0:T(8,128)S(1)}, f32[144,128]{1,0:T(8,128)S(1)}, u32[]{:S(2)}, u32[]{:S(2)}) %collective-permute-start.9) | collective-permute-done | bytes 73760 | tf_op jit(solution)/shard_map/ppermute | solution.py:428
  27.4 2.6 %collective-permute-done.8.p2 = f32[144,128]{1,0:T(8,128)S(1)} collective-permute-done((f32[144,128]{1,0:T(8,128)S(1)}, f32[144,128]{1,0:T(8,128)S(1)}, u32[]{:S(2)}, u32[]{:S(2)}) %collective-permute-start.8) | collective-permute-done | bytes 73760 | tf_op jit(solution)/shard_map/ppermute | solution.py:428
  30.0 0.2 collective-permute-done.7.p1
  30.2 1.3 %aerial_kernel.1 = (f32[512,512]{1,0:T(8,128)S(1)}, f32[64,256]{1,0:T(8,128)S(1)}) custom-call(f32[144,128]{1,0:T(8,128)S(1)} %band_kernel.1.p0, f32[144,128]{1,0:T(8,128)S(1)} %collective-permute-done.7.p1, f32[144,128]{1,0:T(8,128)S(1)} %collective-permute-done.8.p2, f32[144,128]{1,0:T(8,128)S(1)} %collective-permute-done.9.p3, ...), custom_call_target="tpu_custom_call" | custom-call | flops 4000000000 | bytes 1000000 | tf_op jit(solution)/shard_map/aerial_kernel/pallas_call | solution.py:413
  31.5 2.9 %collective-permute-start.13 = (f32[64,256]{1,0:T(8,128)S(1)}, f32[64,256]{1,0:T(8,128)S(1)}, u32[]{:S(2)}, u32[]{:S(2)}) collective-permute-start(f32[64,256]{1,0:T(8,128)S(1)} %get-tuple-element.28.i0), channel_id=1, source_target_pairs={{0,2},{1,3},{2,0},{3,1},{4,6},{5,7},{6,4},{7,5},{8,10},{9,11},{10,... | collective-permute-start | bytes 196616 | tf_op jit(solution)/shard_map/ppermute | solution.py:432
  34.4 2.2 %collective-permute-start.12 = (f32[64,256]{1,0:T(8,128)S(1)}, f32[64,256]{1,0:T(8,128)S(1)}, u32[]{:S(2)}, u32[]{:S(2)}) collective-permute-start(f32[64,256]{1,0:T(8,128)S(1)} %get-tuple-element.28.i0), channel_id=1, source_target_pairs={{0,3},{1,2},{2,1},{3,0},{4,7},{5,6},{6,5},{7,4},{8,11},{9,10},{10,... | collective-permute-start | bytes 196616 | tf_op jit(solution)/shard_map/ppermute | solution.py:432
  36.6 1.5 %collective-permute-start.11 = (f32[64,256]{1,0:T(8,128)S(1)}, f32[64,256]{1,0:T(8,128)S(1)}, u32[]{:S(2)}, u32[]{:S(2)}) collective-permute-start(f32[64,256]{1,0:T(8,128)S(1)} %get-tuple-element.28.i0), channel_id=1, source_target_pairs={{0,1},{1,0},{2,3},{3,2},{4,5},{5,4},{6,7},{7,6},{8,9},{9,8},{10,11... | collective-permute-start | bytes 196616 | tf_op jit(solution)/shard_map/ppermute | solution.py:432
  38.1 3.7 %collective-permute-done.13.i3 = f32[64,256]{1,0:T(8,128)S(1)} collective-permute-done((f32[64,256]{1,0:T(8,128)S(1)}, f32[64,256]{1,0:T(8,128)S(1)}, u32[]{:S(2)}, u32[]{:S(2)}) %collective-permute-start.13) | collective-permute-done | bytes 65568 | tf_op jit(solution)/shard_map/ppermute | solution.py:432
  41.8 0.3 collective-permute-done.11.i1
  42.2 2.2 %slope_kernel.1 = (f32[176,128]{1,0:T(8,128)S(1)}, f32[176,128]{1,0:T(8,128)S(1)}, f32[176,128]{1,0:T(8,128)S(1)}, f32[176,128]{1,0:T(8,128)S(1)}) custom-call(f32[64,256]{1,0:T(8,128)S(1)} %get-tuple-element.28.i0, f32[64,256]{1,0:T(8,128)S(1)} %collective-permute-done.11.i1, f32[64,256]{1,0:T(8,128)S(1)} %collective-permute-done.12.i2, ...), custom_call_target="tpu_custom_call" | custom-call | flops 4000000000 | bytes 1000000 | tf_op jit(solution)/shard_map/slope_kernel/pallas_call | solution.py:413
  44.3 0.6 collective-permute-start.14
  45.0 2.4 %collective-permute-start.15 = (f32[176,128]{1,0:T(8,128)S(1)}, f32[176,128]{1,0:T(8,128)S(1)}, u32[]{:S(2)}, u32[]{:S(2)}) collective-permute-start(f32[176,128]{1,0:T(8,128)S(1)} %get-tuple-element.32), channel_id=1, source_target_pairs={{0,8},{1,9},{2,10},{3,11},{4,12},{5,13},{6,14},{7,15},{8,0},{9,1},... | collective-permute-start | bytes 270344 | tf_op jit(solution)/shard_map/ppermute | solution.py:428
  47.3 1.8 %collective-permute-start.16 = (f32[176,128]{1,0:T(8,128)S(1)}, f32[176,128]{1,0:T(8,128)S(1)}, u32[]{:S(2)}, u32[]{:S(2)}) collective-permute-start(f32[176,128]{1,0:T(8,128)S(1)} %get-tuple-element.33), channel_id=1, source_target_pairs={{0,12},{1,13},{2,14},{3,15},{4,8},{5,9},{6,10},{7,11},{8,4},{9,5},... | collective-permute-start | bytes 270344 | tf_op jit(solution)/shard_map/ppermute | solution.py:428
  49.1 1.9 %collective-permute-done.15.m2 = f32[176,128]{1,0:T(8,128)S(1)} collective-permute-done((f32[176,128]{1,0:T(8,128)S(1)}, f32[176,128]{1,0:T(8,128)S(1)}, u32[]{:S(2)}, u32[]{:S(2)}) %collective-permute-start.15) | collective-permute-done | bytes 90144 | tf_op jit(solution)/shard_map/ppermute | solution.py:428
  51.0 2.1 %collective-permute-done.16.m3 = f32[176,128]{1,0:T(8,128)S(1)} collective-permute-done((f32[176,128]{1,0:T(8,128)S(1)}, f32[176,128]{1,0:T(8,128)S(1)}, u32[]{:S(2)}, u32[]{:S(2)}) %collective-permute-start.16) | collective-permute-done | bytes 90144 | tf_op jit(solution)/shard_map/ppermute | solution.py:428
  53.1 0.3 columns_kernel.1
  53.4 1.1 %collective-permute-start.17 = (f32[72,128]{1,0:T(8,128)S(1)}, f32[72,128]{1,0:T(8,128)S(1)}, u32[]{:S(2)}, u32[]{:S(2)}) collective-permute-start(f32[72,128]{1,0:T(8,128)S(1)} %get-tuple-element.35), channel_id=1, source_target_pairs={{0,1},{1,0},{2,3},{3,2},{4,5},{5,4},{6,7},{7,6},{8,9},{9,8},{10,11... | collective-permute-start | bytes 110600 | tf_op jit(solution)/shard_map/ppermute | solution.py:432
  54.5 3.5 %collective-permute-start.18 = (f32[72,128]{1,0:T(8,128)S(1)}, f32[72,128]{1,0:T(8,128)S(1)}, u32[]{:S(2)}, u32[]{:S(2)}) collective-permute-start(f32[72,128]{1,0:T(8,128)S(1)} %get-tuple-element.36), channel_id=1, source_target_pairs={{0,2},{1,3},{2,0},{3,1},{4,6},{5,7},{6,4},{7,5},{8,10},{9,11},{10,... | collective-permute-start | bytes 110600 | tf_op jit(solution)/shard_map/ppermute | solution.py:432
  58.0 2.0 %collective-permute-start.19 = (f32[72,128]{1,0:T(8,128)S(1)}, f32[72,128]{1,0:T(8,128)S(1)}, u32[]{:S(2)}, u32[]{:S(2)}) collective-permute-start(f32[72,128]{1,0:T(8,128)S(1)} %get-tuple-element.37), channel_id=1, source_target_pairs={{0,3},{1,2},{2,1},{3,0},{4,7},{5,6},{6,5},{7,4},{8,11},{9,10},{10,... | collective-permute-start | bytes 110600 | tf_op jit(solution)/shard_map/ppermute | solution.py:432
  60.0 2.3 %collective-permute-done.18 = f32[72,128]{1,0:T(8,128)S(1)} collective-permute-done((f32[72,128]{1,0:T(8,128)S(1)}, f32[72,128]{1,0:T(8,128)S(1)}, u32[]{:S(2)}, u32[]{:S(2)}) %collective-permute-start.18) | collective-permute-done | bytes 36896 | tf_op jit(solution)/shard_map/ppermute | solution.py:432
  62.3 1.9 %collective-permute-done.19 = f32[72,128]{1,0:T(8,128)S(1)} collective-permute-done((f32[72,128]{1,0:T(8,128)S(1)}, f32[72,128]{1,0:T(8,128)S(1)}, u32[]{:S(2)}, u32[]{:S(2)}) %collective-permute-start.19) | collective-permute-done | bytes 36896 | tf_op jit(solution)/shard_map/ppermute | solution.py:432
  64.3 0.2 collective-permute-start.21
  64.5 0.2 collective-permute-start.20
  64.6 0.8 %resist_kernel.1 = f32[64,256]{1,0:T(8,128)} custom-call(f32[176,128]{1,0:T(8,128)S(1)} %get-tuple-element.30.m0, f32[176,128]{1,0:T(8,128)S(1)} %collective-permute-done.14.m1, f32[176,128]{1,0:T(8,128)S(1)} %collective-permute-done.15.m2, f32[176,128]{1,0:T(8,128)S(1)} %collective-permute-done.16.m3), custom_call_target="tpu_custom_call" | custom-call | flops 4000000000 | bytes 1000000 | tf_op jit(solution)/shard_map/resist_kernel/pallas_call | solution.py:413
  65.4 4.4 %collective-permute-done.21.outer_ref = f32[72,128]{1,0:T(8,128)S(1)} collective-permute-done((f32[72,128]{1,0:T(8,128)S(1)}, f32[72,128]{1,0:T(8,128)S(1)}, u32[]{:S(2)}, u32[]{:S(2)}) %collective-permute-start.21) | collective-permute-done | bytes 36896 | tf_op jit(solution)/shard_map/ppermute | solution.py:440
  69.8 0.9 %final_kernel.1 = f32[64,256]{1,0:T(8,128)} custom-call(f32[72,128]{1,0:T(8,128)S(1)} %collective-permute-done.20.inner_ref, f32[72,128]{1,0:T(8,128)S(1)} %collective-permute-done.21.outer_ref, f32[72,128]{1,0:T(8,128)S(1)} %add_add_fusion.own_ref, bf16[2,160,256]{2,1,0:T(8,128)(2,1)S(1)} %copy-done.12), custom_call_target="tpu_custom_call" | custom-call | flops 4000000000 | bytes 1000000 | tf_op jit(solution)/shard_map/final_kernel/pallas_call | solution.py:413
  (42 shorter events, 0.1 us)
Async XLA Ops:
  0.6 37.5 %copy-start = (s32[256,1024]{1,0:T(8,128)S(1)}, s32[256,1024]{1,0:T(8,128)}, u32[]{:S(2)}) copy-start(s32[256,1024]{1,0:T(8,128)} %param.19) | copy-start | bytes 3145732
  0.6 5.5 %copy-start.1 = (f32[2,2,128,128]{3,2,1,0:T(8,128)S(1)}, f32[2,2,128,128]{3,2,1,0:T(8,128)}, u32[]{:S(2)}) copy-start(f32[2,2,128,128]{3,2,1,0:T(8,128)} %h0.1) | copy-start | bytes 786436
  0.7 8.8 %copy-start.2 = (f32[256,64]{0,1:T(8,128)S(1)}, f32[256,64]{0,1:T(8,128)}, u32[]{:S(2)}) copy-start(f32[256,64]{0,1:T(8,128)} %param.18) | copy-start | bytes 196612
  0.7 8.8 %collective-permute-start.1 = (f32[64,256]{1,0:T(8,128)}, f32[64,256]{1,0:T(8,128)S(1)}, u32[]{:S(2)}, u32[]{:S(2)}) collective-permute-start(f32[64,256]{1,0:T(8,128)} %bitcast.3), channel_id=1, source_target_pairs={{0,16},{16,0},{32,48},{48,32},{64,80},{80,64},{96,112},{112,96},{1... | collective-permute-start | bytes 196616 | tf_op jit(solution)/shard_map/ppermute | solution.py:436
  0.8 8.7 %collective-permute-start = (f32[64,256]{1,0:T(8,128)}, f32[64,256]{1,0:T(8,128)S(1)}, u32[]{:S(2)}, u32[]{:S(2)}) collective-permute-start(f32[64,256]{1,0:T(8,128)} %bitcast.4), channel_id=1, source_target_pairs={{0,240},{16,32},{32,16},{48,64},{64,48},{80,96},{96,80},{112,128},... | collective-permute-start | bytes 196616 | tf_op jit(solution)/shard_map/ppermute | solution.py:440
  5.0 0.7 copy-start.3
  5.6 3.8 %copy-start.12 = (bf16[2,160,256]{2,1,0:T(8,128)(2,1)S(1)}, bf16[2,160,256]{2,1,0:T(8,128)(2,1)}, u32[]{:S(2)}) copy-start(bf16[2,160,256]{2,1,0:T(8,128)(2,1)} %constant.53.clone.rows_ref) | copy-start | bytes 491524
  6.2 15.3 %copy-start.6 = (bf16[2,16,64,256]{3,2,1,0:T(8,128)(2,1)S(1)}, bf16[2,16,64,256]{3,2,1,0:T(8,128)(2,1)}, u32[]{:S(2)}) copy-start(bf16[2,16,64,256]{3,2,1,0:T(8,128)(2,1)} %constant.54.clone.band_ref) | copy-start | bytes 3145732
  6.2 15.3 %collective-permute-start.6 = (f32[2,2,128,128]{3,2,1,0:T(8,128)S(1)}, f32[2,2,128,128]{3,2,1,0:T(8,128)S(1)}, u32[]{:S(2)}, u32[]{:S(2)}) collective-permute-start(f32[2,2,128,128]{3,2,1,0:T(8,128)S(1)} %copy-done.1), channel_id=1, source_target_pairs={{0,12},{1,13},{2,14},{3,15},{4,8},{5,9},{6,10},{7,11},{8,4},{9,5},... | collective-permute-start | bytes 786440 | tf_op jit(solution)/shard_map/ppermute | solution.py:428
  9.3 12.2 %collective-permute-start.5 = (f32[2,2,128,128]{3,2,1,0:T(8,128)S(1)}, f32[2,2,128,128]{3,2,1,0:T(8,128)S(1)}, u32[]{:S(2)}, u32[]{:S(2)}) collective-permute-start(f32[2,2,128,128]{3,2,1,0:T(8,128)S(1)} %copy-done.1), channel_id=1, source_target_pairs={{0,4},{1,5},{2,6},{3,7},{4,0},{5,1},{6,2},{7,3},{8,12},{9,13},{10,... | collective-permute-start | bytes 786440 | tf_op jit(solution)/shard_map/ppermute | solution.py:428
  9.8 20.4 %copy-start.9 = (bf16[2,256,512]{2,1,0:T(8,128)(2,1)S(1)}, bf16[2,256,512]{2,1,0:T(8,128)(2,1)}, u32[]{:S(2)}) copy-start(bf16[2,256,512]{2,1,0:T(8,128)(2,1)} %constant.63.clone.pixels_ref) | copy-start | bytes 1572868
  9.8 20.4 %copy-start.11 = (bf16[2,4,128,128]{3,2,1,0:T(8,128)(2,1)S(1)}, bf16[2,4,128,128]{3,2,1,0:T(8,128)(2,1)}, u32[]{:S(2)}) copy-start(bf16[2,4,128,128]{3,2,1,0:T(8,128)(2,1)} %constant.61.clone.out_rows_ref) | copy-start | bytes 786436
  9.8 20.4 %copy-start.14 = (bf16[128,256]{1,0:T(8,128)(2,1)S(1)}, bf16[128,256]{1,0:T(8,128)(2,1)}, u32[]{:S(2)}) copy-start(bf16[128,256]{1,0:T(8,128)(2,1)} %constant.57.clone.unfold_ref) | copy-start | bytes 196612
  9.8 20.4 %copy-start.17 = (bf16[64,72]{1,0:T(8,128)(2,1)S(1)}, bf16[64,72]{1,0:T(8,128)(2,1)}, u32[]{:S(2)}) copy-start(bf16[64,72]{1,0:T(8,128)(2,1)} %constant.59.clone.flip_ref) | copy-start | bytes 27652
  9.8 6.6 %collective-permute-start.4 = (f32[72,128]{1,0:T(8,128)S(1)}, f32[72,128]{1,0:T(8,128)S(1)}, u32[]{:S(2)}, u32[]{:S(2)}) collective-permute-start(f32[72,128]{1,0:T(8,128)S(1)} %window_kernel.1.r0), channel_id=1, source_target_pairs={{0,3},{1,2},{2,1},{3,0},{4,7},{5,6},{6,5},{7,4},{8,11},{9,10},{10,... | collective-permute-start | bytes 110600 | tf_op jit(solution)/shard_map/ppermute | solution.py:432
  13.5 8.0 %collective-permute-start.3 = (f32[72,128]{1,0:T(8,128)S(1)}, f32[72,128]{1,0:T(8,128)S(1)}, u32[]{:S(2)}, u32[]{:S(2)}) collective-permute-start(f32[72,128]{1,0:T(8,128)S(1)} %window_kernel.1.r0), channel_id=1, source_target_pairs={{0,2},{1,3},{2,0},{3,1},{4,6},{5,7},{6,4},{7,5},{8,10},{9,11},{10,... | collective-permute-start | bytes 110600 | tf_op jit(solution)/shard_map/ppermute | solution.py:432
  14.5 7.0 %collective-permute-start.2 = (f32[72,128]{1,0:T(8,128)S(1)}, f32[72,128]{1,0:T(8,128)S(1)}, u32[]{:S(2)}, u32[]{:S(2)}) collective-permute-start(f32[72,128]{1,0:T(8,128)S(1)} %window_kernel.1.r0), channel_id=1, source_target_pairs={{0,1},{1,0},{2,3},{3,2},{4,5},{5,4},{6,7},{7,6},{8,9},{9,8},{10,11... | collective-permute-start | bytes 110600 | tf_op jit(solution)/shard_map/ppermute | solution.py:432
  16.4 9.6 %collective-permute-start.10 = (f32[2,2,128,128]{3,2,1,0:T(8,128)S(1)}, f32[2,2,128,128]{3,2,1,0:T(8,128)S(1)}, u32[]{:S(2)}, u32[]{:S(2)}) collective-permute-start(f32[2,2,128,128]{3,2,1,0:T(8,128)S(1)} %copy-done.1), channel_id=1, source_target_pairs={{0,8},{1,9},{2,10},{3,11},{4,12},{5,13},{6,14},{7,15},{8,0},{9,1},... | collective-permute-start | bytes 786440 | tf_op jit(solution)/shard_map/ppermute | solution.py:428
  21.8 5.6 %collective-permute-start.9 = (f32[144,128]{1,0:T(8,128)S(1)}, f32[144,128]{1,0:T(8,128)S(1)}, u32[]{:S(2)}, u32[]{:S(2)}) collective-permute-start(f32[144,128]{1,0:T(8,128)S(1)} %band_kernel.1.p0), channel_id=1, source_target_pairs={{0,12},{1,13},{2,14},{3,15},{4,8},{5,9},{6,10},{7,11},{8,4},{9,5},... | collective-permute-start | bytes 221192 | tf_op jit(solution)/shard_map/ppermute | solution.py:428
  24.1 5.9 %collective-permute-start.8 = (f32[144,128]{1,0:T(8,128)S(1)}, f32[144,128]{1,0:T(8,128)S(1)}, u32[]{:S(2)}, u32[]{:S(2)}) collective-permute-start(f32[144,128]{1,0:T(8,128)S(1)} %band_kernel.1.p0), channel_id=1, source_target_pairs={{0,8},{1,9},{2,10},{3,11},{4,12},{5,13},{6,14},{7,15},{8,0},{9,1},... | collective-permute-start | bytes 221192 | tf_op jit(solution)/shard_map/ppermute | solution.py:428
  25.8 4.4 %collective-permute-start.7 = (f32[144,128]{1,0:T(8,128)S(1)}, f32[144,128]{1,0:T(8,128)S(1)}, u32[]{:S(2)}, u32[]{:S(2)}) collective-permute-start(f32[144,128]{1,0:T(8,128)S(1)} %band_kernel.1.p0), channel_id=1, source_target_pairs={{0,4},{1,5},{2,6},{3,7},{4,0},{5,1},{6,2},{7,3},{8,12},{9,13},{10,... | collective-permute-start | bytes 221192 | tf_op jit(solution)/shard_map/ppermute | solution.py:428
  26.0 16.1 %copy-start.4 = (bf16[3,256,1024]{2,1,0:T(8,128)(2,1)S(1)}, bf16[3,256,1024]{2,1,0:T(8,128)(2,1)}, u32[]{:S(2)}) copy-start(bf16[3,256,1024]{2,1,0:T(8,128)(2,1)} %constant.65.clone.spread_ref) | copy-start | bytes 4718596
  26.0 16.1 %copy-start.5 = (bf16[2,1024,256]{2,1,0:T(8,128)(2,1)S(1)}, bf16[2,1024,256]{2,1,0:T(8,128)(2,1)}, u32[]{:S(2)}) copy-start(bf16[2,1024,256]{2,1,0:T(8,128)(2,1)} %constant.66.clone.spread_back_ref) | copy-start | bytes 3145732
  26.0 16.1 %copy-start.8 = (bf16[2,512,256]{2,1,0:T(8,128)(2,1)S(1)}, bf16[2,512,256]{2,1,0:T(8,128)(2,1)}, u32[]{:S(2)}) copy-start(bf16[2,512,256]{2,1,0:T(8,128)(2,1)} %constant.64.clone.pixels_back_ref) | copy-start | bytes 1572868
  26.0 16.2 %copy-start.10 = (bf16[2,4,128,128]{3,2,1,0:T(8,128)(2,1)S(1)}, bf16[2,4,128,128]{3,2,1,0:T(8,128)(2,1)}, u32[]{:S(2)}) copy-start(bf16[2,4,128,128]{3,2,1,0:T(8,128)(2,1)} %constant.62.clone.out_back_ref) | copy-start | bytes 786436
  26.0 16.2 %copy-start.13 = (bf16[256,128]{1,0:T(8,128)(2,1)S(1)}, bf16[256,128]{1,0:T(8,128)(2,1)}, u32[]{:S(2)}) copy-start(bf16[256,128]{1,0:T(8,128)(2,1)} %constant.58.clone.fold_ref) | copy-start | bytes 196612
  26.0 16.2 %copy-start.16 = (bf16[72,64]{1,0:T(8,128)(2,1)S(1)}, bf16[72,64]{1,0:T(8,128)(2,1)}, u32[]{:S(2)}) copy-start(bf16[72,64]{1,0:T(8,128)(2,1)} %constant.60.clone.flip_back_ref) | copy-start | bytes 27652
  31.5 10.3 %collective-permute-start.13 = (f32[64,256]{1,0:T(8,128)S(1)}, f32[64,256]{1,0:T(8,128)S(1)}, u32[]{:S(2)}, u32[]{:S(2)}) collective-permute-start(f32[64,256]{1,0:T(8,128)S(1)} %get-tuple-element.28.i0), channel_id=1, source_target_pairs={{0,2},{1,3},{2,0},{3,1},{4,6},{5,7},{6,4},{7,5},{8,10},{9,11},{10,... | collective-permute-start | bytes 196616 | tf_op jit(solution)/shard_map/ppermute | solution.py:432
  34.4 7.4 %collective-permute-start.12 = (f32[64,256]{1,0:T(8,128)S(1)}, f32[64,256]{1,0:T(8,128)S(1)}, u32[]{:S(2)}, u32[]{:S(2)}) collective-permute-start(f32[64,256]{1,0:T(8,128)S(1)} %get-tuple-element.28.i0), channel_id=1, source_target_pairs={{0,3},{1,2},{2,1},{3,0},{4,7},{5,6},{6,5},{7,4},{8,11},{9,10},{10,... | collective-permute-start | bytes 196616 | tf_op jit(solution)/shard_map/ppermute | solution.py:432
  36.6 5.5 %collective-permute-start.11 = (f32[64,256]{1,0:T(8,128)S(1)}, f32[64,256]{1,0:T(8,128)S(1)}, u32[]{:S(2)}, u32[]{:S(2)}) collective-permute-start(f32[64,256]{1,0:T(8,128)S(1)} %get-tuple-element.28.i0), channel_id=1, source_target_pairs={{0,1},{1,0},{2,3},{3,2},{4,5},{5,4},{6,7},{7,6},{8,9},{9,8},{10,11... | collective-permute-start | bytes 196616 | tf_op jit(solution)/shard_map/ppermute | solution.py:432
  42.1 10.9 %copy-start.7 = (bf16[2,128,1024]{2,1,0:T(8,128)(2,1)S(1)}, bf16[2,128,1024]{2,1,0:T(8,128)(2,1)}, u32[]{:S(2)}) copy-start(bf16[2,128,1024]{2,1,0:T(8,128)(2,1)} %constant.55.clone.band_back_ref) | copy-start | bytes 1572868
  42.2 10.9 %copy-start.15 = (f32[8,1024]{1,0:T(8,128)S(1)}, f32[8,1024]{1,0:T(8,128)}, u32[]{:S(2)}) copy-start(f32[8,1024]{1,0:T(8,128)} %constant.56.clone.edge_ref) | copy-start | bytes 98308
  44.3 4.8 %collective-permute-start.14 = (f32[176,128]{1,0:T(8,128)S(1)}, f32[176,128]{1,0:T(8,128)S(1)}, u32[]{:S(2)}, u32[]{:S(2)}) collective-permute-start(f32[176,128]{1,0:T(8,128)S(1)} %get-tuple-element.31), channel_id=1, source_target_pairs={{0,4},{1,5},{2,6},{3,7},{4,0},{5,1},{6,2},{7,3},{8,12},{9,13},{10,... | collective-permute-start | bytes 270344 | tf_op jit(solution)/shard_map/ppermute | solution.py:428
  45.0 6.0 %collective-permute-start.15 = (f32[176,128]{1,0:T(8,128)S(1)}, f32[176,128]{1,0:T(8,128)S(1)}, u32[]{:S(2)}, u32[]{:S(2)}) collective-permute-start(f32[176,128]{1,0:T(8,128)S(1)} %get-tuple-element.32), channel_id=1, source_target_pairs={{0,8},{1,9},{2,10},{3,11},{4,12},{5,13},{6,14},{7,15},{8,0},{9,1},... | collective-permute-start | bytes 270344 | tf_op jit(solution)/shard_map/ppermute | solution.py:428
  47.3 5.7 %collective-permute-start.16 = (f32[176,128]{1,0:T(8,128)S(1)}, f32[176,128]{1,0:T(8,128)S(1)}, u32[]{:S(2)}, u32[]{:S(2)}) collective-permute-start(f32[176,128]{1,0:T(8,128)S(1)} %get-tuple-element.33), channel_id=1, source_target_pairs={{0,12},{1,13},{2,14},{3,15},{4,8},{5,9},{6,10},{7,11},{8,4},{9,5},... | collective-permute-start | bytes 270344 | tf_op jit(solution)/shard_map/ppermute | solution.py:428
  53.4 6.6 %collective-permute-start.17 = (f32[72,128]{1,0:T(8,128)S(1)}, f32[72,128]{1,0:T(8,128)S(1)}, u32[]{:S(2)}, u32[]{:S(2)}) collective-permute-start(f32[72,128]{1,0:T(8,128)S(1)} %get-tuple-element.35), channel_id=1, source_target_pairs={{0,1},{1,0},{2,3},{3,2},{4,5},{5,4},{6,7},{7,6},{8,9},{9,8},{10,11... | collective-permute-start | bytes 110600 | tf_op jit(solution)/shard_map/ppermute | solution.py:432
  54.5 7.9 %collective-permute-start.18 = (f32[72,128]{1,0:T(8,128)S(1)}, f32[72,128]{1,0:T(8,128)S(1)}, u32[]{:S(2)}, u32[]{:S(2)}) collective-permute-start(f32[72,128]{1,0:T(8,128)S(1)} %get-tuple-element.36), channel_id=1, source_target_pairs={{0,2},{1,3},{2,0},{3,1},{4,6},{5,7},{6,4},{7,5},{8,10},{9,11},{10,... | collective-permute-start | bytes 110600 | tf_op jit(solution)/shard_map/ppermute | solution.py:432
  58.0 6.3 %collective-permute-start.19 = (f32[72,128]{1,0:T(8,128)S(1)}, f32[72,128]{1,0:T(8,128)S(1)}, u32[]{:S(2)}, u32[]{:S(2)}) collective-permute-start(f32[72,128]{1,0:T(8,128)S(1)} %get-tuple-element.37), channel_id=1, source_target_pairs={{0,3},{1,2},{2,1},{3,0},{4,7},{5,6},{6,5},{7,4},{8,11},{9,10},{10,... | collective-permute-start | bytes 110600 | tf_op jit(solution)/shard_map/ppermute | solution.py:432
  64.3 5.6 %collective-permute-start.21 = (f32[72,128]{1,0:T(8,128)S(1)}, f32[72,128]{1,0:T(8,128)S(1)}, u32[]{:S(2)}, u32[]{:S(2)}) collective-permute-start(f32[72,128]{1,0:T(8,128)S(1)} %add_add_fusion.own_ref), channel_id=1, source_target_pairs={{0,240},{16,32},{32,16},{48,64},{64,48},{80,96},{96,80},{112,128},... | collective-permute-start | bytes 110600 | tf_op jit(solution)/shard_map/ppermute | solution.py:440
  64.5 5.4 %collective-permute-start.20 = (f32[72,128]{1,0:T(8,128)S(1)}, f32[72,128]{1,0:T(8,128)S(1)}, u32[]{:S(2)}, u32[]{:S(2)}) collective-permute-start(f32[72,128]{1,0:T(8,128)S(1)} %add_add_fusion.own_ref), channel_id=1, source_target_pairs={{0,16},{16,0},{32,48},{48,32},{64,80},{80,64},{96,112},{112,96},{1... | collective-permute-start | bytes 110600 | tf_op jit(solution)/shard_map/ppermute | solution.py:436

commit v7 on v6

--- a/solution.py
+++ b/solution.py
@@ -483,9 +483,9 @@
         [(HALF, 2 * SHARD)] * 4,
         *messages, table["band_back"], table["edge_back"], scratch=order,
     )
-    grad = grads[0]
-    for step in (1, 2, 3):
-        grad = grad + swap_z(grads[step], step)
+    near, middle, far = [swap_z(grads[step], step) for step in (1, 2, 3)]
+    near, resist = lax.optimization_barrier((near, resist))
+    grad = (grads[0] + near) + (middle + far)
     mask_grad = call(
         final_kernel, (SHARD, TILE), swap_inner(grad), swap_outer(grad), grad,
         table["rows"],

time: 71.6 us -> 71.6 us (level)
    ppermute x2, waiting for transfers between devices: 4.41 us -> 5.19 us  [swap_outer(): lax.ppermute(value, 'tile', [(i, (i + 1 ^ 1) - 1 & 15) for i in range(16)])]
    ppermute x9, waiting for transfers between devices: 11.8 us -> 11 us  [swap_z(): return lax.ppermute(value, 'kern', [(i, i ^ step) for i in range(16)])]
where the time goes in v7:
time: 71.6 us; the launch traced here: 70.7 us
  starting transfers between devices  38.2 us (53%)
  waiting for transfers between devices  24.3 us (34%)
  Pallas kernels  6.66 us (9%)
  between operations  0.88 us (1%)
  local copies, waits for them, and re-layouts  0.77 us (1%)
    ppermute x9, starting transfers between devices, swap_z(): return lax.ppermute(value, 'kern', [(i, i ^ step) for i in range(16)])  19.7 us
    ppermute x9, starting transfers between devices, swap_y(): return lax.ppermute(value, 'kern', [(i, i ^ 4 * step) for i in range(16)])  13.7 us
    ppermute x9, waiting for transfers between devices, swap_z(): return lax.ppermute(value, 'kern', [(i, i ^ step) for i in range(16)])  11 us
    ppermute x9, waiting for transfers between devices, swap_y(): return lax.ppermute(value, 'kern', [(i, i ^ 4 * step) for i in range(16)])  8.1 us
    pallas_call x8, Pallas kernels, call(): pl.pallas_call(kernel, scratch_shapes=list(scratch), out_shape=out if man...  6.66 us
    ppermute x2, waiting for transfers between devices, swap_outer(): lax.ppermute(value, 'tile', [(i, (i + 1 ^ 1) - 1 & 15) for i in range(16)])  5.19 us
    ppermute x2, starting transfers between devices, swap_outer(): lax.ppermute(value, 'tile', [(i, (i + 1 ^ 1) - 1 & 15) for i in range(16)])  4.43 us
  transfers between devices with their start and end apart: 22, of which 11 were waited for; matrix products, arithmetic and copies ran while one was open for 0% of the time, Pallas kernels for 3%

profile of v7, /device:TPU:64, one launch (start us, length us, event | category | flops | bytes accessed | tf_op | source)
XLA Modules:
  0.0 70.7 jit_solution(15890388271403570827)
XLA Ops:
  0.6 0.0 copy-start
  0.7 0.1 collective-permute-start.1
  0.8 4.2 %collective-permute-start = (f32[64,256]{1,0:T(8,128)}, f32[64,256]{1,0:T(8,128)S(1)}, u32[]{:S(2)}, u32[]{:S(2)}) collective-permute-start(f32[64,256]{1,0:T(8,128)} %bitcast.4), channel_id=1, source_target_pairs={{0,240},{16,32},{32,16},{48,64},{64,48},{80,96},{96,80},{112,128},... | collective-permute-start | bytes 196616 | tf_op jit(solution)/shard_map/ppermute | solution.py:440
  5.0 0.7 copy-done.3
  5.6 0.5 weight_kernel.1.heavy_ref
  6.2 0.0 copy-start.6
  6.2 3.1 %collective-permute-start.6 = (f32[2,2,128,128]{3,2,1,0:T(8,128)S(1)}, f32[2,2,128,128]{3,2,1,0:T(8,128)S(1)}, u32[]{:S(2)}, u32[]{:S(2)}) collective-permute-start(f32[2,2,128,128]{3,2,1,0:T(8,128)S(1)} %copy-done.1), channel_id=1, source_target_pairs={{0,12},{1,13},{2,14},{3,15},{4,8},{5,9},{6,10},{7,11},{8,4},{9,5},... | collective-permute-start | bytes 786440 | tf_op jit(solution)/shard_map/ppermute | solution.py:428
  9.3 0.1 collective-permute-start.5
  9.5 0.3 window_kernel.1.r0
  9.8 0.0 copy-start.9
  9.8 0.0 copy-start.14
  9.8 0.0 copy-start.17
  9.8 3.7 %collective-permute-start.4 = (f32[72,128]{1,0:T(8,128)S(1)}, f32[72,128]{1,0:T(8,128)S(1)}, u32[]{:S(2)}, u32[]{:S(2)}) collective-permute-start(f32[72,128]{1,0:T(8,128)S(1)} %window_kernel.1.r0), channel_id=1, source_target_pairs={{0,3},{1,2},{2,1},{3,0},{4,7},{5,6},{6,5},{7,4},{8,11},{9,10},{10,... | collective-permute-start | bytes 110600 | tf_op jit(solution)/shard_map/ppermute | solution.py:432
  13.5 1.0 %collective-permute-start.3 = (f32[72,128]{1,0:T(8,128)S(1)}, f32[72,128]{1,0:T(8,128)S(1)}, u32[]{:S(2)}, u32[]{:S(2)}) collective-permute-start(f32[72,128]{1,0:T(8,128)S(1)} %window_kernel.1.r0), channel_id=1, source_target_pairs={{0,2},{1,3},{2,0},{3,1},{4,6},{5,7},{6,4},{7,5},{8,10},{9,11},{10,... | collective-permute-start | bytes 110600 | tf_op jit(solution)/shard_map/ppermute | solution.py:432
  14.5 1.9 %collective-permute-start.2 = (f32[72,128]{1,0:T(8,128)S(1)}, f32[72,128]{1,0:T(8,128)S(1)}, u32[]{:S(2)}, u32[]{:S(2)}) collective-permute-start(f32[72,128]{1,0:T(8,128)S(1)} %window_kernel.1.r0), channel_id=1, source_target_pairs={{0,1},{1,0},{2,3},{3,2},{4,5},{5,4},{6,7},{7,6},{8,9},{9,8},{10,11... | collective-permute-start | bytes 110600 | tf_op jit(solution)/shard_map/ppermute | solution.py:432
  16.4 1.5 %collective-permute-start.10 = (f32[2,2,128,128]{3,2,1,0:T(8,128)S(1)}, f32[2,2,128,128]{3,2,1,0:T(8,128)S(1)}, u32[]{:S(2)}, u32[]{:S(2)}) collective-permute-start(f32[2,2,128,128]{3,2,1,0:T(8,128)S(1)} %copy-done.1), channel_id=1, source_target_pairs={{0,8},{1,9},{2,10},{3,11},{4,12},{5,13},{6,14},{7,15},{8,0},{9,1},... | collective-permute-start | bytes 786440 | tf_op jit(solution)/shard_map/ppermute | solution.py:428
  18.0 3.5 %collective-permute-done.3.r2 = f32[72,128]{1,0:T(8,128)S(1)} collective-permute-done((f32[72,128]{1,0:T(8,128)S(1)}, f32[72,128]{1,0:T(8,128)S(1)}, u32[]{:S(2)}, u32[]{:S(2)}) %collective-permute-start.3) | collective-permute-done | bytes 36896 | tf_op jit(solution)/shard_map/ppermute | solution.py:432
  21.5 0.3 band_kernel.1.p0
  21.8 2.3 %collective-permute-start.9 = (f32[144,128]{1,0:T(8,128)S(1)}, f32[144,128]{1,0:T(8,128)S(1)}, u32[]{:S(2)}, u32[]{:S(2)}) collective-permute-start(f32[144,128]{1,0:T(8,128)S(1)} %band_kernel.1.p0), channel_id=1, source_target_pairs={{0,12},{1,13},{2,14},{3,15},{4,8},{5,9},{6,10},{7,11},{8,4},{9,5},... | collective-permute-start | bytes 221192 | tf_op jit(solution)/shard_map/ppermute | solution.py:428
  24.1 1.7 %collective-permute-start.8 = (f32[144,128]{1,0:T(8,128)S(1)}, f32[144,128]{1,0:T(8,128)S(1)}, u32[]{:S(2)}, u32[]{:S(2)}) collective-permute-start(f32[144,128]{1,0:T(8,128)S(1)} %band_kernel.1.p0), channel_id=1, source_target_pairs={{0,8},{1,9},{2,10},{3,11},{4,12},{5,13},{6,14},{7,15},{8,0},{9,1},... | collective-permute-start | bytes 221192 | tf_op jit(solution)/shard_map/ppermute | solution.py:428
  25.8 0.1 collective-permute-start.7
  26.0 0.0 copy-start.13
  26.0 1.4 %collective-permute-done.9.p3 = f32[144,128]{1,0:T(8,128)S(1)} collective-permute-done((f32[144,128]{1,0:T(8,128)S(1)}, f32[144,128]{1,0:T(8,128)S(1)}, u32[]{:S(2)}, u32[]{:S(2)}) %collective-permute-start.9) | collective-permute-done | bytes 73760 | tf_op jit(solution)/shard_map/ppermute | solution.py:428
  27.4 2.6 %collective-permute-done.8.p2 = f32[144,128]{1,0:T(8,128)S(1)} collective-permute-done((f32[144,128]{1,0:T(8,128)S(1)}, f32[144,128]{1,0:T(8,128)S(1)}, u32[]{:S(2)}, u32[]{:S(2)}) %collective-permute-start.8) | collective-permute-done | bytes 73760 | tf_op jit(solution)/shard_map/ppermute | solution.py:428
  30.0 0.2 collective-permute-done.7.p1
  30.2 1.3 %aerial_kernel.1 = (f32[512,512]{1,0:T(8,128)S(1)}, f32[64,256]{1,0:T(8,128)S(1)}) custom-call(f32[144,128]{1,0:T(8,128)S(1)} %band_kernel.1.p0, f32[144,128]{1,0:T(8,128)S(1)} %collective-permute-done.7.p1, f32[144,128]{1,0:T(8,128)S(1)} %collective-permute-done.8.p2, f32[144,128]{1,0:T(8,128)S(1)} %collective-permute-done.9.p3, ...), custom_call_target="tpu_custom_call" | custom-call | flops 4000000000 | bytes 1000000 | tf_op jit(solution)/shard_map/aerial_kernel/pallas_call | solution.py:413
  31.5 2.9 %collective-permute-start.13 = (f32[64,256]{1,0:T(8,128)S(1)}, f32[64,256]{1,0:T(8,128)S(1)}, u32[]{:S(2)}, u32[]{:S(2)}) collective-permute-start(f32[64,256]{1,0:T(8,128)S(1)} %get-tuple-element.30.i0), channel_id=1, source_target_pairs={{0,2},{1,3},{2,0},{3,1},{4,6},{5,7},{6,4},{7,5},{8,10},{9,11},{10,... | collective-permute-start | bytes 196616 | tf_op jit(solution)/shard_map/ppermute | solution.py:432
  34.4 2.2 %collective-permute-start.12 = (f32[64,256]{1,0:T(8,128)S(1)}, f32[64,256]{1,0:T(8,128)S(1)}, u32[]{:S(2)}, u32[]{:S(2)}) collective-permute-start(f32[64,256]{1,0:T(8,128)S(1)} %get-tuple-element.30.i0), channel_id=1, source_target_pairs={{0,3},{1,2},{2,1},{3,0},{4,7},{5,6},{6,5},{7,4},{8,11},{9,10},{10,... | collective-permute-start | bytes 196616 | tf_op jit(solution)/shard_map/ppermute | solution.py:432
  36.6 1.5 %collective-permute-start.11 = (f32[64,256]{1,0:T(8,128)S(1)}, f32[64,256]{1,0:T(8,128)S(1)}, u32[]{:S(2)}, u32[]{:S(2)}) collective-permute-start(f32[64,256]{1,0:T(8,128)S(1)} %get-tuple-element.30.i0), channel_id=1, source_target_pairs={{0,1},{1,0},{2,3},{3,2},{4,5},{5,4},{6,7},{7,6},{8,9},{9,8},{10,11... | collective-permute-start | bytes 196616 | tf_op jit(solution)/shard_map/ppermute | solution.py:432
  38.1 3.7 %collective-permute-done.13.i3 = f32[64,256]{1,0:T(8,128)S(1)} collective-permute-done((f32[64,256]{1,0:T(8,128)S(1)}, f32[64,256]{1,0:T(8,128)S(1)}, u32[]{:S(2)}, u32[]{:S(2)}) %collective-permute-start.13) | collective-permute-done | bytes 65568 | tf_op jit(solution)/shard_map/ppermute | solution.py:432
  41.8 0.3 collective-permute-done.11.i1
  42.2 2.2 %slope_kernel.1 = (f32[176,128]{1,0:T(8,128)S(1)}, f32[176,128]{1,0:T(8,128)S(1)}, f32[176,128]{1,0:T(8,128)S(1)}, f32[176,128]{1,0:T(8,128)S(1)}) custom-call(f32[64,256]{1,0:T(8,128)S(1)} %get-tuple-element.30.i0, f32[64,256]{1,0:T(8,128)S(1)} %collective-permute-done.11.i1, f32[64,256]{1,0:T(8,128)S(1)} %collective-permute-done.12.i2, ...), custom_call_target="tpu_custom_call" | custom-call | flops 4000000000 | bytes 1000000 | tf_op jit(solution)/shard_map/slope_kernel/pallas_call | solution.py:413
  44.3 0.6 collective-permute-start.14
  45.0 2.4 %collective-permute-start.15 = (f32[176,128]{1,0:T(8,128)S(1)}, f32[176,128]{1,0:T(8,128)S(1)}, u32[]{:S(2)}, u32[]{:S(2)}) collective-permute-start(f32[176,128]{1,0:T(8,128)S(1)} %get-tuple-element.34), channel_id=1, source_target_pairs={{0,8},{1,9},{2,10},{3,11},{4,12},{5,13},{6,14},{7,15},{8,0},{9,1},... | collective-permute-start | bytes 270344 | tf_op jit(solution)/shard_map/ppermute | solution.py:428
  47.3 1.8 %collective-permute-start.16 = (f32[176,128]{1,0:T(8,128)S(1)}, f32[176,128]{1,0:T(8,128)S(1)}, u32[]{:S(2)}, u32[]{:S(2)}) collective-permute-start(f32[176,128]{1,0:T(8,128)S(1)} %get-tuple-element.35), channel_id=1, source_target_pairs={{0,12},{1,13},{2,14},{3,15},{4,8},{5,9},{6,10},{7,11},{8,4},{9,5},... | collective-permute-start | bytes 270344 | tf_op jit(solution)/shard_map/ppermute | solution.py:428
  49.1 1.9 %collective-permute-done.15.m2 = f32[176,128]{1,0:T(8,128)S(1)} collective-permute-done((f32[176,128]{1,0:T(8,128)S(1)}, f32[176,128]{1,0:T(8,128)S(1)}, u32[]{:S(2)}, u32[]{:S(2)}) %collective-permute-start.15) | collective-permute-done | bytes 90144 | tf_op jit(solution)/shard_map/ppermute | solution.py:428
  51.0 2.1 %collective-permute-done.16.m3 = f32[176,128]{1,0:T(8,128)S(1)} collective-permute-done((f32[176,128]{1,0:T(8,128)S(1)}, f32[176,128]{1,0:T(8,128)S(1)}, u32[]{:S(2)}, u32[]{:S(2)}) %collective-permute-start.16) | collective-permute-done | bytes 90144 | tf_op jit(solution)/shard_map/ppermute | solution.py:428
  53.1 0.3 columns_kernel.1
  53.4 1.1 %collective-permute-start.17 = (f32[72,128]{1,0:T(8,128)S(1)}, f32[72,128]{1,0:T(8,128)S(1)}, u32[]{:S(2)}, u32[]{:S(2)}) collective-permute-start(f32[72,128]{1,0:T(8,128)S(1)} %get-tuple-element.36), channel_id=1, source_target_pairs={{0,1},{1,0},{2,3},{3,2},{4,5},{5,4},{6,7},{7,6},{8,9},{9,8},{10,11... | collective-permute-start | bytes 110600 | tf_op jit(solution)/shard_map/ppermute | solution.py:432
  54.5 3.5 %collective-permute-start.18 = (f32[72,128]{1,0:T(8,128)S(1)}, f32[72,128]{1,0:T(8,128)S(1)}, u32[]{:S(2)}, u32[]{:S(2)}) collective-permute-start(f32[72,128]{1,0:T(8,128)S(1)} %get-tuple-element.40), channel_id=1, source_target_pairs={{0,2},{1,3},{2,0},{3,1},{4,6},{5,7},{6,4},{7,5},{8,10},{9,11},{10,... | collective-permute-start | bytes 110600 | tf_op jit(solution)/shard_map/ppermute | solution.py:432
  58.0 2.0 %collective-permute-start.19 = (f32[72,128]{1,0:T(8,128)S(1)}, f32[72,128]{1,0:T(8,128)S(1)}, u32[]{:S(2)}, u32[]{:S(2)}) collective-permute-start(f32[72,128]{1,0:T(8,128)S(1)} %get-tuple-element.41), channel_id=1, source_target_pairs={{0,3},{1,2},{2,1},{3,0},{4,7},{5,6},{6,5},{7,4},{8,11},{9,10},{10,... | collective-permute-start | bytes 110600 | tf_op jit(solution)/shard_map/ppermute | solution.py:432
  60.0 0.8 %resist_kernel.1 = f32[64,256]{1,0:T(8,128)} custom-call(f32[176,128]{1,0:T(8,128)S(1)} %get-tuple-element.32.m0, f32[176,128]{1,0:T(8,128)S(1)} %collective-permute-done.14.m1, f32[176,128]{1,0:T(8,128)S(1)} %collective-permute-done.15.m2, f32[176,128]{1,0:T(8,128)S(1)} %collective-permute-done.16.m3), custom_call_target="tpu_custom_call" | custom-call | flops 4000000000 | bytes 1000000 | tf_op jit(solution)/shard_map/resist_kernel/pallas_call | solution.py:413
  60.8 1.6 %collective-permute-done.18 = f32[72,128]{1,0:T(8,128)S(1)} collective-permute-done((f32[72,128]{1,0:T(8,128)S(1)}, f32[72,128]{1,0:T(8,128)S(1)}, u32[]{:S(2)}, u32[]{:S(2)}) %collective-permute-start.18) | collective-permute-done | bytes 36896 | tf_op jit(solution)/shard_map/ppermute | solution.py:432
  62.3 1.9 %collective-permute-done.19 = f32[72,128]{1,0:T(8,128)S(1)} collective-permute-done((f32[72,128]{1,0:T(8,128)S(1)}, f32[72,128]{1,0:T(8,128)S(1)}, u32[]{:S(2)}, u32[]{:S(2)}) %collective-permute-start.19) | collective-permute-done | bytes 36896 | tf_op jit(solution)/shard_map/ppermute | solution.py:432
  64.3 0.2 collective-permute-start.21
  64.5 0.2 collective-permute-start.20
  64.6 5.2 %collective-permute-done.21.outer_ref = f32[72,128]{1,0:T(8,128)S(1)} collective-permute-done((f32[72,128]{1,0:T(8,128)S(1)}, f32[72,128]{1,0:T(8,128)S(1)}, u32[]{:S(2)}, u32[]{:S(2)}) %collective-permute-start.21) | collective-permute-done | bytes 36896 | tf_op jit(solution)/shard_map/ppermute | solution.py:440
  69.8 0.9 %final_kernel.1 = f32[64,256]{1,0:T(8,128)} custom-call(f32[72,128]{1,0:T(8,128)S(1)} %collective-permute-done.20.inner_ref, f32[72,128]{1,0:T(8,128)S(1)} %collective-permute-done.21.outer_ref, f32[72,128]{1,0:T(8,128)S(1)} %add_add_fusion.own_ref, bf16[2,160,256]{2,1,0:T(8,128)(2,1)S(1)} %copy-done.12), custom_call_target="tpu_custom_call" | custom-call | flops 4000000000 | bytes 1000000 | tf_op jit(solution)/shard_map/final_kernel/pallas_call | solution.py:413
  (42 shorter events, 0.1 us)
Async XLA Ops:
  0.6 37.5 %copy-start = (s32[256,1024]{1,0:T(8,128)S(1)}, s32[256,1024]{1,0:T(8,128)}, u32[]{:S(2)}) copy-start(s32[256,1024]{1,0:T(8,128)} %param.19) | copy-start | bytes 3145732
  0.6 5.5 %copy-start.1 = (f32[2,2,128,128]{3,2,1,0:T(8,128)S(1)}, f32[2,2,128,128]{3,2,1,0:T(8,128)}, u32[]{:S(2)}) copy-start(f32[2,2,128,128]{3,2,1,0:T(8,128)} %h0.1) | copy-start | bytes 786436
  0.7 8.8 %copy-start.2 = (f32[256,64]{0,1:T(8,128)S(1)}, f32[256,64]{0,1:T(8,128)}, u32[]{:S(2)}) copy-start(f32[256,64]{0,1:T(8,128)} %param.18) | copy-start | bytes 196612
  0.7 8.8 %collective-permute-start.1 = (f32[64,256]{1,0:T(8,128)}, f32[64,256]{1,0:T(8,128)S(1)}, u32[]{:S(2)}, u32[]{:S(2)}) collective-permute-start(f32[64,256]{1,0:T(8,128)} %bitcast.3), channel_id=1, source_target_pairs={{0,16},{16,0},{32,48},{48,32},{64,80},{80,64},{96,112},{112,96},{1... | collective-permute-start | bytes 196616 | tf_op jit(solution)/shard_map/ppermute | solution.py:436
  0.8 8.7 %collective-permute-start = (f32[64,256]{1,0:T(8,128)}, f32[64,256]{1,0:T(8,128)S(1)}, u32[]{:S(2)}, u32[]{:S(2)}) collective-permute-start(f32[64,256]{1,0:T(8,128)} %bitcast.4), channel_id=1, source_target_pairs={{0,240},{16,32},{32,16},{48,64},{64,48},{80,96},{96,80},{112,128},... | collective-permute-start | bytes 196616 | tf_op jit(solution)/shard_map/ppermute | solution.py:440
  5.0 0.7 copy-start.3
  5.6 3.8 %copy-start.12 = (bf16[2,160,256]{2,1,0:T(8,128)(2,1)S(1)}, bf16[2,160,256]{2,1,0:T(8,128)(2,1)}, u32[]{:S(2)}) copy-start(bf16[2,160,256]{2,1,0:T(8,128)(2,1)} %constant.53.clone.rows_ref) | copy-start | bytes 491524
  6.2 15.3 %copy-start.6 = (bf16[2,16,64,256]{3,2,1,0:T(8,128)(2,1)S(1)}, bf16[2,16,64,256]{3,2,1,0:T(8,128)(2,1)}, u32[]{:S(2)}) copy-start(bf16[2,16,64,256]{3,2,1,0:T(8,128)(2,1)} %constant.54.clone.band_ref) | copy-start | bytes 3145732
  6.2 15.3 %collective-permute-start.6 = (f32[2,2,128,128]{3,2,1,0:T(8,128)S(1)}, f32[2,2,128,128]{3,2,1,0:T(8,128)S(1)}, u32[]{:S(2)}, u32[]{:S(2)}) collective-permute-start(f32[2,2,128,128]{3,2,1,0:T(8,128)S(1)} %copy-done.1), channel_id=1, source_target_pairs={{0,12},{1,13},{2,14},{3,15},{4,8},{5,9},{6,10},{7,11},{8,4},{9,5},... | collective-permute-start | bytes 786440 | tf_op jit(solution)/shard_map/ppermute | solution.py:428
  9.3 12.2 %collective-permute-start.5 = (f32[2,2,128,128]{3,2,1,0:T(8,128)S(1)}, f32[2,2,128,128]{3,2,1,0:T(8,128)S(1)}, u32[]{:S(2)}, u32[]{:S(2)}) collective-permute-start(f32[2,2,128,128]{3,2,1,0:T(8,128)S(1)} %copy-done.1), channel_id=1, source_target_pairs={{0,4},{1,5},{2,6},{3,7},{4,0},{5,1},{6,2},{7,3},{8,12},{9,13},{10,... | collective-permute-start | bytes 786440 | tf_op jit(solution)/shard_map/ppermute | solution.py:428
  9.8 20.4 %copy-start.9 = (bf16[2,256,512]{2,1,0:T(8,128)(2,1)S(1)}, bf16[2,256,512]{2,1,0:T(8,128)(2,1)}, u32[]{:S(2)}) copy-start(bf16[2,256,512]{2,1,0:T(8,128)(2,1)} %constant.63.clone.pixels_ref) | copy-start | bytes 1572868
  9.8 20.4 %copy-start.11 = (bf16[2,4,128,128]{3,2,1,0:T(8,128)(2,1)S(1)}, bf16[2,4,128,128]{3,2,1,0:T(8,128)(2,1)}, u32[]{:S(2)}) copy-start(bf16[2,4,128,128]{3,2,1,0:T(8,128)(2,1)} %constant.61.clone.out_rows_ref) | copy-start | bytes 786436
  9.8 20.4 %copy-start.14 = (bf16[128,256]{1,0:T(8,128)(2,1)S(1)}, bf16[128,256]{1,0:T(8,128)(2,1)}, u32[]{:S(2)}) copy-start(bf16[128,256]{1,0:T(8,128)(2,1)} %constant.57.clone.unfold_ref) | copy-start | bytes 196612
  9.8 20.4 %copy-start.17 = (bf16[64,72]{1,0:T(8,128)(2,1)S(1)}, bf16[64,72]{1,0:T(8,128)(2,1)}, u32[]{:S(2)}) copy-start(bf16[64,72]{1,0:T(8,128)(2,1)} %constant.59.clone.flip_ref) | copy-start | bytes 27652
  9.8 6.6 %collective-permute-start.4 = (f32[72,128]{1,0:T(8,128)S(1)}, f32[72,128]{1,0:T(8,128)S(1)}, u32[]{:S(2)}, u32[]{:S(2)}) collective-permute-start(f32[72,128]{1,0:T(8,128)S(1)} %window_kernel.1.r0), channel_id=1, source_target_pairs={{0,3},{1,2},{2,1},{3,0},{4,7},{5,6},{6,5},{7,4},{8,11},{9,10},{10,... | collective-permute-start | bytes 110600 | tf_op jit(solution)/shard_map/ppermute | solution.py:432
  13.5 8.0 %collective-permute-start.3 = (f32[72,128]{1,0:T(8,128)S(1)}, f32[72,128]{1,0:T(8,128)S(1)}, u32[]{:S(2)}, u32[]{:S(2)}) collective-permute-start(f32[72,128]{1,0:T(8,128)S(1)} %window_kernel.1.r0), channel_id=1, source_target_pairs={{0,2},{1,3},{2,0},{3,1},{4,6},{5,7},{6,4},{7,5},{8,10},{9,11},{10,... | collective-permute-start | bytes 110600 | tf_op jit(solution)/shard_map/ppermute | solution.py:432
  14.5 7.0 %collective-permute-start.2 = (f32[72,128]{1,0:T(8,128)S(1)}, f32[72,128]{1,0:T(8,128)S(1)}, u32[]{:S(2)}, u32[]{:S(2)}) collective-permute-start(f32[72,128]{1,0:T(8,128)S(1)} %window_kernel.1.r0), channel_id=1, source_target_pairs={{0,1},{1,0},{2,3},{3,2},{4,5},{5,4},{6,7},{7,6},{8,9},{9,8},{10,11... | collective-permute-start | bytes 110600 | tf_op jit(solution)/shard_map/ppermute | solution.py:432
  16.4 9.6 %collective-permute-start.10 = (f32[2,2,128,128]{3,2,1,0:T(8,128)S(1)}, f32[2,2,128,128]{3,2,1,0:T(8,128)S(1)}, u32[]{:S(2)}, u32[]{:S(2)}) collective-permute-start(f32[2,2,128,128]{3,2,1,0:T(8,128)S(1)} %copy-done.1), channel_id=1, source_target_pairs={{0,8},{1,9},{2,10},{3,11},{4,12},{5,13},{6,14},{7,15},{8,0},{9,1},... | collective-permute-start | bytes 786440 | tf_op jit(solution)/shard_map/ppermute | solution.py:428
  21.8 5.6 %collective-permute-start.9 = (f32[144,128]{1,0:T(8,128)S(1)}, f32[144,128]{1,0:T(8,128)S(1)}, u32[]{:S(2)}, u32[]{:S(2)}) collective-permute-start(f32[144,128]{1,0:T(8,128)S(1)} %band_kernel.1.p0), channel_id=1, source_target_pairs={{0,12},{1,13},{2,14},{3,15},{4,8},{5,9},{6,10},{7,11},{8,4},{9,5},... | collective-permute-start | bytes 221192 | tf_op jit(solution)/shard_map/ppermute | solution.py:428
  24.1 5.9 %collective-permute-start.8 = (f32[144,128]{1,0:T(8,128)S(1)}, f32[144,128]{1,0:T(8,128)S(1)}, u32[]{:S(2)}, u32[]{:S(2)}) collective-permute-start(f32[144,128]{1,0:T(8,128)S(1)} %band_kernel.1.p0), channel_id=1, source_target_pairs={{0,8},{1,9},{2,10},{3,11},{4,12},{5,13},{6,14},{7,15},{8,0},{9,1},... | collective-permute-start | bytes 221192 | tf_op jit(solution)/shard_map/ppermute | solution.py:428
  25.8 4.4 %collective-permute-start.7 = (f32[144,128]{1,0:T(8,128)S(1)}, f32[144,128]{1,0:T(8,128)S(1)}, u32[]{:S(2)}, u32[]{:S(2)}) collective-permute-start(f32[144,128]{1,0:T(8,128)S(1)} %band_kernel.1.p0), channel_id=1, source_target_pairs={{0,4},{1,5},{2,6},{3,7},{4,0},{5,1},{6,2},{7,3},{8,12},{9,13},{10,... | collective-permute-start | bytes 221192 | tf_op jit(solution)/shard_map/ppermute | solution.py:428
  26.0 16.1 %copy-start.4 = (bf16[3,256,1024]{2,1,0:T(8,128)(2,1)S(1)}, bf16[3,256,1024]{2,1,0:T(8,128)(2,1)}, u32[]{:S(2)}) copy-start(bf16[3,256,1024]{2,1,0:T(8,128)(2,1)} %constant.65.clone.spread_ref) | copy-start | bytes 4718596
  26.0 16.1 %copy-start.5 = (bf16[2,1024,256]{2,1,0:T(8,128)(2,1)S(1)}, bf16[2,1024,256]{2,1,0:T(8,128)(2,1)}, u32[]{:S(2)}) copy-start(bf16[2,1024,256]{2,1,0:T(8,128)(2,1)} %constant.66.clone.spread_back_ref) | copy-start | bytes 3145732
  26.0 16.1 %copy-start.8 = (bf16[2,512,256]{2,1,0:T(8,128)(2,1)S(1)}, bf16[2,512,256]{2,1,0:T(8,128)(2,1)}, u32[]{:S(2)}) copy-start(bf16[2,512,256]{2,1,0:T(8,128)(2,1)} %constant.64.clone.pixels_back_ref) | copy-start | bytes 1572868
  26.0 16.2 %copy-start.10 = (bf16[2,4,128,128]{3,2,1,0:T(8,128)(2,1)S(1)}, bf16[2,4,128,128]{3,2,1,0:T(8,128)(2,1)}, u32[]{:S(2)}) copy-start(bf16[2,4,128,128]{3,2,1,0:T(8,128)(2,1)} %constant.62.clone.out_back_ref) | copy-start | bytes 786436
  26.0 16.2 %copy-start.13 = (bf16[256,128]{1,0:T(8,128)(2,1)S(1)}, bf16[256,128]{1,0:T(8,128)(2,1)}, u32[]{:S(2)}) copy-start(bf16[256,128]{1,0:T(8,128)(2,1)} %constant.58.clone.fold_ref) | copy-start | bytes 196612
  26.0 16.2 %copy-start.16 = (bf16[72,64]{1,0:T(8,128)(2,1)S(1)}, bf16[72,64]{1,0:T(8,128)(2,1)}, u32[]{:S(2)}) copy-start(bf16[72,64]{1,0:T(8,128)(2,1)} %constant.60.clone.flip_back_ref) | copy-start | bytes 27652
  31.5 10.3 %collective-permute-start.13 = (f32[64,256]{1,0:T(8,128)S(1)}, f32[64,256]{1,0:T(8,128)S(1)}, u32[]{:S(2)}, u32[]{:S(2)}) collective-permute-start(f32[64,256]{1,0:T(8,128)S(1)} %get-tuple-element.30.i0), channel_id=1, source_target_pairs={{0,2},{1,3},{2,0},{3,1},{4,6},{5,7},{6,4},{7,5},{8,10},{9,11},{10,... | collective-permute-start | bytes 196616 | tf_op jit(solution)/shard_map/ppermute | solution.py:432
  34.4 7.4 %collective-permute-start.12 = (f32[64,256]{1,0:T(8,128)S(1)}, f32[64,256]{1,0:T(8,128)S(1)}, u32[]{:S(2)}, u32[]{:S(2)}) collective-permute-start(f32[64,256]{1,0:T(8,128)S(1)} %get-tuple-element.30.i0), channel_id=1, source_target_pairs={{0,3},{1,2},{2,1},{3,0},{4,7},{5,6},{6,5},{7,4},{8,11},{9,10},{10,... | collective-permute-start | bytes 196616 | tf_op jit(solution)/shard_map/ppermute | solution.py:432
  36.6 5.5 %collective-permute-start.11 = (f32[64,256]{1,0:T(8,128)S(1)}, f32[64,256]{1,0:T(8,128)S(1)}, u32[]{:S(2)}, u32[]{:S(2)}) collective-permute-start(f32[64,256]{1,0:T(8,128)S(1)} %get-tuple-element.30.i0), channel_id=1, source_target_pairs={{0,1},{1,0},{2,3},{3,2},{4,5},{5,4},{6,7},{7,6},{8,9},{9,8},{10,11... | collective-permute-start | bytes 196616 | tf_op jit(solution)/shard_map/ppermute | solution.py:432
  42.1 10.9 %copy-start.7 = (bf16[2,128,1024]{2,1,0:T(8,128)(2,1)S(1)}, bf16[2,128,1024]{2,1,0:T(8,128)(2,1)}, u32[]{:S(2)}) copy-start(bf16[2,128,1024]{2,1,0:T(8,128)(2,1)} %constant.55.clone.band_back_ref) | copy-start | bytes 1572868
  42.2 10.9 %copy-start.15 = (f32[8,1024]{1,0:T(8,128)S(1)}, f32[8,1024]{1,0:T(8,128)}, u32[]{:S(2)}) copy-start(f32[8,1024]{1,0:T(8,128)} %constant.56.clone.edge_ref) | copy-start | bytes 98308
  44.3 4.8 %collective-permute-start.14 = (f32[176,128]{1,0:T(8,128)S(1)}, f32[176,128]{1,0:T(8,128)S(1)}, u32[]{:S(2)}, u32[]{:S(2)}) collective-permute-start(f32[176,128]{1,0:T(8,128)S(1)} %get-tuple-element.33), channel_id=1, source_target_pairs={{0,4},{1,5},{2,6},{3,7},{4,0},{5,1},{6,2},{7,3},{8,12},{9,13},{10,... | collective-permute-start | bytes 270344 | tf_op jit(solution)/shard_map/ppermute | solution.py:428
  45.0 6.0 %collective-permute-start.15 = (f32[176,128]{1,0:T(8,128)S(1)}, f32[176,128]{1,0:T(8,128)S(1)}, u32[]{:S(2)}, u32[]{:S(2)}) collective-permute-start(f32[176,128]{1,0:T(8,128)S(1)} %get-tuple-element.34), channel_id=1, source_target_pairs={{0,8},{1,9},{2,10},{3,11},{4,12},{5,13},{6,14},{7,15},{8,0},{9,1},... | collective-permute-start | bytes 270344 | tf_op jit(solution)/shard_map/ppermute | solution.py:428
  47.3 5.7 %collective-permute-start.16 = (f32[176,128]{1,0:T(8,128)S(1)}, f32[176,128]{1,0:T(8,128)S(1)}, u32[]{:S(2)}, u32[]{:S(2)}) collective-permute-start(f32[176,128]{1,0:T(8,128)S(1)} %get-tuple-element.35), channel_id=1, source_target_pairs={{0,12},{1,13},{2,14},{3,15},{4,8},{5,9},{6,10},{7,11},{8,4},{9,5},... | collective-permute-start | bytes 270344 | tf_op jit(solution)/shard_map/ppermute | solution.py:428
  53.4 7.4 %collective-permute-start.17 = (f32[72,128]{1,0:T(8,128)S(1)}, f32[72,128]{1,0:T(8,128)S(1)}, u32[]{:S(2)}, u32[]{:S(2)}) collective-permute-start(f32[72,128]{1,0:T(8,128)S(1)} %get-tuple-element.36), channel_id=1, source_target_pairs={{0,1},{1,0},{2,3},{3,2},{4,5},{5,4},{6,7},{7,6},{8,9},{9,8},{10,11... | collective-permute-start | bytes 110600 | tf_op jit(solution)/shard_map/ppermute | solution.py:432
  54.5 7.9 %collective-permute-start.18 = (f32[72,128]{1,0:T(8,128)S(1)}, f32[72,128]{1,0:T(8,128)S(1)}, u32[]{:S(2)}, u32[]{:S(2)}) collective-permute-start(f32[72,128]{1,0:T(8,128)S(1)} %get-tuple-element.40), channel_id=1, source_target_pairs={{0,2},{1,3},{2,0},{3,1},{4,6},{5,7},{6,4},{7,5},{8,10},{9,11},{10,... | collective-permute-start | bytes 110600 | tf_op jit(solution)/shard_map/ppermute | solution.py:432
  58.0 6.3 %collective-permute-start.19 = (f32[72,128]{1,0:T(8,128)S(1)}, f32[72,128]{1,0:T(8,128)S(1)}, u32[]{:S(2)}, u32[]{:S(2)}) collective-permute-start(f32[72,128]{1,0:T(8,128)S(1)} %get-tuple-element.41), channel_id=1, source_target_pairs={{0,3},{1,2},{2,1},{3,0},{4,7},{5,6},{6,5},{7,4},{8,11},{9,10},{10,... | collective-permute-start | bytes 110600 | tf_op jit(solution)/shard_map/ppermute | solution.py:432
  64.3 5.6 %collective-permute-start.21 = (f32[72,128]{1,0:T(8,128)S(1)}, f32[72,128]{1,0:T(8,128)S(1)}, u32[]{:S(2)}, u32[]{:S(2)}) collective-permute-start(f32[72,128]{1,0:T(8,128)S(1)} %add_add_fusion.own_ref), channel_id=1, source_target_pairs={{0,240},{16,32},{32,16},{48,64},{64,48},{80,96},{96,80},{112,128},... | collective-permute-start | bytes 110600 | tf_op jit(solution)/shard_map/ppermute | solution.py:440
  64.5 5.4 %collective-permute-start.20 = (f32[72,128]{1,0:T(8,128)S(1)}, f32[72,128]{1,0:T(8,128)S(1)}, u32[]{:S(2)}, u32[]{:S(2)}) collective-permute-start(f32[72,128]{1,0:T(8,128)S(1)} %add_add_fusion.own_ref), channel_id=1, source_target_pairs={{0,16},{16,0},{32,48},{48,32},{64,80},{80,64},{96,112},{112,96},{1... | collective-permute-start | bytes 110600 | tf_op jit(solution)/shard_map/ppermute | solution.py:436

commit v8 on v7

--- a/solution.py
+++ b/solution.py
@@ -383,7 +383,7 @@
     resist_ref[...] = jnp.concatenate(spots, 1)
 
 
-def final_kernel(inner_ref, outer_ref, own_ref, rows_ref, out_ref):
+def final_kernel(inner_ref, outer_ref, own_ref, rows_ref, out_hbm, out_ref, sems):
     above, below = neighbours(outer_ref[...], inner_ref[...])
     own = own_ref[...]
     sign = 2.0 * alternate(own.shape)
@@ -392,6 +392,7 @@
         own + above * sign,
         own + below * sign,
     )
+    copies = []
     for slot, side in enumerate(sides):
         side = split(jnp.concatenate([side, jnp.zeros((ROOM - HALF, 2 * SHARD), F32)], 0).T)
         cols = slice(slot * HALO, (slot + 1) * HALO)
@@ -402,10 +403,18 @@
                 tuple(rows_ref[i, half * ROOM : (half + 1) * ROOM, cols] for i in range(2)),
             )
             total = part if total is None else total + part
-        out_ref[:, cols] = total
-
-
-def call(kernel, shapes, *operands, flops=4 * 10**9, smem=(), hbm=(), scratch=()):
+        out_ref[slot] = total
+        copies.append(
+            pltpu.make_async_copy(out_ref.at[slot], out_hbm.at[:, cols], sems.at[slot])
+        )
+        copies[-1].start()
+    for copy in copies:
+        copy.wait()
+
+
+def call(
+    kernel, shapes, *operands, flops=4 * 10**9, smem=(), hbm=(), scratch=(), out_space=pltpu.VMEM
+):
     many = isinstance(shapes, list)
     space = lambda i: pltpu.SMEM if i in smem else pltpu.HBM if i in hbm else pltpu.VMEM
     spec = lambda i: pl.BlockSpec(memory_space=space(i))
@@ -417,7 +426,7 @@
         in_specs=[spec(i) for i in range(len(operands))],
         out_specs=[pl.BlockSpec(memory_space=pltpu.VMEM)] * len(out)
         if many
-        else pl.BlockSpec(memory_space=pltpu.VMEM),
+        else pl.BlockSpec(memory_space=out_space),
         compiler_params=pltpu.CompilerParams(vmem_limit_bytes=32 * 2**20),
         cost_estimate=pl.CostEstimate(flops=flops, bytes_accessed=10**6, transcendentals=0),
         name=kernel.__name__,
@@ -489,6 +498,8 @@
     mask_grad = call(
         final_kernel, (SHARD, TILE), swap_inner(grad), swap_outer(grad), grad,
         table["rows"],
+        scratch=[pltpu.VMEM((2, SHARD, HALO), F32), pltpu.SemaphoreType.DMA((2,))],
+        out_space=pltpu.HBM,
     )
     return (resist.T, mask_grad.T)
 

time: 71.6 us -> 71.8 us (level)
  no operation moved by 1% of the time
where the time goes in v8:
time: 71.8 us; the launch traced here: 70.9 us
  starting transfers between devices  38.2 us (53%)
  waiting for transfers between devices  24.3 us (34%)
  Pallas kernels  6.67 us (9%)
  between operations  1.04 us (1%)
  local copies, waits for them, and re-layouts  0.77 us (1%)
    ppermute x9, starting transfers between devices, swap_z(): return lax.ppermute(value, 'kern', [(i, i ^ step) for i in range(16)])  19.7 us
    ppermute x9, starting transfers between devices, swap_y(): return lax.ppermute(value, 'kern', [(i, i ^ 4 * step) for i in range(16)])  13.7 us
    ppermute x9, waiting for transfers between devices, swap_z(): return lax.ppermute(value, 'kern', [(i, i ^ step) for i in range(16)])  11 us
    ppermute x9, waiting for transfers between devices, swap_y(): return lax.ppermute(value, 'kern', [(i, i ^ 4 * step) for i in range(16)])  8.1 us
    pallas_call x8, Pallas kernels, call(): pl.pallas_call(kernel, scratch_shapes=list(scratch), out_shape=out if man...  6.67 us
    ppermute x2, waiting for transfers between devices, swap_outer(): lax.ppermute(value, 'tile', [(i, (i + 1 ^ 1) - 1 & 15) for i in range(16)])  5.19 us
    ppermute x2, starting transfers between devices, swap_outer(): lax.ppermute(value, 'tile', [(i, (i + 1 ^ 1) - 1 & 15) for i in range(16)])  4.43 us
  transfers between devices with their start and end apart: 22, of which 11 were waited for; matrix products, arithmetic and copies ran while one was open for 0% of the time, Pallas kernels for 3%

profile of v8, /device:TPU:64, one launch (start us, length us, event | category | flops | bytes accessed | tf_op | source)
XLA Modules:
  0.0 70.9 jit_solution(11520875758990738734)
XLA Ops:
  0.6 0.0 copy-start
  0.7 0.1 collective-permute-start.1
  0.8 4.2 %collective-permute-start = (f32[64,256]{1,0:T(8,128)}, f32[64,256]{1,0:T(8,128)S(1)}, u32[]{:S(2)}, u32[]{:S(2)}) collective-permute-start(f32[64,256]{1,0:T(8,128)} %bitcast.4), channel_id=1, source_target_pairs={{0,240},{16,32},{32,16},{48,64},{64,48},{80,96},{96,80},{112,128},... | collective-permute-start | bytes 196616 | tf_op jit(solution)/shard_map/ppermute | solution.py:449
  5.0 0.7 copy-done.3
  5.6 0.5 weight_kernel.1.heavy_ref
  6.2 0.0 copy-start.6
  6.2 3.1 %collective-permute-start.6 = (f32[2,2,128,128]{3,2,1,0:T(8,128)S(1)}, f32[2,2,128,128]{3,2,1,0:T(8,128)S(1)}, u32[]{:S(2)}, u32[]{:S(2)}) collective-permute-start(f32[2,2,128,128]{3,2,1,0:T(8,128)S(1)} %copy-done.1), channel_id=1, source_target_pairs={{0,12},{1,13},{2,14},{3,15},{4,8},{5,9},{6,10},{7,11},{8,4},{9,5},... | collective-permute-start | bytes 786440 | tf_op jit(solution)/shard_map/ppermute | solution.py:437
  9.3 0.1 collective-permute-start.5
  9.5 0.3 window_kernel.1.r0
  9.8 0.0 copy-start.9
  9.8 0.0 copy-start.14
  9.8 0.0 copy-start.17
  9.8 3.7 %collective-permute-start.4 = (f32[72,128]{1,0:T(8,128)S(1)}, f32[72,128]{1,0:T(8,128)S(1)}, u32[]{:S(2)}, u32[]{:S(2)}) collective-permute-start(f32[72,128]{1,0:T(8,128)S(1)} %window_kernel.1.r0), channel_id=1, source_target_pairs={{0,3},{1,2},{2,1},{3,0},{4,7},{5,6},{6,5},{7,4},{8,11},{9,10},{10,... | collective-permute-start | bytes 110600 | tf_op jit(solution)/shard_map/ppermute | solution.py:441
  13.5 1.0 %collective-permute-start.3 = (f32[72,128]{1,0:T(8,128)S(1)}, f32[72,128]{1,0:T(8,128)S(1)}, u32[]{:S(2)}, u32[]{:S(2)}) collective-permute-start(f32[72,128]{1,0:T(8,128)S(1)} %window_kernel.1.r0), channel_id=1, source_target_pairs={{0,2},{1,3},{2,0},{3,1},{4,6},{5,7},{6,4},{7,5},{8,10},{9,11},{10,... | collective-permute-start | bytes 110600 | tf_op jit(solution)/shard_map/ppermute | solution.py:441
  14.5 1.9 %collective-permute-start.2 = (f32[72,128]{1,0:T(8,128)S(1)}, f32[72,128]{1,0:T(8,128)S(1)}, u32[]{:S(2)}, u32[]{:S(2)}) collective-permute-start(f32[72,128]{1,0:T(8,128)S(1)} %window_kernel.1.r0), channel_id=1, source_target_pairs={{0,1},{1,0},{2,3},{3,2},{4,5},{5,4},{6,7},{7,6},{8,9},{9,8},{10,11... | collective-permute-start | bytes 110600 | tf_op jit(solution)/shard_map/ppermute | solution.py:441
  16.4 1.5 %collective-permute-start.10 = (f32[2,2,128,128]{3,2,1,0:T(8,128)S(1)}, f32[2,2,128,128]{3,2,1,0:T(8,128)S(1)}, u32[]{:S(2)}, u32[]{:S(2)}) collective-permute-start(f32[2,2,128,128]{3,2,1,0:T(8,128)S(1)} %copy-done.1), channel_id=1, source_target_pairs={{0,8},{1,9},{2,10},{3,11},{4,12},{5,13},{6,14},{7,15},{8,0},{9,1},... | collective-permute-start | bytes 786440 | tf_op jit(solution)/shard_map/ppermute | solution.py:437
  18.0 3.5 %collective-permute-done.3.r2 = f32[72,128]{1,0:T(8,128)S(1)} collective-permute-done((f32[72,128]{1,0:T(8,128)S(1)}, f32[72,128]{1,0:T(8,128)S(1)}, u32[]{:S(2)}, u32[]{:S(2)}) %collective-permute-start.3) | collective-permute-done | bytes 36896 | tf_op jit(solution)/shard_map/ppermute | solution.py:441
  21.5 0.3 band_kernel.1.p0
  21.8 2.3 %collective-permute-start.9 = (f32[144,128]{1,0:T(8,128)S(1)}, f32[144,128]{1,0:T(8,128)S(1)}, u32[]{:S(2)}, u32[]{:S(2)}) collective-permute-start(f32[144,128]{1,0:T(8,128)S(1)} %band_kernel.1.p0), channel_id=1, source_target_pairs={{0,12},{1,13},{2,14},{3,15},{4,8},{5,9},{6,10},{7,11},{8,4},{9,5},... | collective-permute-start | bytes 221192 | tf_op jit(solution)/shard_map/ppermute | solution.py:437
  24.1 1.7 %collective-permute-start.8 = (f32[144,128]{1,0:T(8,128)S(1)}, f32[144,128]{1,0:T(8,128)S(1)}, u32[]{:S(2)}, u32[]{:S(2)}) collective-permute-start(f32[144,128]{1,0:T(8,128)S(1)} %band_kernel.1.p0), channel_id=1, source_target_pairs={{0,8},{1,9},{2,10},{3,11},{4,12},{5,13},{6,14},{7,15},{8,0},{9,1},... | collective-permute-start | bytes 221192 | tf_op jit(solution)/shard_map/ppermute | solution.py:437
  25.8 0.1 collective-permute-start.7
  26.0 0.0 copy-start.13
  26.0 1.4 %collective-permute-done.9.p3 = f32[144,128]{1,0:T(8,128)S(1)} collective-permute-done((f32[144,128]{1,0:T(8,128)S(1)}, f32[144,128]{1,0:T(8,128)S(1)}, u32[]{:S(2)}, u32[]{:S(2)}) %collective-permute-start.9) | collective-permute-done | bytes 73760 | tf_op jit(solution)/shard_map/ppermute | solution.py:437
  27.4 2.6 %collective-permute-done.8.p2 = f32[144,128]{1,0:T(8,128)S(1)} collective-permute-done((f32[144,128]{1,0:T(8,128)S(1)}, f32[144,128]{1,0:T(8,128)S(1)}, u32[]{:S(2)}, u32[]{:S(2)}) %collective-permute-start.8) | collective-permute-done | bytes 73760 | tf_op jit(solution)/shard_map/ppermute | solution.py:437
  30.0 0.2 collective-permute-done.7.p1
  30.2 1.3 %aerial_kernel.1 = (f32[512,512]{1,0:T(8,128)S(1)}, f32[64,256]{1,0:T(8,128)S(1)}) custom-call(f32[144,128]{1,0:T(8,128)S(1)} %band_kernel.1.p0, f32[144,128]{1,0:T(8,128)S(1)} %collective-permute-done.7.p1, f32[144,128]{1,0:T(8,128)S(1)} %collective-permute-done.8.p2, f32[144,128]{1,0:T(8,128)S(1)} %collective-permute-done.9.p3, ...), custom_call_target="tpu_custom_call" | custom-call | flops 4000000000 | bytes 1000000 | tf_op jit(solution)/shard_map/aerial_kernel/pallas_call | solution.py:422
  31.5 2.9 %collective-permute-start.13 = (f32[64,256]{1,0:T(8,128)S(1)}, f32[64,256]{1,0:T(8,128)S(1)}, u32[]{:S(2)}, u32[]{:S(2)}) collective-permute-start(f32[64,256]{1,0:T(8,128)S(1)} %get-tuple-element.30.i0), channel_id=1, source_target_pairs={{0,2},{1,3},{2,0},{3,1},{4,6},{5,7},{6,4},{7,5},{8,10},{9,11},{10,... | collective-permute-start | bytes 196616 | tf_op jit(solution)/shard_map/ppermute | solution.py:441
  34.4 2.2 %collective-permute-start.12 = (f32[64,256]{1,0:T(8,128)S(1)}, f32[64,256]{1,0:T(8,128)S(1)}, u32[]{:S(2)}, u32[]{:S(2)}) collective-permute-start(f32[64,256]{1,0:T(8,128)S(1)} %get-tuple-element.30.i0), channel_id=1, source_target_pairs={{0,3},{1,2},{2,1},{3,0},{4,7},{5,6},{6,5},{7,4},{8,11},{9,10},{10,... | collective-permute-start | bytes 196616 | tf_op jit(solution)/shard_map/ppermute | solution.py:441
  36.6 1.5 %collective-permute-start.11 = (f32[64,256]{1,0:T(8,128)S(1)}, f32[64,256]{1,0:T(8,128)S(1)}, u32[]{:S(2)}, u32[]{:S(2)}) collective-permute-start(f32[64,256]{1,0:T(8,128)S(1)} %get-tuple-element.30.i0), channel_id=1, source_target_pairs={{0,1},{1,0},{2,3},{3,2},{4,5},{5,4},{6,7},{7,6},{8,9},{9,8},{10,11... | collective-permute-start | bytes 196616 | tf_op jit(solution)/shard_map/ppermute | solution.py:441
  38.1 3.7 %collective-permute-done.13.i3 = f32[64,256]{1,0:T(8,128)S(1)} collective-permute-done((f32[64,256]{1,0:T(8,128)S(1)}, f32[64,256]{1,0:T(8,128)S(1)}, u32[]{:S(2)}, u32[]{:S(2)}) %collective-permute-start.13) | collective-permute-done | bytes 65568 | tf_op jit(solution)/shard_map/ppermute | solution.py:441
  41.8 0.3 collective-permute-done.11.i1
  42.2 2.2 %slope_kernel.1 = (f32[176,128]{1,0:T(8,128)S(1)}, f32[176,128]{1,0:T(8,128)S(1)}, f32[176,128]{1,0:T(8,128)S(1)}, f32[176,128]{1,0:T(8,128)S(1)}) custom-call(f32[64,256]{1,0:T(8,128)S(1)} %get-tuple-element.30.i0, f32[64,256]{1,0:T(8,128)S(1)} %collective-permute-done.11.i1, f32[64,256]{1,0:T(8,128)S(1)} %collective-permute-done.12.i2, ...), custom_call_target="tpu_custom_call" | custom-call | flops 4000000000 | bytes 1000000 | tf_op jit(solution)/shard_map/slope_kernel/pallas_call | solution.py:422
  44.3 0.6 collective-permute-start.14
  45.0 2.4 %collective-permute-start.15 = (f32[176,128]{1,0:T(8,128)S(1)}, f32[176,128]{1,0:T(8,128)S(1)}, u32[]{:S(2)}, u32[]{:S(2)}) collective-permute-start(f32[176,128]{1,0:T(8,128)S(1)} %get-tuple-element.34), channel_id=1, source_target_pairs={{0,8},{1,9},{2,10},{3,11},{4,12},{5,13},{6,14},{7,15},{8,0},{9,1},... | collective-permute-start | bytes 270344 | tf_op jit(solution)/shard_map/ppermute | solution.py:437
  47.3 1.8 %collective-permute-start.16 = (f32[176,128]{1,0:T(8,128)S(1)}, f32[176,128]{1,0:T(8,128)S(1)}, u32[]{:S(2)}, u32[]{:S(2)}) collective-permute-start(f32[176,128]{1,0:T(8,128)S(1)} %get-tuple-element.35), channel_id=1, source_target_pairs={{0,12},{1,13},{2,14},{3,15},{4,8},{5,9},{6,10},{7,11},{8,4},{9,5},... | collective-permute-start | bytes 270344 | tf_op jit(solution)/shard_map/ppermute | solution.py:437
  49.1 1.9 %collective-permute-done.15.m2 = f32[176,128]{1,0:T(8,128)S(1)} collective-permute-done((f32[176,128]{1,0:T(8,128)S(1)}, f32[176,128]{1,0:T(8,128)S(1)}, u32[]{:S(2)}, u32[]{:S(2)}) %collective-permute-start.15) | collective-permute-done | bytes 90144 | tf_op jit(solution)/shard_map/ppermute | solution.py:437
  51.0 2.1 %collective-permute-done.16.m3 = f32[176,128]{1,0:T(8,128)S(1)} collective-permute-done((f32[176,128]{1,0:T(8,128)S(1)}, f32[176,128]{1,0:T(8,128)S(1)}, u32[]{:S(2)}, u32[]{:S(2)}) %collective-permute-start.16) | collective-permute-done | bytes 90144 | tf_op jit(solution)/shard_map/ppermute | solution.py:437
  53.1 0.3 columns_kernel.1
  53.4 1.1 %collective-permute-start.17 = (f32[72,128]{1,0:T(8,128)S(1)}, f32[72,128]{1,0:T(8,128)S(1)}, u32[]{:S(2)}, u32[]{:S(2)}) collective-permute-start(f32[72,128]{1,0:T(8,128)S(1)} %get-tuple-element.36), channel_id=1, source_target_pairs={{0,1},{1,0},{2,3},{3,2},{4,5},{5,4},{6,7},{7,6},{8,9},{9,8},{10,11... | collective-permute-start | bytes 110600 | tf_op jit(solution)/shard_map/ppermute | solution.py:441
  54.5 3.5 %collective-permute-start.18 = (f32[72,128]{1,0:T(8,128)S(1)}, f32[72,128]{1,0:T(8,128)S(1)}, u32[]{:S(2)}, u32[]{:S(2)}) collective-permute-start(f32[72,128]{1,0:T(8,128)S(1)} %get-tuple-element.40), channel_id=1, source_target_pairs={{0,2},{1,3},{2,0},{3,1},{4,6},{5,7},{6,4},{7,5},{8,10},{9,11},{10,... | collective-permute-start | bytes 110600 | tf_op jit(solution)/shard_map/ppermute | solution.py:441
  58.0 2.0 %collective-permute-start.19 = (f32[72,128]{1,0:T(8,128)S(1)}, f32[72,128]{1,0:T(8,128)S(1)}, u32[]{:S(2)}, u32[]{:S(2)}) collective-permute-start(f32[72,128]{1,0:T(8,128)S(1)} %get-tuple-element.41), channel_id=1, source_target_pairs={{0,3},{1,2},{2,1},{3,0},{4,7},{5,6},{6,5},{7,4},{8,11},{9,10},{10,... | collective-permute-start | bytes 110600 | tf_op jit(solution)/shard_map/ppermute | solution.py:441
  60.0 0.8 %resist_kernel.1 = f32[64,256]{1,0:T(8,128)} custom-call(f32[176,128]{1,0:T(8,128)S(1)} %get-tuple-element.32.m0, f32[176,128]{1,0:T(8,128)S(1)} %collective-permute-done.14.m1, f32[176,128]{1,0:T(8,128)S(1)} %collective-permute-done.15.m2, f32[176,128]{1,0:T(8,128)S(1)} %collective-permute-done.16.m3), custom_call_target="tpu_custom_call" | custom-call | flops 4000000000 | bytes 1000000 | tf_op jit(solution)/shard_map/resist_kernel/pallas_call | solution.py:422
  60.8 1.6 %collective-permute-done.18 = f32[72,128]{1,0:T(8,128)S(1)} collective-permute-done((f32[72,128]{1,0:T(8,128)S(1)}, f32[72,128]{1,0:T(8,128)S(1)}, u32[]{:S(2)}, u32[]{:S(2)}) %collective-permute-start.18) | collective-permute-done | bytes 36896 | tf_op jit(solution)/shard_map/ppermute | solution.py:441
  62.3 1.9 %collective-permute-done.19 = f32[72,128]{1,0:T(8,128)S(1)} collective-permute-done((f32[72,128]{1,0:T(8,128)S(1)}, f32[72,128]{1,0:T(8,128)S(1)}, u32[]{:S(2)}, u32[]{:S(2)}) %collective-permute-start.19) | collective-permute-done | bytes 36896 | tf_op jit(solution)/shard_map/ppermute | solution.py:441
  64.3 0.2 collective-permute-start.21
  64.5 0.2 collective-permute-start.20
  64.6 5.2 %collective-permute-done.21.outer_ref = f32[72,128]{1,0:T(8,128)S(1)} collective-permute-done((f32[72,128]{1,0:T(8,128)S(1)}, f32[72,128]{1,0:T(8,128)S(1)}, u32[]{:S(2)}, u32[]{:S(2)}) %collective-permute-start.21) | collective-permute-done | bytes 36896 | tf_op jit(solution)/shard_map/ppermute | solution.py:449
  69.8 0.9 %final_kernel.1 = f32[64,256]{1,0:T(8,128)} custom-call(f32[72,128]{1,0:T(8,128)S(1)} %collective-permute-done.20.inner_ref, f32[72,128]{1,0:T(8,128)S(1)} %collective-permute-done.21.outer_ref, f32[72,128]{1,0:T(8,128)S(1)} %add_add_fusion.own_ref, bf16[2,160,256]{2,1,0:T(8,128)(2,1)S(1)} %copy-done.12), custom_call_target="tpu_custom_call" | custom-call | flops 4000000000 | bytes 1000000 | tf_op jit(solution)/shard_map/final_kernel/pallas_call | solution.py:422
  (42 shorter events, 0.1 us)
Async XLA Ops:
  0.6 37.5 %copy-start = (s32[256,1024]{1,0:T(8,128)S(1)}, s32[256,1024]{1,0:T(8,128)}, u32[]{:S(2)}) copy-start(s32[256,1024]{1,0:T(8,128)} %param.19) | copy-start | bytes 3145732
  0.6 5.5 %copy-start.1 = (f32[2,2,128,128]{3,2,1,0:T(8,128)S(1)}, f32[2,2,128,128]{3,2,1,0:T(8,128)}, u32[]{:S(2)}) copy-start(f32[2,2,128,128]{3,2,1,0:T(8,128)} %h0.1) | copy-start | bytes 786436
  0.7 8.8 %copy-start.2 = (f32[256,64]{0,1:T(8,128)S(1)}, f32[256,64]{0,1:T(8,128)}, u32[]{:S(2)}) copy-start(f32[256,64]{0,1:T(8,128)} %param.18) | copy-start | bytes 196612
  0.7 8.8 %collective-permute-start.1 = (f32[64,256]{1,0:T(8,128)}, f32[64,256]{1,0:T(8,128)S(1)}, u32[]{:S(2)}, u32[]{:S(2)}) collective-permute-start(f32[64,256]{1,0:T(8,128)} %bitcast.3), channel_id=1, source_target_pairs={{0,16},{16,0},{32,48},{48,32},{64,80},{80,64},{96,112},{112,96},{1... | collective-permute-start | bytes 196616 | tf_op jit(solution)/shard_map/ppermute | solution.py:445
  0.8 8.7 %collective-permute-start = (f32[64,256]{1,0:T(8,128)}, f32[64,256]{1,0:T(8,128)S(1)}, u32[]{:S(2)}, u32[]{:S(2)}) collective-permute-start(f32[64,256]{1,0:T(8,128)} %bitcast.4), channel_id=1, source_target_pairs={{0,240},{16,32},{32,16},{48,64},{64,48},{80,96},{96,80},{112,128},... | collective-permute-start | bytes 196616 | tf_op jit(solution)/shard_map/ppermute | solution.py:449
  5.0 0.7 copy-start.3
  5.6 3.8 %copy-start.12 = (bf16[2,160,256]{2,1,0:T(8,128)(2,1)S(1)}, bf16[2,160,256]{2,1,0:T(8,128)(2,1)}, u32[]{:S(2)}) copy-start(bf16[2,160,256]{2,1,0:T(8,128)(2,1)} %constant.53.clone.rows_ref) | copy-start | bytes 491524
  6.2 15.3 %copy-start.6 = (bf16[2,16,64,256]{3,2,1,0:T(8,128)(2,1)S(1)}, bf16[2,16,64,256]{3,2,1,0:T(8,128)(2,1)}, u32[]{:S(2)}) copy-start(bf16[2,16,64,256]{3,2,1,0:T(8,128)(2,1)} %constant.54.clone.band_ref) | copy-start | bytes 3145732
  6.2 15.3 %collective-permute-start.6 = (f32[2,2,128,128]{3,2,1,0:T(8,128)S(1)}, f32[2,2,128,128]{3,2,1,0:T(8,128)S(1)}, u32[]{:S(2)}, u32[]{:S(2)}) collective-permute-start(f32[2,2,128,128]{3,2,1,0:T(8,128)S(1)} %copy-done.1), channel_id=1, source_target_pairs={{0,12},{1,13},{2,14},{3,15},{4,8},{5,9},{6,10},{7,11},{8,4},{9,5},... | collective-permute-start | bytes 786440 | tf_op jit(solution)/shard_map/ppermute | solution.py:437
  9.3 12.2 %collective-permute-start.5 = (f32[2,2,128,128]{3,2,1,0:T(8,128)S(1)}, f32[2,2,128,128]{3,2,1,0:T(8,128)S(1)}, u32[]{:S(2)}, u32[]{:S(2)}) collective-permute-start(f32[2,2,128,128]{3,2,1,0:T(8,128)S(1)} %copy-done.1), channel_id=1, source_target_pairs={{0,4},{1,5},{2,6},{3,7},{4,0},{5,1},{6,2},{7,3},{8,12},{9,13},{10,... | collective-permute-start | bytes 786440 | tf_op jit(solution)/shard_map/ppermute | solution.py:437
  9.8 20.4 %copy-start.9 = (bf16[2,256,512]{2,1,0:T(8,128)(2,1)S(1)}, bf16[2,256,512]{2,1,0:T(8,128)(2,1)}, u32[]{:S(2)}) copy-start(bf16[2,256,512]{2,1,0:T(8,128)(2,1)} %constant.63.clone.pixels_ref) | copy-start | bytes 1572868
  9.8 20.4 %copy-start.11 = (bf16[2,4,128,128]{3,2,1,0:T(8,128)(2,1)S(1)}, bf16[2,4,128,128]{3,2,1,0:T(8,128)(2,1)}, u32[]{:S(2)}) copy-start(bf16[2,4,128,128]{3,2,1,0:T(8,128)(2,1)} %constant.61.clone.out_rows_ref) | copy-start | bytes 786436
  9.8 20.4 %copy-start.14 = (bf16[128,256]{1,0:T(8,128)(2,1)S(1)}, bf16[128,256]{1,0:T(8,128)(2,1)}, u32[]{:S(2)}) copy-start(bf16[128,256]{1,0:T(8,128)(2,1)} %constant.57.clone.unfold_ref) | copy-start | bytes 196612
  9.8 20.4 %copy-start.17 = (bf16[64,72]{1,0:T(8,128)(2,1)S(1)}, bf16[64,72]{1,0:T(8,128)(2,1)}, u32[]{:S(2)}) copy-start(bf16[64,72]{1,0:T(8,128)(2,1)} %constant.59.clone.flip_ref) | copy-start | bytes 27652
  9.8 6.6 %collective-permute-start.4 = (f32[72,128]{1,0:T(8,128)S(1)}, f32[72,128]{1,0:T(8,128)S(1)}, u32[]{:S(2)}, u32[]{:S(2)}) collective-permute-start(f32[72,128]{1,0:T(8,128)S(1)} %window_kernel.1.r0), channel_id=1, source_target_pairs={{0,3},{1,2},{2,1},{3,0},{4,7},{5,6},{6,5},{7,4},{8,11},{9,10},{10,... | collective-permute-start | bytes 110600 | tf_op jit(solution)/shard_map/ppermute | solution.py:441
  13.5 8.0 %collective-permute-start.3 = (f32[72,128]{1,0:T(8,128)S(1)}, f32[72,128]{1,0:T(8,128)S(1)}, u32[]{:S(2)}, u32[]{:S(2)}) collective-permute-start(f32[72,128]{1,0:T(8,128)S(1)} %window_kernel.1.r0), channel_id=1, source_target_pairs={{0,2},{1,3},{2,0},{3,1},{4,6},{5,7},{6,4},{7,5},{8,10},{9,11},{10,... | collective-permute-start | bytes 110600 | tf_op jit(solution)/shard_map/ppermute | solution.py:441
  14.5 7.0 %collective-permute-start.2 = (f32[72,128]{1,0:T(8,128)S(1)}, f32[72,128]{1,0:T(8,128)S(1)}, u32[]{:S(2)}, u32[]{:S(2)}) collective-permute-start(f32[72,128]{1,0:T(8,128)S(1)} %window_kernel.1.r0), channel_id=1, source_target_pairs={{0,1},{1,0},{2,3},{3,2},{4,5},{5,4},{6,7},{7,6},{8,9},{9,8},{10,11... | collective-permute-start | bytes 110600 | tf_op jit(solution)/shard_map/ppermute | solution.py:441
  16.4 9.6 %collective-permute-start.10 = (f32[2,2,128,128]{3,2,1,0:T(8,128)S(1)}, f32[2,2,128,128]{3,2,1,0:T(8,128)S(1)}, u32[]{:S(2)}, u32[]{:S(2)}) collective-permute-start(f32[2,2,128,128]{3,2,1,0:T(8,128)S(1)} %copy-done.1), channel_id=1, source_target_pairs={{0,8},{1,9},{2,10},{3,11},{4,12},{5,13},{6,14},{7,15},{8,0},{9,1},... | collective-permute-start | bytes 786440 | tf_op jit(solution)/shard_map/ppermute | solution.py:437
  21.8 5.6 %collective-permute-start.9 = (f32[144,128]{1,0:T(8,128)S(1)}, f32[144,128]{1,0:T(8,128)S(1)}, u32[]{:S(2)}, u32[]{:S(2)}) collective-permute-start(f32[144,128]{1,0:T(8,128)S(1)} %band_kernel.1.p0), channel_id=1, source_target_pairs={{0,12},{1,13},{2,14},{3,15},{4,8},{5,9},{6,10},{7,11},{8,4},{9,5},... | collective-permute-start | bytes 221192 | tf_op jit(solution)/shard_map/ppermute | solution.py:437
  24.1 5.9 %collective-permute-start.8 = (f32[144,128]{1,0:T(8,128)S(1)}, f32[144,128]{1,0:T(8,128)S(1)}, u32[]{:S(2)}, u32[]{:S(2)}) collective-permute-start(f32[144,128]{1,0:T(8,128)S(1)} %band_kernel.1.p0), channel_id=1, source_target_pairs={{0,8},{1,9},{2,10},{3,11},{4,12},{5,13},{6,14},{7,15},{8,0},{9,1},... | collective-permute-start | bytes 221192 | tf_op jit(solution)/shard_map/ppermute | solution.py:437
  25.8 4.4 %collective-permute-start.7 = (f32[144,128]{1,0:T(8,128)S(1)}, f32[144,128]{1,0:T(8,128)S(1)}, u32[]{:S(2)}, u32[]{:S(2)}) collective-permute-start(f32[144,128]{1,0:T(8,128)S(1)} %band_kernel.1.p0), channel_id=1, source_target_pairs={{0,4},{1,5},{2,6},{3,7},{4,0},{5,1},{6,2},{7,3},{8,12},{9,13},{10,... | collective-permute-start | bytes 221192 | tf_op jit(solution)/shard_map/ppermute | solution.py:437
  26.0 16.1 %copy-start.4 = (bf16[3,256,1024]{2,1,0:T(8,128)(2,1)S(1)}, bf16[3,256,1024]{2,1,0:T(8,128)(2,1)}, u32[]{:S(2)}) copy-start(bf16[3,256,1024]{2,1,0:T(8,128)(2,1)} %constant.65.clone.spread_ref) | copy-start | bytes 4718596
  26.0 16.1 %copy-start.5 = (bf16[2,1024,256]{2,1,0:T(8,128)(2,1)S(1)}, bf16[2,1024,256]{2,1,0:T(8,128)(2,1)}, u32[]{:S(2)}) copy-start(bf16[2,1024,256]{2,1,0:T(8,128)(2,1)} %constant.66.clone.spread_back_ref) | copy-start | bytes 3145732
  26.0 16.1 %copy-start.8 = (bf16[2,512,256]{2,1,0:T(8,128)(2,1)S(1)}, bf16[2,512,256]{2,1,0:T(8,128)(2,1)}, u32[]{:S(2)}) copy-start(bf16[2,512,256]{2,1,0:T(8,128)(2,1)} %constant.64.clone.pixels_back_ref) | copy-start | bytes 1572868
  26.0 16.2 %copy-start.10 = (bf16[2,4,128,128]{3,2,1,0:T(8,128)(2,1)S(1)}, bf16[2,4,128,128]{3,2,1,0:T(8,128)(2,1)}, u32[]{:S(2)}) copy-start(bf16[2,4,128,128]{3,2,1,0:T(8,128)(2,1)} %constant.62.clone.out_back_ref) | copy-start | bytes 786436
  26.0 16.2 %copy-start.13 = (bf16[256,128]{1,0:T(8,128)(2,1)S(1)}, bf16[256,128]{1,0:T(8,128)(2,1)}, u32[]{:S(2)}) copy-start(bf16[256,128]{1,0:T(8,128)(2,1)} %constant.58.clone.fold_ref) | copy-start | bytes 196612
  26.0 16.2 %copy-start.16 = (bf16[72,64]{1,0:T(8,128)(2,1)S(1)}, bf16[72,64]{1,0:T(8,128)(2,1)}, u32[]{:S(2)}) copy-start(bf16[72,64]{1,0:T(8,128)(2,1)} %constant.60.clone.flip_back_ref) | copy-start | bytes 27652
  31.5 10.3 %collective-permute-start.13 = (f32[64,256]{1,0:T(8,128)S(1)}, f32[64,256]{1,0:T(8,128)S(1)}, u32[]{:S(2)}, u32[]{:S(2)}) collective-permute-start(f32[64,256]{1,0:T(8,128)S(1)} %get-tuple-element.30.i0), channel_id=1, source_target_pairs={{0,2},{1,3},{2,0},{3,1},{4,6},{5,7},{6,4},{7,5},{8,10},{9,11},{10,... | collective-permute-start | bytes 196616 | tf_op jit(solution)/shard_map/ppermute | solution.py:441
  34.4 7.4 %collective-permute-start.12 = (f32[64,256]{1,0:T(8,128)S(1)}, f32[64,256]{1,0:T(8,128)S(1)}, u32[]{:S(2)}, u32[]{:S(2)}) collective-permute-start(f32[64,256]{1,0:T(8,128)S(1)} %get-tuple-element.30.i0), channel_id=1, source_target_pairs={{0,3},{1,2},{2,1},{3,0},{4,7},{5,6},{6,5},{7,4},{8,11},{9,10},{10,... | collective-permute-start | bytes 196616 | tf_op jit(solution)/shard_map/ppermute | solution.py:441
  36.6 5.5 %collective-permute-start.11 = (f32[64,256]{1,0:T(8,128)S(1)}, f32[64,256]{1,0:T(8,128)S(1)}, u32[]{:S(2)}, u32[]{:S(2)}) collective-permute-start(f32[64,256]{1,0:T(8,128)S(1)} %get-tuple-element.30.i0), channel_id=1, source_target_pairs={{0,1},{1,0},{2,3},{3,2},{4,5},{5,4},{6,7},{7,6},{8,9},{9,8},{10,11... | collective-permute-start | bytes 196616 | tf_op jit(solution)/shard_map/ppermute | solution.py:441
  42.1 10.9 %copy-start.7 = (bf16[2,128,1024]{2,1,0:T(8,128)(2,1)S(1)}, bf16[2,128,1024]{2,1,0:T(8,128)(2,1)}, u32[]{:S(2)}) copy-start(bf16[2,128,1024]{2,1,0:T(8,128)(2,1)} %constant.55.clone.band_back_ref) | copy-start | bytes 1572868
  42.2 10.9 %copy-start.15 = (f32[8,1024]{1,0:T(8,128)S(1)}, f32[8,1024]{1,0:T(8,128)}, u32[]{:S(2)}) copy-start(f32[8,1024]{1,0:T(8,128)} %constant.56.clone.edge_ref) | copy-start | bytes 98308
  44.3 4.8 %collective-permute-start.14 = (f32[176,128]{1,0:T(8,128)S(1)}, f32[176,128]{1,0:T(8,128)S(1)}, u32[]{:S(2)}, u32[]{:S(2)}) collective-permute-start(f32[176,128]{1,0:T(8,128)S(1)} %get-tuple-element.33), channel_id=1, source_target_pairs={{0,4},{1,5},{2,6},{3,7},{4,0},{5,1},{6,2},{7,3},{8,12},{9,13},{10,... | collective-permute-start | bytes 270344 | tf_op jit(solution)/shard_map/ppermute | solution.py:437
  45.0 6.0 %collective-permute-start.15 = (f32[176,128]{1,0:T(8,128)S(1)}, f32[176,128]{1,0:T(8,128)S(1)}, u32[]{:S(2)}, u32[]{:S(2)}) collective-permute-start(f32[176,128]{1,0:T(8,128)S(1)} %get-tuple-element.34), channel_id=1, source_target_pairs={{0,8},{1,9},{2,10},{3,11},{4,12},{5,13},{6,14},{7,15},{8,0},{9,1},... | collective-permute-start | bytes 270344 | tf_op jit(solution)/shard_map/ppermute | solution.py:437
  47.3 5.7 %collective-permute-start.16 = (f32[176,128]{1,0:T(8,128)S(1)}, f32[176,128]{1,0:T(8,128)S(1)}, u32[]{:S(2)}, u32[]{:S(2)}) collective-permute-start(f32[176,128]{1,0:T(8,128)S(1)} %get-tuple-element.35), channel_id=1, source_target_pairs={{0,12},{1,13},{2,14},{3,15},{4,8},{5,9},{6,10},{7,11},{8,4},{9,5},... | collective-permute-start | bytes 270344 | tf_op jit(solution)/shard_map/ppermute | solution.py:437
  53.4 7.4 %collective-permute-start.17 = (f32[72,128]{1,0:T(8,128)S(1)}, f32[72,128]{1,0:T(8,128)S(1)}, u32[]{:S(2)}, u32[]{:S(2)}) collective-permute-start(f32[72,128]{1,0:T(8,128)S(1)} %get-tuple-element.36), channel_id=1, source_target_pairs={{0,1},{1,0},{2,3},{3,2},{4,5},{5,4},{6,7},{7,6},{8,9},{9,8},{10,11... | collective-permute-start | bytes 110600 | tf_op jit(solution)/shard_map/ppermute | solution.py:441
  54.5 7.9 %collective-permute-start.18 = (f32[72,128]{1,0:T(8,128)S(1)}, f32[72,128]{1,0:T(8,128)S(1)}, u32[]{:S(2)}, u32[]{:S(2)}) collective-permute-start(f32[72,128]{1,0:T(8,128)S(1)} %get-tuple-element.40), channel_id=1, source_target_pairs={{0,2},{1,3},{2,0},{3,1},{4,6},{5,7},{6,4},{7,5},{8,10},{9,11},{10,... | collective-permute-start | bytes 110600 | tf_op jit(solution)/shard_map/ppermute | solution.py:441
  58.0 6.3 %collective-permute-start.19 = (f32[72,128]{1,0:T(8,128)S(1)}, f32[72,128]{1,0:T(8,128)S(1)}, u32[]{:S(2)}, u32[]{:S(2)}) collective-permute-start(f32[72,128]{1,0:T(8,128)S(1)} %get-tuple-element.41), channel_id=1, source_target_pairs={{0,3},{1,2},{2,1},{3,0},{4,7},{5,6},{6,5},{7,4},{8,11},{9,10},{10,... | collective-permute-start | bytes 110600 | tf_op jit(solution)/shard_map/ppermute | solution.py:441
  64.3 5.6 %collective-permute-start.21 = (f32[72,128]{1,0:T(8,128)S(1)}, f32[72,128]{1,0:T(8,128)S(1)}, u32[]{:S(2)}, u32[]{:S(2)}) collective-permute-start(f32[72,128]{1,0:T(8,128)S(1)} %add_add_fusion.own_ref), channel_id=1, source_target_pairs={{0,240},{16,32},{32,16},{48,64},{64,48},{80,96},{96,80},{112,128},... | collective-permute-start | bytes 110600 | tf_op jit(solution)/shard_map/ppermute | solution.py:449
  64.5 5.4 %collective-permute-start.20 = (f32[72,128]{1,0:T(8,128)S(1)}, f32[72,128]{1,0:T(8,128)S(1)}, u32[]{:S(2)}, u32[]{:S(2)}) collective-permute-start(f32[72,128]{1,0:T(8,128)S(1)} %add_add_fusion.own_ref), channel_id=1, source_target_pairs={{0,16},{16,0},{32,48},{48,32},{64,80},{80,64},{96,112},{112,96},{1... | collective-permute-start | bytes 110600 | tf_op jit(solution)/shard_map/ppermute | solution.py:445
